TPU v7x, 256 devices: a whole 4x4x8 slice. The times are simulated.
256 devices in a mesh: section: 8 (over y, core), expert: 32 (over x, z).
Axes of the slice: x: 4, y: 4, z: 8, core: 2. Of those that a mesh axis runs over, the one named last changes fastest.
Arguments:
- down_tokens: bfloat16 [8, 2048, 7168], P('section', 'expert'), may hold values from -6 to 6
- up_tokens: bfloat16 [8, 2048, 7168], P('section', 'expert'), may hold values from -6 to 6
- down_routes: int32 [8, 2048, 1], P('section', 'expert'), may hold values from 0 to 3; in each aligned block of 64 rows (0 to 63, 64 to 127, ..., all dimensions but the last counted through in order) at most 32 rows name the same one
- up_routes: int32 [8, 2048, 1], P('section', 'expert'), may hold values from 0 to 3; in each aligned block of 64 rows (0 to 63, 64 to 127, ..., all dimensions but the last counted through in order) at most 32 rows name the same one
- down_gates: float32 [8, 2048, 1], P('section', 'expert'), may hold values from 0.3 to 2
- up_gates: float32 [8, 2048, 1], P('section', 'expert'), may hold values from 0.3 to 2
- w_gate: bfloat16 [8, 7168, 4096], P('section', None, 'expert'), may hold values from -0.0625 to 0.0625
- w_up: bfloat16 [8, 7168, 4096], P('section', None, 'expert'), may hold values from -0.0625 to 0.0625
- w_down: bfloat16 [8, 4096, 7168], P('section', 'expert'), may hold values from -0.1875 to 0.1875
Outputs:
- next_down: bfloat16 [8, 2048, 7168], P('section', 'expert')
- next_up: bfloat16 [8, 2048, 7168], P('section', 'expert')
Inputs may be any that keep to these rules, and one draw needn't show every extreme that they name: `down_routes`: each row names 1 different experts. In every aligned block of 64 rows (the rows of one device), no expert is named more than 32 times, a bound that some block reaches. `up_routes`: as for down_routes.
All inputs are finite; a program needn't handle non-finite values.
Results may differ from a plain program's by a relative error of at most 0.01.
Values may be sent and summed in bfloat16 or wider, within the bound.
No kernel may reach another device: no remote copies, remote signals or barrier semaphores. Data moves between devices by JAX's collectives and lax.ppermute only.
A program may use at most 192 MiB of HBM per device.

v0:
```python
import jax
import jax.numpy as jnp
from jax import lax
from jax.sharding import PartitionSpec as P

SPLIT = 8
TOP = 1


def passed_along(block, axis, distance):
    devices = range(lax.axis_size(axis))
    route = [(i - distance, i) for i in devices if i - distance in devices]
    return lax.ppermute(block, axis, route)


def build_buffer(block_tokens, block_routes, experts, capacity):
    rows = block_tokens.shape[0]
    one_hot = (
        block_routes[:, :, None] == jnp.arange(experts, dtype=jnp.int32)[None, None, :]
    ).astype(jnp.int32)
    flat = one_hot.reshape(rows * TOP, experts)
    before = jnp.cumsum(flat, axis=0) - flat
    slot = jnp.sum(before * flat, axis=1).reshape(rows, TOP)
    target = block_routes * capacity + slot
    select = (
        target.reshape(-1)[None, :] == jnp.arange(experts * capacity, dtype=jnp.int32)[:, None]
    ).astype(jnp.bfloat16)
    repeated = jnp.repeat(block_tokens, TOP, axis=0)
    buffer = jnp.dot(select, repeated, preferred_element_type=jnp.float32).astype(jnp.bfloat16)
    outgoing = jnp.repeat(buffer.reshape(experts, capacity, block_tokens.shape[1]), SPLIT, axis=0)
    return (outgoing, target)


def expert_slice(received, w_gate, w_up, w_down):
    width = received.shape[2]
    rows = received.reshape(-1, width)
    gate = jnp.dot(rows, w_gate, preferred_element_type=jnp.float32)
    up = jnp.dot(rows, w_up, preferred_element_type=jnp.float32)
    hidden = (jax.nn.silu(gate) * up).astype(jnp.bfloat16)
    part = jnp.dot(hidden, w_down, preferred_element_type=jnp.float32).astype(jnp.bfloat16)
    return part.reshape(received.shape)


def finish(tokens, returned, target, gates, experts, capacity):
    width = tokens.shape[1]
    summed = jnp.sum(returned.reshape(experts, SPLIT, capacity, width).astype(jnp.float32), axis=1)
    values = summed.reshape(experts * capacity, width)
    picked = jnp.take(values, target.reshape(-1), axis=0).reshape(tokens.shape[0], TOP, width)
    mixed = jnp.sum(picked * gates[:, :, None], axis=1)
    return (tokens.astype(jnp.float32) + mixed).astype(jnp.bfloat16)


def body(
    down_tokens, up_tokens, down_routes, up_routes, down_gates, up_gates, w_gate, w_up, w_down
):
    experts = lax.axis_size("expert") // SPLIT
    rows = down_tokens.shape[1]
    capacity = min(rows, 2 * ((rows * TOP + experts - 1) // experts))
    gate_local = w_gate[0]
    up_local = w_up[0]
    down_local = w_down[0]
    send_down, target_down = build_buffer(down_tokens[0], down_routes[0], experts, capacity)
    send_up, target_up = build_buffer(up_tokens[0], up_routes[0], experts, capacity)
    part = expert_slice(
        lax.all_to_all(send_down, "expert", split_axis=0, concat_axis=0, tiled=True),
        gate_local,
        up_local,
        down_local,
    )
    back_down = lax.all_to_all(part, "expert", split_axis=0, concat_axis=0, tiled=True)
    part = expert_slice(
        lax.all_to_all(send_up, "expert", split_axis=0, concat_axis=0, tiled=True),
        gate_local,
        up_local,
        down_local,
    )
    back_up = lax.all_to_all(part, "expert", split_axis=0, concat_axis=0, tiled=True)
    y_down = finish(down_tokens[0], back_down, target_down, down_gates[0], experts, capacity)
    y_up = finish(up_tokens[0], back_up, target_up, up_gates[0], experts, capacity)
    section_index = lax.axis_index("section")
    sections = lax.axis_size("section")
    from_below = passed_along(y_down, "section", 1)
    from_above = passed_along(y_up, "section", -1)
    next_down = jnp.where(section_index == 0, y_up, from_below)
    next_up = jnp.where(section_index == sections - 1, y_down, from_above)
    return (next_down[None], next_up[None])


def solution(mesh):
    placed = (
        P("section", "expert", None),
        P("section", "expert", None),
        P("section", "expert", None),
        P("section", "expert", None),
        P("section", "expert", None),
        P("section", "expert", None),
        P("section", None, "expert"),
        P("section", None, "expert"),
        P("section", "expert", None),
    )
    return jax.shard_map(
        body,
        mesh=mesh,
        in_specs=placed,
        out_specs=(P("section", "expert", None), P("section", "expert", None)),
        check_vma=False,
    )
```

profile of v0, /device:TPU:1, one launch (start us, length us, event | category | flops | bytes accessed | tf_op | source)
XLA Modules:
  0.0 1464.9 jit_solution(16945116835477711188)
XLA Ops:
  0.6 0.0 copy-start
  0.6 0.9 fusion.47
  1.5 0.1 reduce_window_sum.17
  1.6 0.8 select_reduce_fusion.1
  2.4 0.7 compare_and_fusion.1
  3.1 1.8 convolution_convert_fusion.3
  4.9 5.5 broadcast_in_dim.25
  10.4 0.0 copy-start.3
  10.4 0.0 copy-start.2
  10.4 12.1 all-to-all-start
  22.5 0.0 copy-done.3
  22.5 0.1 fusion.45
  22.6 0.1 reduce_window_sum.18
  22.7 0.2 select_reduce_fusion
  22.9 0.0 copy-done.2
  22.9 1.8 convolution_convert_fusion.2
  24.7 331.5 %all-to-all-done = bf16[32,32,7168]{2,1,0:T(8,128)(2,1)} async-done(((bf16[32,32,7168]{2,1,0:T(8,128)(2,1)}), bf16[32,32,7168]{2,1,0:T(8,128)(2,1)}, u32[]{:S(2)}, u32[]{:S(2)}) %all-to-all-start) | async-done | bytes 14680096 | tf_op jit(solution)/shard_map/all_to_all | solution.py:72
  356.3 6.4 broadcast_in_dim.26
  362.7 17.8 %all-to-all-start.2 = ((bf16[32,32,7168]{2,1,0:T(8,128)(2,1)}), bf16[32,32,7168]{2,1,0:T(8,128)(2,1)}, u32[]{:S(2)}, u32[]{:S(2)}) async-start(bf16[32,32,7168]{2,1,0:T(8,128)(2,1)} %bitcast.73), calls=%async_computation.2 | async-start | bytes 29360128 | tf_op jit(solution)/shard_map/all_to_all | solution.py:65
  380.5 7.8 fusion.8
  388.3 0.0 copy-done
  388.3 22.0 %convolution_convert_fusion.1 = bf16[1024,7168]{1,0:T(8,128)(2,1)} fusion(bf16[1,128,7168]{2,1,0:T(8,128)(2,1)S(1)} %copy-done, bf16[1024,7168]{1,0:T(8,128)(2,1)} %bitcast.4, bf16[1,7168,128]{2,1,0:T(8,128)(2,1)} %param.18, f32[1024,128]{1,0:T(8,128)S(1)} %fusion.8), kind=kOutput, calls=%fused_computation.5 | convolution fusion | flops 3766222848 | bytes 33554432 | tf_op jit(solution)/shard_map/dot_general | solution.py:40
  410.3 308.4 %all-to-all-done.2 = bf16[32,32,7168]{2,1,0:T(8,128)(2,1)} async-done(((bf16[32,32,7168]{2,1,0:T(8,128)(2,1)}), bf16[32,32,7168]{2,1,0:T(8,128)(2,1)}, u32[]{:S(2)}, u32[]{:S(2)}) %all-to-all-start.2) | async-done | bytes 14680096 | tf_op jit(solution)/shard_map/all_to_all | solution.py:65
  718.7 19.5 %all-to-all-start.1 = ((bf16[32,32,7168]{2,1,0:T(8,128)(2,1)}), bf16[32,32,7168]{2,1,0:T(8,128)(2,1)}, u32[]{:S(2)}, u32[]{:S(2)}) async-start(bf16[32,32,7168]{2,1,0:T(8,128)(2,1)} %bitcast.72), calls=%async_computation.1 | async-start | bytes 29360128 | tf_op jit(solution)/shard_map/all_to_all | solution.py:77
  738.1 7.8 fusion.6
  745.9 22.1 %convolution_convert_fusion = bf16[1024,7168]{1,0:T(8,128)(2,1)} fusion(bf16[1,128,7168]{2,1,0:T(8,128)(2,1)S(1)} %copy-done, bf16[1024,7168]{1,0:T(8,128)(2,1)} %bitcast.16, bf16[1,7168,128]{2,1,0:T(8,128)(2,1)} %param.18, f32[1024,128]{1,0:T(8,128)S(1)} %fusion.6), kind=kOutput, calls=%fused_computation.4 | convolution fusion | flops 3766222848 | bytes 33554432 | tf_op jit(solution)/shard_map/dot_general | solution.py:40
  768.0 308.5 %all-to-all-done.1 = bf16[32,32,7168]{2,1,0:T(8,128)(2,1)} async-done(((bf16[32,32,7168]{2,1,0:T(8,128)(2,1)}), bf16[32,32,7168]{2,1,0:T(8,128)(2,1)}, u32[]{:S(2)}, u32[]{:S(2)}) %all-to-all-start.1) | async-done | bytes 14680096 | tf_op jit(solution)/shard_map/all_to_all | solution.py:77
  1076.5 15.2 %all-to-all-start.3 = ((bf16[32,32,7168]{2,1,0:T(8,128)(2,1)}), bf16[32,32,7168]{2,1,0:T(8,128)(2,1)}, u32[]{:S(2)}, u32[]{:S(2)}) async-start(bf16[32,32,7168]{2,1,0:T(8,128)(2,1)} %bitcast.70), calls=%async_computation.3 | async-start | bytes 29360128 | tf_op jit(solution)/shard_map/all_to_all | solution.py:70
  1091.7 10.3 convert_reduce_fusion.1
  1102.0 0.0 copy-start.4
  1102.0 4.0 gather_fusion
  1106.0 0.0 copy-done.4
  1106.0 2.4 fusion.13
  1108.5 2.9 collective-permute-start.1
  1111.4 318.4 %all-to-all-done.3 = bf16[32,32,7168]{2,1,0:T(8,128)(2,1)} async-done(((bf16[32,32,7168]{2,1,0:T(8,128)(2,1)}), bf16[32,32,7168]{2,1,0:T(8,128)(2,1)}, u32[]{:S(2)}, u32[]{:S(2)}) %all-to-all-start.3) | async-done | bytes 14680096 | tf_op jit(solution)/shard_map/all_to_all | solution.py:70
  1429.8 10.1 convert_reduce_fusion
  1439.9 0.0 copy-start.5
  1439.9 5.2 gather_fusion.1
  1445.1 0.0 collective-permute-done.1
  1445.1 0.0 copy-done.5
  1445.1 0.0 copy-start.1
  1445.1 3.7 select_bitcast_fusion
  1448.8 4.4 collective-permute-start
  1453.2 10.6 collective-permute-done
  1463.8 1.0 select_bitcast_fusion.1
  1464.9 0.0 copy-done.1
  (5 shorter events, 0.0 us)
Async XLA Ops:
  0.6 387.6 %copy-start = (bf16[1,128,7168]{2,1,0:T(8,128)(2,1)S(1)}, bf16[1,128,7168]{2,1,0:T(8,128)(2,1)}, u32[]{:S(2)}) copy-start(bf16[1,128,7168]{2,1,0:T(8,128)(2,1)} %param.19) | copy-start | bytes 5505028
  10.4 12.1 copy-start.3
  10.4 12.5 copy-start.2
  10.4 345.9 %all-to-all-start = ((bf16[32,32,7168]{2,1,0:T(8,128)(2,1)}), bf16[32,32,7168]{2,1,0:T(8,128)(2,1)}, u32[]{:S(2)}, u32[]{:S(2)}) async-start(bf16[32,32,7168]{2,1,0:T(8,128)(2,1)} %bitcast.71), calls=%async_computation | async-start | bytes 29360128 | tf_op jit(solution)/shard_map/all_to_all | solution.py:72
  362.7 356.0 %all-to-all-start.2 = ((bf16[32,32,7168]{2,1,0:T(8,128)(2,1)}), bf16[32,32,7168]{2,1,0:T(8,128)(2,1)}, u32[]{:S(2)}, u32[]{:S(2)}) async-start(bf16[32,32,7168]{2,1,0:T(8,128)(2,1)} %bitcast.73), calls=%async_computation.2 | async-start | bytes 29360128 | tf_op jit(solution)/shard_map/all_to_all | solution.py:65
  718.7 357.8 %all-to-all-start.1 = ((bf16[32,32,7168]{2,1,0:T(8,128)(2,1)}), bf16[32,32,7168]{2,1,0:T(8,128)(2,1)}, u32[]{:S(2)}, u32[]{:S(2)}) async-start(bf16[32,32,7168]{2,1,0:T(8,128)(2,1)} %bitcast.72), calls=%async_computation.1 | async-start | bytes 29360128 | tf_op jit(solution)/shard_map/all_to_all | solution.py:77
  1076.5 353.3 %all-to-all-start.3 = ((bf16[32,32,7168]{2,1,0:T(8,128)(2,1)}), bf16[32,32,7168]{2,1,0:T(8,128)(2,1)}, u32[]{:S(2)}, u32[]{:S(2)}) async-start(bf16[32,32,7168]{2,1,0:T(8,128)(2,1)} %bitcast.70), calls=%async_computation.3 | async-start | bytes 29360128 | tf_op jit(solution)/shard_map/all_to_all | solution.py:70
  1102.0 4.0 copy-start.4
  1108.5 336.6 %collective-permute-start.1 = (bf16[64,7168]{1,0:T(8,128)(2,1)}, bf16[64,7168]{1,0:T(8,128)(2,1)}, u32[]{:S(2)}, u32[]{:S(2)}) collective-permute-start(bf16[64,7168]{1,0:T(8,128)(2,1)} %fusion.13), channel_id=1, source_target_pairs={{32,0},{64,32},{96,64},{128,96},{160,128},{192,160},{224,192},{33,... | collective-permute-start | bytes 2752520 | tf_op jit(solution)/shard_map/ppermute | solution.py:13
  1439.9 5.2 copy-start.5
  1445.1 19.8 %copy-start.1 = (bf16[1,128,7168]{2,1,0:T(8,128)(2,1)S(1)}, bf16[1,128,7168]{2,1,0:T(8,128)(2,1)}, u32[]{:S(2)}) copy-start(bf16[1,128,7168]{2,1,0:T(8,128)(2,1)} %param.19) | copy-start | bytes 5505028
  1448.8 15.1 %collective-permute-start = (bf16[64,7168]{1,0:T(8,128)(2,1)}, bf16[64,7168]{1,0:T(8,128)(2,1)S(1)}, u32[]{:S(2)}, u32[]{:S(2)}) collective-permute-start(bf16[64,7168]{1,0:T(8,128)(2,1)} %get-tuple-element.4), channel_id=1, source_target_pairs={{0,32},{32,64},{64,96},{96,128},{128,160},{160,192},{192,224},{1,3... | collective-permute-start | bytes 2752520 | tf_op jit(solution)/shard_map/ppermute | solution.py:13
where the time goes:
time: 1480 us; the launch traced here: 1460 us
  waiting for transfers between devices  1280 us (86%)
  starting transfers between devices  71.8 us (5%)
  matrix products  63.3 us (4%)
  other arithmetic  30.4 us (2%)
  local copies, waits for them, and re-layouts  21.1 us (1%)
    all_to_all x2, waiting for transfers between devices, body(): lax.all_to_all(part, 'expert', split_axis=0, concat_axis=0, tiled=True)  627 us
    all_to_all x1, waiting for transfers between devices, body(): lax.all_to_all(send_up, 'expert', split_axis=0, concat_axis=0, tiled=True)  332 us
    all_to_all x1, waiting for transfers between devices, body(): lax.all_to_all(send_down, 'expert', split_axis=0, concat_axis=0, tiled=True)  308 us
    dot_general x2, matrix products, expert_slice(): jnp.dot(hidden, w_down, preferred_element_type=jnp.float32)  44.1 us
    all_to_all x2, starting transfers between devices, body(): lax.all_to_all(part, 'expert', split_axis=0, concat_axis=0, tiled=True)  34.6 us
  transfers between devices with their start and end apart: 6, of which 5 were waited for; matrix products, arithmetic and copies ran while one was open for 6% of the time, Pallas kernels for 0%

commit v1 on v0

v1 whole, which is shorter than its diff:
```python
import jax
import jax.numpy as jnp
from jax import lax
from jax.sharding import Mesh, PartitionSpec as P

SPLIT = 8


def shifted(block, axis, distance):
    n = lax.axis_size(axis)
    return lax.ppermute(block, axis, [(i, (i + distance) % n) for i in range(n)])


def passed_along(block, axis, distance):
    devices = range(lax.axis_size(axis))
    route = [(i - distance, i) for i in devices if i - distance in devices]
    return lax.ppermute(block, axis, route)


def gathered_along_x(block):
    half = block.shape[0] // 2
    before = shifted(block, "x", 1)
    after = shifted(block, "x", -1)
    top = shifted(before[:half], "x", 1)
    bottom = shifted(after[half:], "x", -1)
    return [(0, block), (-1, before), (1, after), (2, (top, bottom))]


def product(rows, block):
    if isinstance(block, tuple):
        half = block[0].shape[0]
        return product(rows[:, :half], block[0]) + product(rows[:, half:], block[1])
    return jnp.dot(rows, block, preferred_element_type=jnp.float32)


def body(
    down_tokens, up_tokens, down_routes, up_routes, down_gates, up_gates, w_gate, w_up, w_down
):
    n_x, n_z = lax.axis_size("x"), lax.axis_size("z")
    me_x = lax.axis_index("x")
    rows, width = down_tokens.shape[1:]
    part = width // n_z
    hid = w_gate.shape[2]
    tokens = (down_tokens[0], up_tokens[0])
    gates = (down_gates[0], up_gates[0])

    routes = lax.all_gather(
        jnp.concatenate([down_routes[0], up_routes[0]], axis=1), "z"
    )
    routes = routes.reshape(n_z * rows, 2)

    w_down_cut = lax.all_to_all(
        w_down[0].reshape(hid, n_z, part).transpose(1, 0, 2), "z", 0, 0
    ).reshape(n_z * hid, part)
    gate_up = gathered_along_x(jnp.concatenate([w_gate[0], w_up[0]], axis=1))
    down = gathered_along_x(w_down_cut)

    results = []
    for p in range(2):
        mine = routes[:, p : p + 1]
        x = lax.all_gather(tokens[p], "z").reshape(n_z * rows, width)
        chosen = None
        for offset, block in gate_up:
            value = product(x, block)
            here = mine == (me_x + offset + n_x) % n_x
            chosen = value if chosen is None else jnp.where(here, value, chosen)
        hidden = (jax.nn.silu(chosen[:, :hid]) * chosen[:, hid:]).astype(jnp.bfloat16)
        hidden = lax.all_gather(hidden, "z", axis=1, tiled=True)
        out = None
        for offset, block in down:
            here = mine == (me_x + offset + n_x) % n_x
            term = product(jnp.where(here, hidden, jnp.zeros_like(hidden)), block)
            out = term if out is None else out + term
        out = out.astype(jnp.bfloat16).reshape(n_z, rows, part)
        out = lax.all_to_all(out, "z", 0, 0)
        out = out.transpose(1, 0, 2).reshape(rows, width)
        y = tokens[p].astype(jnp.float32) + gates[p] * out.astype(jnp.float32)
        results.append(y.astype(jnp.bfloat16))

    y_down, y_up = results
    section = lax.axis_index("section")
    last = lax.axis_size("section") - 1
    next_down = jnp.where(section == 0, y_up, passed_along(y_down, "section", 1))
    next_up = jnp.where(section == last, y_down, passed_along(y_up, "section", -1))
    return next_down[None], next_up[None]


def solution(mesh):
    sections, devices = mesh.devices.shape
    fine = Mesh(mesh.devices.reshape(sections, devices // SPLIT, SPLIT), ("section", "x", "z"))
    by_rows = P("section", ("x", "z"), None)
    by_columns = P("section", None, ("x", "z"))
    return jax.shard_map(
        body,
        mesh=fine,
        in_specs=(by_rows,) * 6 + (by_columns, by_columns, by_rows),
        out_specs=(by_rows, by_rows),
        check_vma=False,
    )
```

time: 1480 us -> 391 us (0.26)
  waiting for transfers between devices: 1280 us -> 223 us
  starting transfers between devices: 71.8 us -> 39.1 us
  other arithmetic: 30.4 us -> 13.4 us
    all_to_all x4 -> x3, waiting for transfers between devices: 1270 us -> 78.2 us  [the longest x1 59.3 us: body(): lax.all_to_all(w_down[0].reshape(hid, n_z, part).transpose(1, 0, 2), 'z',...]
    all_gather x0 -> x4, waiting for transfers between devices: none -> 104 us  [the longest x2 60 us: body(): x = lax.all_gather(tokens[p], 'z').reshape(n_z * rows, width)]
    all_to_all x4 -> x3, starting transfers between devices: 64.5 us -> 19.3 us  [the longest x2 10.2 us: body(): out = lax.all_to_all(out, 'z', 0, 0)]
    ppermute x0 -> x8, waiting for transfers between devices: none -> 29.1 us  [shifted(): lax.ppermute(block, axis, [(i, (i + distance) % n) for i in range(n)])]
    reduce_sum x4 -> x0, other arithmetic: 21.5 us -> none  [the longest x2 20.4 us: finish(): jnp.sum(returned.reshape(experts, SPLIT, capacity, width).astype(jnp.floa...]
    dot_general x6 -> x20, matrix products: 63.3 us -> 66.9 us  [product(): return jnp.dot(rows, block, preferred_element_type=jnp.float32)]
  transfers between devices with their start and end apart: 6 -> 17, of which waited for: 5 -> 8; matrix products, arithmetic and copies ran while one was open for 6% -> 24% of each run, Pallas kernels for 0% -> 0%
where the time goes in v1:
time: 391 us; the launch traced here: 390 us
  waiting for transfers between devices  223 us (57%)
  matrix products  66.9 us (17%)
  starting transfers between devices  39.1 us (10%)
  local copies, waits for them, and re-layouts  19.7 us (5%)
  between operations  14.1 us (4%)
  blocking collectives  13.8 us (4%)
  other arithmetic  13.4 us (3%)
    dot_general x20, matrix products, product(): return jnp.dot(rows, block, preferred_element_type=jnp.float32)  66.9 us
    all_gather x2, waiting for transfers between devices, body(): x = lax.all_gather(tokens[p], 'z').reshape(n_z * rows, width)  60 us
    all_to_all x1, waiting for transfers between devices, body(): lax.all_to_all(w_down[0].reshape(hid, n_z, part).transpose(1, 0, 2), 'z',...  59.3 us
    all_gather x2, waiting for transfers between devices, body(): hidden = lax.all_gather(hidden, 'z', axis=1, tiled=True)  43.9 us
    ppermute x8, waiting for transfers between devices, shifted(): lax.ppermute(block, axis, [(i, (i + distance) % n) for i in range(n)])  29.1 us
    all_to_all x2, waiting for transfers between devices, body(): out = lax.all_to_all(out, 'z', 0, 0)  18.8 us
    all_gather x1, blocking collectives, body(): lax.all_gather(jnp.concatenate([down_routes[0], up_routes[0]], axis=1), 'z')  13.8 us
    ppermute x8, starting transfers between devices, shifted(): lax.ppermute(block, axis, [(i, (i + distance) % n) for i in range(n)])  12.1 us
  transfers between devices with their start and end apart: 17, of which 8 were waited for; matrix products, arithmetic and copies ran while one was open for 24% of the time, Pallas kernels for 0%

profile of v1, /device:TPU:1, one launch (start us, length us, event | category | flops | bytes accessed | tf_op | source)
XLA Modules:
  0.0 390.2 jit_solution(18297038238727868616)
XLA Ops:
  7.2 0.7 all-gather.11.cloned.1.call-update
  7.9 0.7 all-gather.7.cloned.1.call-update
  8.6 3.9 copy.22
  12.5 9.1 %all-to-all-start = ((bf16[8,128,896]{1,2,0:T(8,128)(2,1)}), bf16[8,128,896]{1,2,0:T(8,128)(2,1)}, u32[]{:S(2)}, u32[]{:S(2)}) async-start(bf16[8,128,896]{1,2,0:T(8,128)(2,1)} %bitcast.10), calls=%async_computation | async-start | bytes 3670016 | tf_op jit(solution)/shard_map/all_to_all | solution.py:52
  21.7 3.8 pad_maximum_fusion
  25.5 2.5 collective-permute-start.2
  28.0 59.3 %all-to-all-done = bf16[8,128,896]{1,2,0:T(8,128)(2,1)} async-done(((bf16[8,128,896]{1,2,0:T(8,128)(2,1)}), bf16[8,128,896]{1,2,0:T(8,128)(2,1)}, u32[]{:S(2)}, u32[]{:S(2)}) %all-to-all-start) | async-done | bytes 1835040 | tf_op jit(solution)/shard_map/all_to_all | solution.py:52
  87.3 3.1 copy.23
  90.4 2.6 collective-permute-start.5
  92.9 13.0 %collective-permute-done.2 = bf16[7168,256]{1,0:T(8,128)(2,1)} collective-permute-done((bf16[7168,256]{1,0:T(8,128)(2,1)}, bf16[7168,256]{1,0:T(8,128)(2,1)}, u32[]{:S(2)}, u32[]{:S(2)}) %collective-permute-start.2) | collective-permute-done | bytes 3670048 | tf_op jit(solution)/shard_map/ppermute | solution.py:11
  106.0 2.8 slice.75
  108.8 3.4 collective-permute-start.3
  112.3 13.8 %all-gather.1 = s32[8,64,2]{1,2,0:T(2,128)S(1)} all-gather(s32[1,64,2]{1,2,0:T(2,128)S(1)} %add_bitcast_fusion), channel_id=2, replica_groups=mesh['section'=8,'x'=4,'z'=8] {'z'}, dimensions={0}, use_global_device_ids=true | all-gather | bytes 4608 | tf_op jit(solution)/shard_map/all_gather | solution.py:47
  126.1 0.1 reshape.47
  126.1 0.1 compare_reduce_fusion.3
  126.2 2.9 slice.73
  129.1 16.1 %collective-permute-done.5 = bf16[1024,896]{1,0:T(8,128)(2,1)} collective-permute-done((bf16[1024,896]{1,0:T(8,128)(2,1)S(1)}, bf16[1024,896]{1,0:T(8,128)(2,1)}, u32[]{:S(2)}, u32[]{:S(2)}) %collective-permute-start.5) | collective-permute-done | bytes 1835040 | tf_op jit(solution)/shard_map/ppermute | solution.py:11
  145.2 2.2 slice.82
  147.4 3.6 collective-permute-start.7
  151.0 2.2 slice.80
  153.2 6.4 %fusion.66 = f32[256,512]{1,0:T(8,128)S(1)} fusion(bf16[512,7168]{1,0:T(8,128)(2,1)} %bitcast.82, bf16[7168,128]{1,0:T(8,128)(2,1)} %bitcast.72, bf16[7168,128]{1,0:T(8,128)(2,1)} %bitcast.76), kind=kOutput, calls=%fused_computation.80 | convolution fusion | flops 1886388224 | bytes 11534336 | tf_op jit(solution)/shard_map/dot_general | solution.py:33
  159.6 60.0 %all-gather.7.cloned.1.call-done = bf16[8,64,7168]{2,1,0:T(8,128)(2,1)} async-done(((bf16[1,64,7168]{2,1,0:T(8,128)(2,1)}), bf16[8,64,7168]{2,1,0:T(8,128)(2,1)}) %all-gather.7.cloned.1.call-update) | async-done | bytes 7340048 | tf_op jit(solution)/shard_map/all_gather | solution.py:61
  219.6 6.4 %fusion.67 = f32[256,512]{1,0:T(8,128)S(1)} fusion(bf16[512,7168]{1,0:T(8,128)(2,1)} %bitcast.89, bf16[7168,128]{1,0:T(8,128)(2,1)} %bitcast.73, bf16[7168,128]{1,0:T(8,128)(2,1)} %bitcast.77), kind=kOutput, calls=%fused_computation.81 | convolution fusion | flops 1886388224 | bytes 11534336 | tf_op jit(solution)/shard_map/dot_general | solution.py:33
  226.0 2.7 fusion.4
  228.7 4.1 %convolution_select_fusion.2 = f32[256,512]{1,0:T(8,128)S(1)} fusion(f32[256,512]{1,0:T(8,128)S(1)} %fusion.67, bf16[7168,256]{1,0:T(8,128)(2,1)} %collective-permute-done, bf16[512,7168]{1,0:T(8,128)(2,1)S(1)} %bitcast.91, pred[512]{0:T(512)(128)(4,1)S(1)} %get-tuple-element.5), kind=kOutput, calls=%fused_computation.21 | convolution fusion | flops 1879179264 | bytes 12059136 | tf_op jit(solution)/shard_map/dot_general | solution.py:33
  232.9 4.1 %convolution_select_fusion.3 = f32[256,512]{1,0:T(8,128)S(1)} fusion(f32[256,512]{1,0:T(8,128)S(1)} %convolution_select_fusion.2, bf16[7168,256]{1,0:T(8,128)(2,1)} %collective-permute-done.2, bf16[512,7168]{1,0:T(8,128)(2,1)S(1)} %bitcast.92, pred[512]{0:T(512)(128)(4,1)S(1)} %get-tuple-element.4), kind=kOutput, calls=%fused_computation.22 | convolution fusion | flops 1879179264 | bytes 12059136 | tf_op jit(solution)/shard_map/dot_general | solution.py:33
  237.0 2.7 fusion.25
  239.7 0.7 fusion.59
  240.5 0.3 all-gather.13.cloned.1.call-start
  240.7 6.3 %convolution_select_fusion = f32[256,512]{1,0:T(8,128)S(1)} fusion(f32[256,512]{1,0:T(8,128)S(1)} %fusion.66, bf16[7168,256]{1,0:T(8,128)(2,1)} %collective-permute-done, bf16[512,7168]{1,0:T(8,128)(2,1)} %bitcast.83, pred[512]{0:T(512)(128)(4,1)S(1)} %get-tuple-element.8), kind=kOutput, calls=%fused_computation.19 | convolution fusion | flops 1879179264 | bytes 12059136 | tf_op jit(solution)/shard_map/dot_general | solution.py:33
  247.1 3.9 fusion
  251.0 6.4 %convolution_select_fusion.1 = f32[256,512]{1,0:T(8,128)S(1)} fusion(f32[256,512]{1,0:T(8,128)S(1)} %convolution_select_fusion, bf16[7168,256]{1,0:T(8,128)(2,1)} %collective-permute-done.2, bf16[512,7168]{1,0:T(8,128)(2,1)} %bitcast.85, pred[512]{0:T(512)(128)(4,1)S(1)} %get-tuple-element.7), kind=kOutput, calls=%fused_computation.20 | convolution fusion | flops 1879179264 | bytes 12059136 | tf_op jit(solution)/shard_map/dot_general | solution.py:33
  257.5 2.7 fusion.19
  260.2 0.7 fusion.58
  260.9 12.0 %all-gather.9.cloned.1.call-done = bf16[512,1024]{0,1:T(8,128)(2,1)} async-done(((bf16[512,128]{0,1:T(8,128)(2,1)}), bf16[512,1024]{0,1:T(8,128)(2,1)}) %all-gather.9.cloned.1.call-update) | async-done | bytes 1048592 | tf_op jit(solution)/shard_map/all_gather | solution.py:68
  273.0 1.4 broadcast_select_fusion.1
  274.4 0.1 copy-done.1
  274.5 2.8 fusion.36
  277.3 1.9 fusion.49
  279.2 2.8 fusion.34
  282.0 1.3 fusion.38
  283.3 1.8 add_convert_fusion.1
  285.0 4.5 %all-to-all-start.1 = ((bf16[8,64,896]{2,1,0:T(8,128)(2,1)}), bf16[8,64,896]{2,1,0:T(8,128)(2,1)}, u32[]{:S(2)}, u32[]{:S(2)}) async-start(bf16[8,64,896]{2,1,0:T(8,128)(2,1)} %bitcast.71), calls=%async_computation.1 | async-start | bytes 1835008 | tf_op jit(solution)/shard_map/all_to_all | solution.py:75
  289.5 31.8 %all-gather.13.cloned.1.call-done = bf16[512,1024]{0,1:T(8,128)(2,1)} async-done(((bf16[512,128]{0,1:T(8,128)(2,1)}), bf16[512,1024]{0,1:T(8,128)(2,1)}) %all-gather.13.cloned.1.call-update) | async-done | bytes 1048592 | tf_op jit(solution)/shard_map/all_gather | solution.py:68
  321.4 1.3 broadcast_select_fusion
  322.7 2.0 fusion.46
  324.7 2.8 fusion.28
  327.5 2.8 fusion.30
  330.2 1.3 fusion.32
  331.5 1.8 add_convert_fusion
  333.3 5.7 %all-to-all-start.2 = ((bf16[8,64,896]{2,1,0:T(8,128)(2,1)}), bf16[8,64,896]{2,1,0:T(8,128)(2,1)S(1)}, u32[]{:S(2)}, u32[]{:S(2)}) async-start(bf16[8,64,896]{2,1,0:T(8,128)(2,1)} %bitcast.18), calls=%async_computation.2 | async-start | bytes 1835008 | tf_op jit(solution)/shard_map/all_to_all | solution.py:75
  339.0 1.3 convert_bitcast_fusion.1
  340.4 0.1 copy.26
  340.5 1.0 copy-done.2
  341.5 1.2 fusion.9
  342.8 3.8 collective-permute-start.9
  346.6 18.8 %all-to-all-done.2 = bf16[8,64,896]{2,1,0:T(8,128)(2,1)S(1)} async-done(((bf16[8,64,896]{2,1,0:T(8,128)(2,1)}), bf16[8,64,896]{2,1,0:T(8,128)(2,1)S(1)}, u32[]{:S(2)}, u32[]{:S(2)}) %all-to-all-start.2) | async-done | bytes 917536 | tf_op jit(solution)/shard_map/all_to_all | solution.py:75
  365.4 0.1 convert_bitcast_fusion
  365.6 0.1 copy.27
  365.7 1.0 copy-done.3
  366.7 1.7 select_bitcast_fusion
  368.5 3.5 collective-permute-start.8
  372.0 10.6 %collective-permute-done.8 = bf16[64,7168]{1,0:T(8,128)(2,1)S(1)} collective-permute-done((bf16[64,7168]{1,0:T(8,128)(2,1)}, bf16[64,7168]{1,0:T(8,128)(2,1)S(1)}, u32[]{:S(2)}, u32[]{:S(2)}) %collective-permute-start.8) | collective-permute-done | bytes 917536 | tf_op jit(solution)/shard_map/ppermute | solution.py:17
  382.6 1.0 select_bitcast_fusion.1
  (42 shorter events, 0.2 us)
Async XLA Ops:
  7.2 146.0 %all-gather.11.cloned.1.call-start = ((), (), s32[]{:S(2)}) async-start(), calls=%async_computation.5 | async-start | bytes 8257536 | tf_op jit(solution)/shard_map/all_gather | solution.py:61
  7.9 211.7 %all-gather.7.cloned.1.call-start = ((), (), s32[]{:S(2)}) async-start(), calls=%async_computation.3 | async-start | bytes 8257536 | tf_op jit(solution)/shard_map/all_gather | solution.py:61
  12.5 9.2 %copy-start.4 = (bf16[1,7168,128]{2,1,0:T(8,128)(2,1)S(1)}, bf16[1,7168,128]{2,1,0:T(8,128)(2,1)}, u32[]{:S(2)}) copy-start(bf16[1,7168,128]{2,1,0:T(8,128)(2,1)} %param.16) | copy-start | bytes 5505028
  12.5 74.8 %all-to-all-start = ((bf16[8,128,896]{1,2,0:T(8,128)(2,1)}), bf16[8,128,896]{1,2,0:T(8,128)(2,1)}, u32[]{:S(2)}, u32[]{:S(2)}) async-start(bf16[8,128,896]{1,2,0:T(8,128)(2,1)} %bitcast.10), calls=%async_computation | async-start | bytes 3670016 | tf_op jit(solution)/shard_map/all_to_all | solution.py:52
  21.7 251.3 %all-gather.9.cloned.1.call-start = ((), (), s32[]{:S(2)}) async-start(), calls=%async_computation.4 | async-start | bytes 1179648 | tf_op jit(solution)/shard_map/all_gather | solution.py:68
  25.5 80.5 %collective-permute-start.2 = (bf16[7168,256]{1,0:T(8,128)(2,1)}, bf16[7168,256]{1,0:T(8,128)(2,1)}, u32[]{:S(2)}, u32[]{:S(2)}) collective-permute-start(bf16[7168,256]{1,0:T(8,128)(2,1)} %pad_maximum_fusion), channel_id=1, source_target_pairs={{0,24},{8,0},{16,8},{24,16},{1,25},{9,1},{17,9},{25,17},{2,26},{10... | collective-permute-start | bytes 11010056 | tf_op jit(solution)/shard_map/ppermute | solution.py:11
  28.0 98.2 %collective-permute-start = (bf16[7168,256]{1,0:T(8,128)(2,1)}, bf16[7168,256]{1,0:T(8,128)(2,1)}, u32[]{:S(2)}, u32[]{:S(2)}) collective-permute-start(bf16[7168,256]{1,0:T(8,128)(2,1)} %pad_maximum_fusion), channel_id=1, source_target_pairs={{0,8},{8,16},{16,24},{24,0},{1,9},{9,17},{17,25},{25,1},{2,10},{10... | collective-permute-start | bytes 11010056 | tf_op jit(solution)/shard_map/ppermute | solution.py:11
  90.4 21.9 %copy-start.6 = (s32[1,64,1]{1,2,0:T(1,128)S(1)}, s32[1,64,1]{1,2,0:T(1,128)}, u32[]{:S(2)}) copy-start(s32[1,64,1]{1,2,0:T(1,128)} %param.12) | copy-start | bytes 772
  90.4 21.9 %copy-start.7 = (s32[1,64,1]{1,2,0:T(1,128)S(1)}, s32[1,64,1]{1,2,0:T(1,128)}, u32[]{:S(2)}) copy-start(s32[1,64,1]{1,2,0:T(1,128)} %param.11) | copy-start | bytes 772
  90.4 54.8 %collective-permute-start.5 = (bf16[1024,896]{1,0:T(8,128)(2,1)S(1)}, bf16[1024,896]{1,0:T(8,128)(2,1)}, u32[]{:S(2)}, u32[]{:S(2)}) collective-permute-start(bf16[1024,896]{1,0:T(8,128)(2,1)S(1)} %bitcast.65), channel_id=1, source_target_pairs={{0,24},{8,0},{16,8},{24,16},{1,25},{9,1},{17,9},{25,17},{2,26},{10... | collective-permute-start | bytes 5505032 | tf_op jit(solution)/shard_map/ppermute | solution.py:11
  92.9 58.1 %collective-permute-start.4 = (bf16[1024,896]{1,0:T(8,128)(2,1)S(1)}, bf16[1024,896]{1,0:T(8,128)(2,1)}, u32[]{:S(2)}, u32[]{:S(2)}) collective-permute-start(bf16[1024,896]{1,0:T(8,128)(2,1)S(1)} %bitcast.66), channel_id=1, source_target_pairs={{0,8},{8,16},{16,24},{24,0},{1,9},{9,17},{17,25},{25,1},{2,10},{10... | collective-permute-start | bytes 5505032 | tf_op jit(solution)/shard_map/ppermute | solution.py:11
  108.8 117.2 %collective-permute-start.3 = (bf16[3584,256]{1,0:T(8,128)(2,1)}, bf16[3584,256]{1,0:T(8,128)(2,1)}, u32[]{:S(2)}, u32[]{:S(2)}) collective-permute-start(bf16[3584,256]{1,0:T(8,128)(2,1)} %slice.75), channel_id=1, source_target_pairs={{0,24},{8,0},{16,8},{24,16},{1,25},{9,1},{17,9},{25,17},{2,26},{10... | collective-permute-start | bytes 5505032 | tf_op jit(solution)/shard_map/ppermute | solution.py:11
  129.1 107.9 %collective-permute-start.1 = (bf16[3584,256]{1,0:T(8,128)(2,1)}, bf16[3584,256]{1,0:T(8,128)(2,1)}, u32[]{:S(2)}, u32[]{:S(2)}) collective-permute-start(bf16[3584,256]{1,0:T(8,128)(2,1)} %slice.73), channel_id=1, source_target_pairs={{0,8},{8,16},{16,24},{24,0},{1,9},{9,17},{17,25},{25,1},{2,10},{10... | collective-permute-start | bytes 5505032 | tf_op jit(solution)/shard_map/ppermute | solution.py:11
  147.4 129.9 %collective-permute-start.7 = (bf16[512,896]{1,0:T(8,128)(2,1)}, bf16[512,896]{1,0:T(8,128)(2,1)}, u32[]{:S(2)}, u32[]{:S(2)}) collective-permute-start(bf16[512,896]{1,0:T(8,128)(2,1)} %slice.82), channel_id=1, source_target_pairs={{0,24},{8,0},{16,8},{24,16},{1,25},{9,1},{17,9},{25,17},{2,26},{10... | collective-permute-start | bytes 2752520 | tf_op jit(solution)/shard_map/ppermute | solution.py:11
  153.2 130.1 %collective-permute-start.6 = (bf16[512,896]{1,0:T(8,128)(2,1)}, bf16[512,896]{1,0:T(8,128)(2,1)S(1)}, u32[]{:S(2)}, u32[]{:S(2)}) collective-permute-start(bf16[512,896]{1,0:T(8,128)(2,1)} %slice.80), channel_id=1, source_target_pairs={{0,8},{8,16},{16,24},{24,0},{1,9},{9,17},{17,25},{25,1},{2,10},{10... | collective-permute-start | bytes 2752520 | tf_op jit(solution)/shard_map/ppermute | solution.py:11
  219.6 6.5 %copy-start.9 = (bf16[8,64,7168]{2,1,0:T(8,128)(2,1)S(1)}, bf16[8,64,7168]{2,1,0:T(8,128)(2,1)}, u32[]{:S(2)}) copy-start(bf16[8,64,7168]{2,1,0:T(8,128)(2,1)} %all-gather.7.cloned.1.call-done) | copy-start | bytes 22020100
  240.5 80.9 %all-gather.13.cloned.1.call-start = ((), (), s32[]{:S(2)}) async-start(), calls=%async_computation.6 | async-start | bytes 1179648 | tf_op jit(solution)/shard_map/all_gather | solution.py:68
  247.0 10.4 %slice-start = ((s8[7340032]{0:T(1024)(128)(4,1)}), s8[4194304]{0:T(1024)(128)(4,1)S(1)}, s32[]{:S(2)}) async-start(s8[7340032]{0:T(1024)(128)(4,1)} %bitcast.86), calls=%async_computation.7 | async-start | bytes 8388608
  251.0 6.5 %slice-start.1 = ((s8[7340032]{0:T(1024)(128)(4,1)}), s8[3145728]{0:T(1024)(128)(4,1)S(1)}, s32[]{:S(2)}) async-start(s8[7340032]{0:T(1024)(128)(4,1)} %bitcast.86), calls=%async_computation.8 | async-start | bytes 6291456
  273.0 1.5 copy-start.1
  285.0 48.3 %all-to-all-start.1 = ((bf16[8,64,896]{2,1,0:T(8,128)(2,1)}), bf16[8,64,896]{2,1,0:T(8,128)(2,1)}, u32[]{:S(2)}, u32[]{:S(2)}) async-start(bf16[8,64,896]{2,1,0:T(8,128)(2,1)} %bitcast.71), calls=%async_computation.1 | async-start | bytes 1835008 | tf_op jit(solution)/shard_map/all_to_all | solution.py:75
  322.7 2.0 copy-start
  333.3 32.1 %all-to-all-start.2 = ((bf16[8,64,896]{2,1,0:T(8,128)(2,1)}), bf16[8,64,896]{2,1,0:T(8,128)(2,1)S(1)}, u32[]{:S(2)}, u32[]{:S(2)}) async-start(bf16[8,64,896]{2,1,0:T(8,128)(2,1)} %bitcast.18), calls=%async_computation.2 | async-start | bytes 1835008 | tf_op jit(solution)/shard_map/all_to_all | solution.py:75
  340.3 1.2 copy-start.2
  340.4 1.2 copy-start.8
  342.8 23.0 %collective-permute-start.9 = (bf16[64,7168]{1,0:T(8,128)(2,1)}, bf16[64,7168]{1,0:T(8,128)(2,1)S(1)}, u32[]{:S(2)}, u32[]{:S(2)}) collective-permute-start(bf16[64,7168]{1,0:T(8,128)(2,1)} %fusion.9), channel_id=1, source_target_pairs={{32,0},{64,32},{96,64},{128,96},{160,128},{192,160},{224,192},{33,... | collective-permute-start | bytes 2752520 | tf_op jit(solution)/shard_map/ppermute | solution.py:17
  365.6 1.2 copy-start.3
  365.6 1.2 copy-start.5
  368.5 14.2 %collective-permute-start.8 = (bf16[64,7168]{1,0:T(8,128)(2,1)}, bf16[64,7168]{1,0:T(8,128)(2,1)S(1)}, u32[]{:S(2)}, u32[]{:S(2)}) collective-permute-start(bf16[64,7168]{1,0:T(8,128)(2,1)} %get-tuple-element.11), channel_id=1, source_target_pairs={{0,32},{32,64},{64,96},{96,128},{128,160},{160,192},{192,224},{1,3... | collective-permute-start | bytes 2752520 | tf_op jit(solution)/shard_map/ppermute | solution.py:17
Sparse Core Ops, SparseCore 0:
  9.8 124.7 all-gather.10
  136.4 83.1 all-gather.6
  240.6 32.3 all-gather.8
  274.6 46.7 all-gather.12

commit v2 on v1

v2 whole, which is shorter than its diff:
```python
import functools

import jax
import jax.numpy as jnp
from jax import lax
from jax.experimental import pallas as pl
from jax.experimental.pallas import tpu as pltpu
from jax.sharding import Mesh, PartitionSpec as P

SPLIT = 8
VMEM_BYTES = 60 * 1024 * 1024


def shifted(block, axis, distance):
    n = lax.axis_size(axis)
    return lax.ppermute(block, axis, [(i, (i + distance) % n) for i in range(n)])


class Order:
    def __init__(self, mark):
        self.mark = mark

    def __call__(self, *values):
        self.mark, *values = lax.optimization_barrier((self.mark, *values))
        return values


class Ring:
    def __init__(self, block, axis):
        self.axis, self.n, self.step = axis, lax.axis_size(axis), 0
        self.last = (block, block)
        self.up, self.down = [block], []

    def send(self):
        up, down = self.last
        self.step += 1
        if self.step == self.n // 2:
            half = up.shape[0] // 2
            up, down = up[:half], down[half:]
        self.last = (shifted(up, self.axis, -1), shifted(down, self.axis, 1))

    def wait(self, order, *others):
        self.last, *others = order(self.last, *others)
        if self.step < self.n // 2:
            self.up.append(self.last[0])
            self.down.insert(0, self.last[1])
        return others

    def near(self):
        return self.up + self.down


def hidden_kernel(n_rows, *refs):
    rows, tails, weights = refs[:n_rows], refs[n_rows : 2 * n_rows], refs[2 * n_rows]
    hidden, route, total = refs[-3:]
    n_experts, _, pair = weights.shape
    n_hid = pair // 2
    step = pl.program_id(0)

    def joined(blocks):
        blocks = [r[...] for r in blocks]
        return blocks[0] if len(blocks) == 1 else jnp.concatenate(blocks, axis=0)

    @pl.when(step == 0)
    def _():
        total[...] = jnp.zeros_like(total)
        route[...] = joined(tails)

    x = joined(rows)
    for e in range(n_experts):
        at = slice(pair * e, pair * (e + 1))
        total[:, at] += jnp.dot(x, weights[e], preferred_element_type=jnp.float32)

    @pl.when(step == pl.num_programs(0) - 1)
    def _():
        named = route[...].astype(jnp.float32)
        gate, up = total[:, :n_hid], total[:, n_hid:pair]
        for e in range(1, n_experts):
            here, at = named == e, pair * e
            gate = jnp.where(here, total[:, at : at + n_hid], gate)
            up = jnp.where(here, total[:, at + n_hid : at + pair], up)
        hidden[...] = (gate / (1.0 + jnp.exp(-gate)) * up).astype(hidden.dtype)


def hidden_of(rows, weights, block):
    n_experts, width, pair = weights.shape
    n_hid = pair // 2
    count = sum(r.shape[0] for r in rows)
    made = jax.ShapeDtypeStruct((count, n_hid), jnp.bfloat16)
    return pl.pallas_call(
        functools.partial(hidden_kernel, len(rows)),
        grid=(width // block,),
        in_specs=[pl.BlockSpec((r.shape[0], block), lambda k: (0, k)) for r in rows]
        + [pl.BlockSpec((r.shape[0], n_hid), lambda k: (0, width // n_hid)) for r in rows]
        + [pl.BlockSpec((n_experts, block, pair), lambda k: (0, k, 0))],
        out_specs=[pl.BlockSpec((count, n_hid), lambda k: (0, 0))] * 2,
        out_shape=[made, made],
        scratch_shapes=[pltpu.VMEM((count, pair * n_experts), jnp.float32)],
        compiler_params=pltpu.CompilerParams(
            dimension_semantics=("arbitrary",), vmem_limit_bytes=VMEM_BYTES
        ),
        cost_estimate=pl.CostEstimate(
            flops=2 * count * width * pair * n_experts,
            bytes_accessed=2 * width * (count + pair * n_experts),
            transcendentals=count * n_hid,
        ),
    )(*rows, *rows, weights)


def out_kernel(n_experts, slices, route, *refs):
    hidden, weights = refs[:slices], refs[slices : slices + 2]
    out, total = refs[-2:]
    step = pl.program_id(0)
    named = route[...].astype(jnp.float32)

    @pl.when(step == 0)
    def _():
        total[...] = jnp.zeros_like(total)

    for now in range(slices // 2):

        @pl.when(step == now)
        def _():
            sums = total[...]
            for half, weight in zip((hidden[now], hidden[now + slices // 2]), weights):
                terms = [jnp.where(named == e, half[...], jnp.zeros_like(half)) for e in range(n_experts)]
                sums += jnp.dot(
                    jnp.concatenate(terms, axis=1),
                    weight[...].reshape(-1, weight.shape[2]),
                    preferred_element_type=jnp.float32,
                )
            total[...] = sums

    @pl.when(step == pl.num_programs(0) - 1)
    def _():
        out[...] = total[...].astype(out.dtype)


def out_of(route, hidden, weights):
    slices = len(hidden)
    n_experts, _, part = weights.shape
    count, n_hid = route.shape
    steps = slices // 2
    return pl.pallas_call(
        functools.partial(out_kernel, n_experts, slices),
        grid=(steps,),
        in_specs=[pl.BlockSpec((count, n_hid), lambda k: (0, 0))]
        + [pl.BlockSpec((count, n_hid), lambda k, at=at: (at, 0)) for _, at in hidden]
        + [pl.BlockSpec((n_experts, n_hid, part), lambda k: (0, k, 0))]
        + [pl.BlockSpec((n_experts, n_hid, part), lambda k: (0, k + steps, 0))],
        out_specs=pl.BlockSpec((count, part), lambda k: (0, 0)),
        out_shape=jax.ShapeDtypeStruct((count, part), jnp.bfloat16),
        scratch_shapes=[pltpu.VMEM((count, part), jnp.float32)],
        compiler_params=pltpu.CompilerParams(
            dimension_semantics=("arbitrary",), vmem_limit_bytes=VMEM_BYTES
        ),
        cost_estimate=pl.CostEstimate(
            flops=2 * count * slices * n_hid * n_experts * part,
            bytes_accessed=2 * slices * n_hid * (count + n_experts * part),
            transcendentals=0,
        ),
    )(route, *[h for h, _ in hidden], weights, weights)


def body(
    down_tokens, up_tokens, down_routes, up_routes, down_gates, up_gates, w_gate, w_up, w_down
):
    n_x, n_z = lax.axis_size("x"), lax.axis_size("z")
    me_x, me_z = lax.axis_index("x"), lax.axis_index("z")
    section = lax.axis_index("section")
    sections = lax.axis_size("section")
    even = section % 2 == 0
    rows, width = down_tokens.shape[1:]
    part = width // n_z
    hid = w_gate.shape[2]

    def streams(down, up):
        return jnp.where(even, up, down), jnp.where(even, down, up)

    tokens = streams(down_tokens[0], up_tokens[0])
    gates = streams(down_gates[0], up_gates[0])
    routes = streams(down_routes[0], up_routes[0])

    def marked(s):
        route = jnp.broadcast_to(routes[s].astype(jnp.bfloat16), (rows, hid))
        return jnp.concatenate([tokens[s], route], axis=1)

    def by_place(near, far, s):
        near = near.reshape(2, n_z - 1, rows, hid)[s]
        far = far.reshape(2, 1, rows, hid)[s]
        turned = jnp.concatenate([near[: n_z // 2], far, near[n_z // 2 :]], axis=0)
        return jnp.roll(turned, me_z, axis=0).reshape(-1, hid)

    def finished(s, out):
        out = out.transpose(1, 0, 2).reshape(rows, width)
        y = tokens[s].astype(jnp.float32) + gates[s] * out.astype(jnp.float32)
        return y.astype(jnp.bfloat16)

    order = Order(gates[0])
    gate_up = lax.all_gather(jnp.concatenate([w_gate[0], w_up[0]], axis=1), "x")
    b, a = Ring(marked(0), "z"), Ring(marked(1), "z")
    b.send()
    a.send()
    w_cut = w_down[0].reshape(hid, n_z, part).transpose(1, 0, 2)
    w_cut = lax.all_to_all(w_cut, "z", 0, 0)
    b.wait(order)
    b.send()
    a.wait(order)
    a.send()
    (w_cut,) = b.wait(order, w_cut)
    b.send()
    w_cut = jnp.roll(w_cut, -me_z, axis=0).reshape(n_z * hid, part)
    a.wait(order)
    a.send()
    b.wait(order)
    b.send()
    a.wait(order)
    a.send()
    down = lax.all_gather(w_cut, "x")
    near = jnp.concatenate(b.near() + a.near(), axis=0)
    near, near_route = hidden_of([near], gate_up, 1024)
    (near,) = b.wait(order, near)
    a.wait(order)
    far, far_route = hidden_of(b.last + a.last, gate_up, 1024)
    both = jnp.concatenate([by_place(near, far, s) for s in range(2)], axis=0)
    named = [by_place(near_route, far_route, s) for s in range(2)]
    h = Ring(both, "z")
    h.send()
    h.wait(order)
    h.send()
    h.wait(order)
    h.send()
    h.wait(order)
    h.send()
    h.wait(order)
    (down,) = order(down)

    def out_rows(s):
        hidden = [(piece, s) for piece in h.up] + [(h.last[s], 0)] + [(piece, s) for piece in h.down]
        return out_of(named[s], hidden, down).reshape(n_z, rows, part)

    out_b = lax.all_to_all(out_rows(0), "z", 0, 0)
    out_b, out_a = order(out_b, out_rows(1))
    out_a = lax.all_to_all(out_a, "z", 0, 0)
    gates = (order.mark, gates[1])
    results = [finished(0, out_b), finished(1, out_a)]

    near = [(i, i ^ 1) for i in range(sections)]
    away = [(i, min(max(((i + 1) ^ 1) - 1, 0), sections - 1)) for i in range(sections)]
    from_away = lax.ppermute(results[0], "section", away)
    from_near = lax.ppermute(results[1], "section", near)
    next_down = jnp.where(even, from_away, from_near)
    next_up = jnp.where(even, from_near, from_away)
    return next_down[None], next_up[None]


def solution(mesh):
    sections, devices = mesh.devices.shape
    fine = Mesh(mesh.devices.reshape(sections, devices // SPLIT, SPLIT), ("section", "x", "z"))
    by_rows = P("section", ("x", "z"), None)
    by_columns = P("section", None, ("x", "z"))
    return jax.shard_map(
        body,
        mesh=fine,
        in_specs=(by_rows,) * 6 + (by_columns, by_columns, by_rows),
        out_specs=(by_rows, by_rows),
        check_vma=False,
    )
```

time: 391 us -> 345 us (0.88)
  matrix products: 66.9 us -> 0 us
  waiting for transfers between devices: 223 us -> 163 us
  Pallas kernels: 0 us -> 44.4 us
  starting transfers between devices: 39.1 us -> 67.2 us
  local copies, waits for them, and re-layouts: 19.7 us -> 38 us
  blocking collectives: 13.8 us -> 0 us
    ppermute x8 -> x24, waiting for transfers between devices: 29.1 us -> 154 us  [shifted(): lax.ppermute(block, axis, [(i, (i + distance) % n) for i in range(n)])]
    all_gather x4 -> x2, waiting for transfers between devices: 104 us -> 0.01 us  [the longest x1 0.01 us: body(): gate_up = lax.all_gather(jnp.concatenate([w_gate[0], w_up[0]], axis=1), 'x')]
    all_to_all x3, waiting for transfers between devices: 78.2 us -> 7.23 us  [the longest x1 7.23 us: body(): out_b = lax.all_to_all(out_rows(0), 'z', 0, 0)]
    dot_general x20 -> x0, matrix products: 66.9 us -> none  [product(): return jnp.dot(rows, block, preferred_element_type=jnp.float32)]
    pallas_call x0 -> x4, Pallas kernels: none -> 44.4 us  [the longest x2 28 us: hidden_of(): pl.pallas_call(functools.partial(hidden_kernel, len(rows)), grid=(width /...]
    unnamed x26 -> x46, local copies, waits for them, and re-layouts: 6.21 us -> 25.9 us
    ppermute x2, starting transfers between devices: 7.3 us -> 25.2 us  [the longest x1 13.8 us: body(): from_away = lax.ppermute(results[0], 'section', away)]
    all_gather x1 -> x0, blocking collectives: 13.8 us -> none  [body(): lax.all_gather(jnp.concatenate([down_routes[0], up_routes[0]], axis=1), 'z')]
  transfers between devices with their start and end apart: 17 -> 31, of which waited for: 8 -> 22; matrix products, arithmetic and copies ran while one was open for 24% -> 14% of each run, Pallas kernels for 0% -> 11%
where the time goes in v2:
time: 345 us; the launch traced here: 344 us
  waiting for transfers between devices  163 us (47%)
  starting transfers between devices  67.2 us (19%)
  Pallas kernels  44.4 us (13%)
  local copies, waits for them, and re-layouts  38 us (11%)
  other arithmetic  17.1 us (5%)
  between operations  14.4 us (4%)
    ppermute x24, waiting for transfers between devices, shifted(): lax.ppermute(block, axis, [(i, (i + distance) % n) for i in range(n)])  154 us
    pallas_call x2, Pallas kernels, hidden_of(): pl.pallas_call(functools.partial(hidden_kernel, len(rows)), grid=(width /...  28 us
    unnamed x46, local copies, waits for them, and re-layouts  25.9 us
    ppermute x24, starting transfers between devices, shifted(): lax.ppermute(block, axis, [(i, (i + distance) % n) for i in range(n)])  23.4 us
    pallas_call x2, Pallas kernels, out_of(): pl.pallas_call(functools.partial(out_kernel, n_experts, slices), grid=(st...  16.4 us
    ppermute x1, starting transfers between devices, body(): from_away = lax.ppermute(results[0], 'section', away)  13.8 us
    ppermute x1, starting transfers between devices, body(): from_near = lax.ppermute(results[1], 'section', near)  11.5 us
    all_to_all x1, starting transfers between devices, body(): w_cut = lax.all_to_all(w_cut, 'z', 0, 0)  9.01 us
  transfers between devices with their start and end apart: 31, of which 22 were waited for; matrix products, arithmetic and copies ran while one was open for 14% of the time, Pallas kernels for 11%

profile of v2, /device:TPU:1, one launch (start us, length us, event | category | flops | bytes accessed | tf_op | source)
XLA Modules:
  0.0 344.0 jit_solution(18194985533210243928)
XLA Ops:
  7.2 4.2 %pad_maximum_fusion = bf16[7168,256]{1,0:T(8,128)(2,1)} fusion(bf16[7168,128]{1,0:T(8,128)(2,1)} %bitcast.65, bf16[7168,128]{1,0:T(8,128)(2,1)} %bitcast.66), kind=kLoop, calls=%fused_computation | loop fusion | flops 7340032 | bytes 7340032 | tf_op jit(solution)/shard_map/concatenate | solution.py:200
  11.5 1.9 copy.19
  13.4 1.5 copy.21
  14.9 9.0 %all-to-all-start = ((bf16[8,128,896]{2,1,0:T(8,128)(2,1)}), bf16[8,128,896]{2,1,0:T(8,128)(2,1)}, u32[]{:S(2)}, u32[]{:S(2)}) async-start(bf16[8,128,896]{2,1,0:T(8,128)(2,1)} %bitcast.56), calls=%async_computation | async-start | bytes 3670016 | tf_op jit(solution)/shard_map/all_to_all | solution.py:205
  24.0 1.3 select_bitcast_fusion.2
  26.5 2.6 collective-permute-start
  29.3 2.7 collective-permute-start.2
  32.1 52.8 %collective-permute-done = bf16[64,7296]{1,0:T(8,128)(2,1)} collective-permute-done((bf16[64,7296]{1,0:T(8,128)(2,1)S(1)}, bf16[64,7296]{1,0:T(8,128)(2,1)}, u32[]{:S(2)}, u32[]{:S(2)}) %collective-permute-start) | collective-permute-done | bytes 933920 | tf_op jit(solution)/shard_map/ppermute | solution.py:16
  84.8 1.6 collective-permute-done.1
  86.5 1.3 collective-permute-start.4
  87.9 16.9 %collective-permute-done.2 = bf16[64,7296]{1,0:T(8,128)(2,1)} collective-permute-done((bf16[64,7296]{1,0:T(8,128)(2,1)S(1)}, bf16[64,7296]{1,0:T(8,128)(2,1)}, u32[]{:S(2)}, u32[]{:S(2)}) %collective-permute-start.2) | collective-permute-done | bytes 933920 | tf_op jit(solution)/shard_map/ppermute | solution.py:16
  104.8 1.6 collective-permute-done.3
  106.5 1.3 collective-permute-start.6
  107.9 2.2 constant_dynamic-update-slice_fusion.12
  110.2 14.7 %collective-permute-done.4 = bf16[64,7296]{1,0:T(8,128)(2,1)} collective-permute-done((bf16[64,7296]{1,0:T(8,128)(2,1)}, bf16[64,7296]{1,0:T(8,128)(2,1)}, u32[]{:S(2)}, u32[]{:S(2)}) %collective-permute-start.4) | collective-permute-done | bytes 933920 | tf_op jit(solution)/shard_map/ppermute | solution.py:16
  124.9 1.6 collective-permute-done.5
  126.5 18.4 %collective-permute-done.6 = bf16[64,7296]{1,0:T(8,128)(2,1)} collective-permute-done((bf16[64,7296]{1,0:T(8,128)(2,1)}, bf16[64,7296]{1,0:T(8,128)(2,1)}, u32[]{:S(2)}, u32[]{:S(2)}) %collective-permute-start.6) | collective-permute-done | bytes 933920 | tf_op jit(solution)/shard_map/ppermute | solution.py:16
  144.9 1.6 collective-permute-done.7
  146.5 1.3 collective-permute-start.8
  148.0 2.5 collective-permute-start.10
  150.5 3.5 %fusion = bf16[8,128,896]{2,1,0:T(8,128)(2,1)} fusion(s32[]{:T(128)S(6)} %select_n.120, bf16[8,128,896]{2,1,0:T(8,128)(2,1)} %all-to-all-done), kind=kLoop, calls=%fused_computation.3 | loop fusion | flops 917504 | bytes 3670020 | tf_op jit(solution)/shard_map/jit(_roll_dynamic)/concatenate | solution.py:212
  154.0 2.2 constant_dynamic-update-slice_fusion.11
  156.2 11.4 %collective-permute-done.8 = bf16[64,7296]{1,0:T(8,128)(2,1)} collective-permute-done((bf16[64,7296]{1,0:T(8,128)(2,1)}, bf16[64,7296]{1,0:T(8,128)(2,1)}, u32[]{:S(2)}, u32[]{:S(2)}) %collective-permute-start.8) | collective-permute-done | bytes 933920 | tf_op jit(solution)/shard_map/ppermute | solution.py:16
  167.6 2.2 collective-permute-done.9
  169.8 2.3 constant_dynamic-update-slice_fusion.10
  172.1 2.3 constant_dynamic-update-slice_fusion.9
  174.4 1.9 slice.98
  176.2 1.8 slice.99
  178.1 2.2 constant_dynamic-update-slice_fusion.8
  180.2 7.4 %collective-permute-done.10 = bf16[64,7296]{1,0:T(8,128)(2,1)S(1)} collective-permute-done((bf16[64,7296]{1,0:T(8,128)(2,1)}, bf16[64,7296]{1,0:T(8,128)(2,1)S(1)}, u32[]{:S(2)}, u32[]{:S(2)}) %collective-permute-start.10) | collective-permute-done | bytes 933920 | tf_op jit(solution)/shard_map/ppermute | solution.py:16
  187.6 2.2 collective-permute-done.11
  189.8 1.1 collective-permute-start.12
  192.1 2.4 collective-permute-start.14
  194.5 1.8 slice.101
  196.3 2.2 constant_dynamic-update-slice_fusion.7
  199.5 2.2 constant_dynamic-update-slice_fusion.5
  201.7 2.2 constant_dynamic-update-slice_fusion.4
  205.0 2.2 constant_dynamic-update-slice_fusion.2
  207.2 2.2 constant_dynamic-update-slice_fusion.1
  210.4 18.4 %shard_map.104 = (bf16[896,128]{1,0:T(8,128)(2,1)}, bf16[896,128]{1,0:T(8,128)(2,1)}) custom-call(bf16[896,7296]{1,0:T(8,128)(2,1)} %constant_dynamic-update-slice_fusion.refs_0_.refs_1_, bf16[896,7296]{1,0:T(8,128)(2,1)} %constant_dynamic-update-slice_fusion.refs_0_.refs_1_, bf16[4,7168,256]{2,1,0:T(8,128)(2,1)} %bitcast.57), custom_call_target="tpu_custom_call" | custom-call | flops 13153337344 | bytes 27525120 | tf_op jit(solution)/shard_map/pallas_call | solution.py:90
  229.5 9.6 %shard_map.105 = (bf16[128,128]{1,0:T(8,128)(2,1)}, bf16[128,128]{1,0:T(8,128)(2,1)}) custom-call(bf16[32,7296]{1,0:T(8,128)(2,1)} %copy-done.1, bf16[32,7296]{1,0:T(8,128)(2,1)} %collective-permute-done.13.refs_1_.refs_5_, bf16[32,7296]{1,0:T(8,128)(2,1)} %collective-permute-done.14.refs_2_.refs_6_, ...), custom_call_target="tpu_custom_call" | custom-call | flops 1879048192 | bytes 16515072 | tf_op jit(solution)/shard_map/pallas_call | solution.py:90
  240.3 2.8 collective-permute-start.16
  243.0 3.3 collective-permute-done.16.refs_1_
  246.4 3.1 collective-permute-done.17.refs_7_
  249.6 1.4 collective-permute-start.19
  250.9 3.8 %collective-permute-done.18.refs_2_ = bf16[1024,128]{1,0:T(8,128)(2,1)S(1)} collective-permute-done((bf16[1024,128]{1,0:T(8,128)(2,1)S(1)}, bf16[1024,128]{1,0:T(8,128)(2,1)S(1)}, u32[]{:S(2)}, u32[]{:S(2)}) %collective-permute-start.18) | collective-permute-done | bytes 262176 | tf_op jit(solution)/shard_map/ppermute | solution.py:16
  254.7 1.3 collective-permute-done.19.refs_6_
  256.1 1.4 collective-permute-start.21
  257.5 4.9 %collective-permute-done.20.refs_3_ = bf16[1024,128]{1,0:T(8,128)(2,1)S(1)} collective-permute-done((bf16[1024,128]{1,0:T(8,128)(2,1)S(1)}, bf16[1024,128]{1,0:T(8,128)(2,1)S(1)}, u32[]{:S(2)}, u32[]{:S(2)}) %collective-permute-start.20) | collective-permute-done | bytes 262176 | tf_op jit(solution)/shard_map/ppermute | solution.py:16
  262.4 1.3 collective-permute-done.21.refs_5_
  263.8 1.5 collective-permute-start.23
  267.0 2.2 collective-permute-done.22.refs_4_
  269.2 1.3 collective-permute-done.23.refs_4_
  270.6 8.2 %shard_map.106 = bf16[512,896]{1,0:T(8,128)(2,1)} custom-call(bf16[512,128]{1,0:T(8,128)(2,1)} %bitcast.69, bf16[1024,128]{1,0:T(8,128)(2,1)} %copy-done, bf16[1024,128]{1,0:T(8,128)(2,1)} %copy-done.4, bf16[1024,128]{1,0:T(8,128)(2,1)} %copy-done.6, bf16[1024,128]{1,0:T(8,128)(2,1)} %copy-done.2, bf16[512,128]{1,0:T(8,128)(2,1)} %collective-permute-done.22.refs_4_, ...), custom_call_target="tpu_custom_call" | custom-call | flops 3758096384 | bytes 8388608 | tf_op jit(solution)/shard_map/pallas_call | solution.py:144
  278.8 4.8 %all-to-all-start.1 = ((bf16[8,64,896]{2,1,0:T(8,128)(2,1)}), bf16[8,64,896]{2,1,0:T(8,128)(2,1)S(1)}, u32[]{:S(2)}, u32[]{:S(2)}) async-start(bf16[8,64,896]{2,1,0:T(8,128)(2,1)} %bitcast.64), calls=%async_computation.1 | async-start | bytes 1835008 | tf_op jit(solution)/shard_map/all_to_all | solution.py:242
  283.6 8.2 %shard_map.107 = bf16[512,896]{1,0:T(8,128)(2,1)} custom-call(bf16[512,128]{1,0:T(8,128)(2,1)} %bitcast.68, bf16[1024,128]{1,0:T(8,128)(2,1)} %copy-done, bf16[1024,128]{1,0:T(8,128)(2,1)} %copy-done.4, bf16[1024,128]{1,0:T(8,128)(2,1)} %copy-done.6, bf16[1024,128]{1,0:T(8,128)(2,1)} %copy-done.2, bf16[512,128]{1,0:T(8,128)(2,1)} %collective-permute-done.23.refs_4_, ...), custom_call_target="tpu_custom_call" | custom-call | flops 3758096384 | bytes 8388608 | tf_op jit(solution)/shard_map/pallas_call | solution.py:144
  291.8 7.2 %all-to-all-done.1 = bf16[8,64,896]{2,1,0:T(8,128)(2,1)S(1)} async-done(((bf16[8,64,896]{2,1,0:T(8,128)(2,1)}), bf16[8,64,896]{2,1,0:T(8,128)(2,1)S(1)}, u32[]{:S(2)}, u32[]{:S(2)}) %all-to-all-start.1) | async-done | bytes 917536 | tf_op jit(solution)/shard_map/all_to_all | solution.py:242
  299.2 1.4 copy.17
  300.6 4.6 %all-to-all-start.2 = ((bf16[8,64,896]{2,1,0:T(8,128)(2,1)}), bf16[8,64,896]{2,1,0:T(8,128)(2,1)S(1)}, u32[]{:S(2)}, u32[]{:S(2)}) async-start(bf16[8,64,896]{2,1,0:T(8,128)(2,1)} %bitcast.63), calls=%async_computation.2 | async-start | bytes 1835008 | tf_op jit(solution)/shard_map/all_to_all | solution.py:244
  305.2 2.7 add_convert_fusion.1
  307.9 13.8 %collective-permute-start.24 = (bf16[64,7168]{1,0:T(8,128)(2,1)}, bf16[64,7168]{1,0:T(8,128)(2,1)S(1)}, u32[]{:S(2)}, u32[]{:S(2)}) collective-permute-start(bf16[64,7168]{1,0:T(8,128)(2,1)} %add_convert_fusion.1), channel_id=1, source_target_pairs={{0,0},{32,64},{64,32},{96,128},{128,96},{160,192},{192,160},{224,2... | collective-permute-start | bytes 2752520 | tf_op jit(solution)/shard_map/ppermute | solution.py:250
  322.2 11.5 %collective-permute-start.25 = (bf16[64,7168]{1,0:T(8,128)(2,1)S(1)}, bf16[64,7168]{1,0:T(8,128)(2,1)S(1)}, u32[]{:S(2)}, u32[]{:S(2)}) collective-permute-start(bf16[64,7168]{1,0:T(8,128)(2,1)S(1)} %add_convert_fusion), channel_id=1, source_target_pairs={{0,32},{32,0},{64,96},{96,64},{128,160},{160,128},{192,224},{224,1... | collective-permute-start | bytes 2752520 | tf_op jit(solution)/shard_map/ppermute | solution.py:251
  333.7 2.1 collective-permute-done.25
  335.8 1.3 select_bitcast_fusion
  (84 shorter events, 10.7 us)
Async XLA Ops:
  7.2 203.2 %all-gather.6.cloned.1.call-start = ((), (), s32[]{:S(2)}) async-start(), calls=%async_computation.4 | async-start | bytes 18350080 | tf_op jit(solution)/shard_map/all_gather | solution.py:200
  11.4 12.6 %copy-start.13 = (s32[1,64,1]{1,2,0:T(1,128)S(1)}, s32[1,64,1]{1,2,0:T(1,128)}, u32[]{:S(2)}) copy-start(s32[1,64,1]{1,2,0:T(1,128)} %param.13) | copy-start | bytes 772
  11.4 12.6 %copy-start.14 = (s32[1,64,1]{1,2,0:T(1,128)S(1)}, s32[1,64,1]{1,2,0:T(1,128)}, u32[]{:S(2)}) copy-start(s32[1,64,1]{1,2,0:T(1,128)} %param.14) | copy-start | bytes 772
  11.4 12.6 %copy-start.10 = (bf16[1,64,7168]{2,1,0:T(8,128)(2,1)S(1)}, bf16[1,64,7168]{2,1,0:T(8,128)(2,1)}, u32[]{:S(2)}) copy-start(bf16[1,64,7168]{2,1,0:T(8,128)(2,1)} %param.11) | copy-start | bytes 2752516
  13.4 18.7 %copy-start.15 = (f32[1,64,1]{1,2,0:T(1,128)S(1)}, f32[1,64,1]{1,2,0:T(1,128)}, u32[]{:S(2)}) copy-start(f32[1,64,1]{1,2,0:T(1,128)} %param.15) | copy-start | bytes 772
  13.4 18.7 %copy-start.16 = (f32[1,64,1]{1,2,0:T(1,128)S(1)}, f32[1,64,1]{1,2,0:T(1,128)}, u32[]{:S(2)}) copy-start(f32[1,64,1]{1,2,0:T(1,128)} %param.16) | copy-start | bytes 772
  14.9 111.6 %all-to-all-start = ((bf16[8,128,896]{2,1,0:T(8,128)(2,1)}), bf16[8,128,896]{2,1,0:T(8,128)(2,1)}, u32[]{:S(2)}, u32[]{:S(2)}) async-start(bf16[8,128,896]{2,1,0:T(8,128)(2,1)} %bitcast.56), calls=%async_computation | async-start | bytes 3670016 | tf_op jit(solution)/shard_map/all_to_all | solution.py:205
  23.9 246.6 %all-gather.4.cloned.1.call-start = ((), (), s32[]{:S(2)}) async-start(), calls=%async_computation.3 | async-start | bytes 9175040 | tf_op jit(solution)/shard_map/all_gather | solution.py:219
  26.5 58.3 %collective-permute-start = (bf16[64,7296]{1,0:T(8,128)(2,1)S(1)}, bf16[64,7296]{1,0:T(8,128)(2,1)}, u32[]{:S(2)}, u32[]{:S(2)}) collective-permute-start(bf16[64,7296]{1,0:T(8,128)(2,1)S(1)} %get-tuple-element.102), channel_id=1, source_target_pairs={{0,7},{1,0},{2,1},{3,2},{4,3},{5,4},{6,5},{7,6},{8,15},{9,8},{10,9... | collective-permute-start | bytes 2801672 | tf_op jit(solution)/shard_map/ppermute | solution.py:16
  29.1 57.3 %collective-permute-start.1 = (bf16[64,7296]{1,0:T(8,128)(2,1)S(1)}, bf16[64,7296]{1,0:T(8,128)(2,1)}, u32[]{:S(2)}, u32[]{:S(2)}) collective-permute-start(bf16[64,7296]{1,0:T(8,128)(2,1)S(1)} %get-tuple-element.102), channel_id=1, source_target_pairs={{0,1},{1,2},{2,3},{3,4},{4,5},{5,6},{6,7},{7,0},{8,9},{9,10},{10,1... | collective-permute-start | bytes 2801672 | tf_op jit(solution)/shard_map/ppermute | solution.py:16
  29.3 75.5 %collective-permute-start.2 = (bf16[64,7296]{1,0:T(8,128)(2,1)S(1)}, bf16[64,7296]{1,0:T(8,128)(2,1)}, u32[]{:S(2)}, u32[]{:S(2)}) collective-permute-start(bf16[64,7296]{1,0:T(8,128)(2,1)S(1)} %pad_maximum_fusion.2), channel_id=1, source_target_pairs={{0,7},{1,0},{2,1},{3,2},{4,3},{5,4},{6,5},{7,6},{8,15},{9,8},{10,9... | collective-permute-start | bytes 2801672 | tf_op jit(solution)/shard_map/ppermute | solution.py:16
  32.0 74.4 %collective-permute-start.3 = (bf16[64,7296]{1,0:T(8,128)(2,1)S(1)}, bf16[64,7296]{1,0:T(8,128)(2,1)S(1)}, u32[]{:S(2)}, u32[]{:S(2)}) collective-permute-start(bf16[64,7296]{1,0:T(8,128)(2,1)S(1)} %pad_maximum_fusion.2), channel_id=1, source_target_pairs={{0,1},{1,2},{2,3},{3,4},{4,5},{5,6},{6,7},{7,0},{8,9},{9,10},{10,1... | collective-permute-start | bytes 2801672 | tf_op jit(solution)/shard_map/ppermute | solution.py:16
  86.5 38.4 %collective-permute-start.4 = (bf16[64,7296]{1,0:T(8,128)(2,1)}, bf16[64,7296]{1,0:T(8,128)(2,1)}, u32[]{:S(2)}, u32[]{:S(2)}) collective-permute-start(bf16[64,7296]{1,0:T(8,128)(2,1)} %collective-permute-done), channel_id=1, source_target_pairs={{0,7},{1,0},{2,1},{3,2},{4,3},{5,4},{6,5},{7,6},{8,15},{9,8},{10,9... | collective-permute-start | bytes 2801672 | tf_op jit(solution)/shard_map/ppermute | solution.py:16
  87.8 38.7 %collective-permute-start.5 = (bf16[64,7296]{1,0:T(8,128)(2,1)}, bf16[64,7296]{1,0:T(8,128)(2,1)}, u32[]{:S(2)}, u32[]{:S(2)}) collective-permute-start(bf16[64,7296]{1,0:T(8,128)(2,1)} %collective-permute-done.1), channel_id=1, source_target_pairs={{0,1},{1,2},{2,3},{3,4},{4,5},{5,6},{6,7},{7,0},{8,9},{9,10},{10,1... | collective-permute-start | bytes 2801672 | tf_op jit(solution)/shard_map/ppermute | solution.py:16
  106.5 41.3 %copy-start.8 = (bf16[64,7296]{1,0:T(8,128)(2,1)}, bf16[64,7296]{1,0:T(8,128)(2,1)S(1)}, u32[]{:S(2)}) copy-start(bf16[64,7296]{1,0:T(8,128)(2,1)S(1)} %collective-permute-done.3) | copy-start | bytes 2801668
  106.5 38.4 %collective-permute-start.6 = (bf16[64,7296]{1,0:T(8,128)(2,1)}, bf16[64,7296]{1,0:T(8,128)(2,1)}, u32[]{:S(2)}, u32[]{:S(2)}) collective-permute-start(bf16[64,7296]{1,0:T(8,128)(2,1)} %collective-permute-done.2), channel_id=1, source_target_pairs={{0,7},{1,0},{2,1},{3,2},{4,3},{5,4},{6,5},{7,6},{8,15},{9,8},{10,9... | collective-permute-start | bytes 2801672 | tf_op jit(solution)/shard_map/ppermute | solution.py:16
  107.8 38.7 %collective-permute-start.7 = (bf16[64,7296]{1,0:T(8,128)(2,1)S(1)}, bf16[64,7296]{1,0:T(8,128)(2,1)}, u32[]{:S(2)}, u32[]{:S(2)}) collective-permute-start(bf16[64,7296]{1,0:T(8,128)(2,1)S(1)} %collective-permute-done.3), channel_id=1, source_target_pairs={{0,1},{1,2},{2,3},{3,4},{4,5},{5,6},{6,7},{7,0},{8,9},{9,10},{10,1... | collective-permute-start | bytes 2801672 | tf_op jit(solution)/shard_map/ppermute | solution.py:16
  146.5 21.1 %collective-permute-start.8 = (bf16[64,7296]{1,0:T(8,128)(2,1)}, bf16[64,7296]{1,0:T(8,128)(2,1)}, u32[]{:S(2)}, u32[]{:S(2)}) collective-permute-start(bf16[64,7296]{1,0:T(8,128)(2,1)} %collective-permute-done.4), channel_id=1, source_target_pairs={{0,7},{1,0},{2,1},{3,2},{4,3},{5,4},{6,5},{7,6},{8,15},{9,8},{10,9... | collective-permute-start | bytes 2801672 | tf_op jit(solution)/shard_map/ppermute | solution.py:16
  147.8 22.0 %collective-permute-start.9 = (bf16[64,7296]{1,0:T(8,128)(2,1)}, bf16[64,7296]{1,0:T(8,128)(2,1)}, u32[]{:S(2)}, u32[]{:S(2)}) collective-permute-start(bf16[64,7296]{1,0:T(8,128)(2,1)} %collective-permute-done.5), channel_id=1, source_target_pairs={{0,1},{1,2},{2,3},{3,4},{4,5},{5,6},{6,7},{7,0},{8,9},{9,10},{10,1... | collective-permute-start | bytes 2801672 | tf_op jit(solution)/shard_map/ppermute | solution.py:16
  148.0 39.6 %collective-permute-start.10 = (bf16[64,7296]{1,0:T(8,128)(2,1)}, bf16[64,7296]{1,0:T(8,128)(2,1)S(1)}, u32[]{:S(2)}, u32[]{:S(2)}) collective-permute-start(bf16[64,7296]{1,0:T(8,128)(2,1)} %collective-permute-done.6), channel_id=1, source_target_pairs={{0,7},{1,0},{2,1},{3,2},{4,3},{5,4},{6,5},{7,6},{8,15},{9,8},{10,9... | collective-permute-start | bytes 2801672 | tf_op jit(solution)/shard_map/ppermute | solution.py:16
  150.5 39.3 %collective-permute-start.11 = (bf16[64,7296]{1,0:T(8,128)(2,1)}, bf16[64,7296]{1,0:T(8,128)(2,1)}, u32[]{:S(2)}, u32[]{:S(2)}) collective-permute-start(bf16[64,7296]{1,0:T(8,128)(2,1)} %collective-permute-done.7), channel_id=1, source_target_pairs={{0,1},{1,2},{2,3},{3,4},{4,5},{5,6},{6,7},{7,0},{8,9},{9,10},{10,1... | collective-permute-start | bytes 2801672 | tf_op jit(solution)/shard_map/ppermute | solution.py:16
  180.2 29.2 %copy-start.9 = (bf16[64,7296]{1,0:T(8,128)(2,1)S(1)}, bf16[64,7296]{1,0:T(8,128)(2,1)}, u32[]{:S(2)}) copy-start(bf16[64,7296]{1,0:T(8,128)(2,1)} %copy-done.8) | copy-start | bytes 2801668
  189.8 38.9 %collective-permute-start.12 = (bf16[32,7296]{1,0:T(8,128)(2,1)}, bf16[32,7296]{1,0:T(8,128)(2,1)S(1)}, u32[]{:S(2)}, u32[]{:S(2)}) collective-permute-start(bf16[32,7296]{1,0:T(8,128)(2,1)} %slice.98), channel_id=1, source_target_pairs={{0,7},{1,0},{2,1},{3,2},{4,3},{5,4},{6,5},{7,6},{8,15},{9,8},{10,9... | collective-permute-start | bytes 1400840 | tf_op jit(solution)/shard_map/ppermute | solution.py:16
  191.0 37.8 %collective-permute-start.13 = (bf16[32,7296]{1,0:T(8,128)(2,1)}, bf16[32,7296]{1,0:T(8,128)(2,1)}, u32[]{:S(2)}, u32[]{:S(2)}) collective-permute-start(bf16[32,7296]{1,0:T(8,128)(2,1)} %slice.99), channel_id=1, source_target_pairs={{0,1},{1,2},{2,3},{3,4},{4,5},{5,6},{6,7},{7,0},{8,9},{9,10},{10,1... | collective-permute-start | bytes 1400840 | tf_op jit(solution)/shard_map/ppermute | solution.py:16
  192.1 36.7 %collective-permute-start.14 = (bf16[32,7296]{1,0:T(8,128)(2,1)}, bf16[32,7296]{1,0:T(8,128)(2,1)}, u32[]{:S(2)}, u32[]{:S(2)}) collective-permute-start(bf16[32,7296]{1,0:T(8,128)(2,1)} %slice.100), channel_id=1, source_target_pairs={{0,7},{1,0},{2,1},{3,2},{4,3},{5,4},{6,5},{7,6},{8,15},{9,8},{10,9... | collective-permute-start | bytes 1400840 | tf_op jit(solution)/shard_map/ppermute | solution.py:16
  196.3 32.5 %collective-permute-start.15 = (bf16[32,7296]{1,0:T(8,128)(2,1)}, bf16[32,7296]{1,0:T(8,128)(2,1)}, u32[]{:S(2)}, u32[]{:S(2)}) collective-permute-start(bf16[32,7296]{1,0:T(8,128)(2,1)} %slice.101), channel_id=1, source_target_pairs={{0,1},{1,2},{2,3},{3,4},{4,5},{5,6},{6,7},{7,0},{8,9},{9,10},{10,1... | collective-permute-start | bytes 1400840 | tf_op jit(solution)/shard_map/ppermute | solution.py:16
  228.8 0.8 copy-start.1
  228.8 11.1 %copy-start.12 = (bf16[896,128]{1,0:T(8,128)(2,1)S(1)}, bf16[896,128]{1,0:T(8,128)(2,1)}, u32[]{:S(2)}) copy-start(bf16[896,128]{1,0:T(8,128)(2,1)} %get-tuple-element.71) | copy-start | bytes 688132
  228.8 28.7 %copy-start.11 = (bf16[896,128]{1,0:T(8,128)(2,1)S(1)}, bf16[896,128]{1,0:T(8,128)(2,1)}, u32[]{:S(2)}) copy-start(bf16[896,128]{1,0:T(8,128)(2,1)} %get-tuple-element.89) | copy-start | bytes 688132
  240.3 30.3 %copy-start = (bf16[1024,128]{1,0:T(8,128)(2,1)}, bf16[1024,128]{1,0:T(8,128)(2,1)S(1)}, u32[]{:S(2)}) copy-start(bf16[1024,128]{1,0:T(8,128)(2,1)S(1)} %pad_maximum_fusion.3.refs_0_) | copy-start | bytes 786436
  240.3 6.1 %collective-permute-start.16 = (bf16[1024,128]{1,0:T(8,128)(2,1)S(1)}, bf16[1024,128]{1,0:T(8,128)(2,1)S(1)}, u32[]{:S(2)}, u32[]{:S(2)}) collective-permute-start(bf16[1024,128]{1,0:T(8,128)(2,1)S(1)} %pad_maximum_fusion.3.refs_0_), channel_id=1, source_target_pairs={{0,7},{1,0},{2,1},{3,2},{4,3},{5,4},{6,5},{7,6},{8,15},{9,8},{10,9... | collective-permute-start | bytes 786440 | tf_op jit(solution)/shard_map/ppermute | solution.py:16
  243.0 6.4 %collective-permute-start.17 = (bf16[1024,128]{1,0:T(8,128)(2,1)S(1)}, bf16[1024,128]{1,0:T(8,128)(2,1)S(1)}, u32[]{:S(2)}, u32[]{:S(2)}) collective-permute-start(bf16[1024,128]{1,0:T(8,128)(2,1)S(1)} %pad_maximum_fusion.3.refs_0_), channel_id=1, source_target_pairs={{0,1},{1,2},{2,3},{3,4},{4,5},{5,6},{6,7},{7,0},{8,9},{9,10},{10,1... | collective-permute-start | bytes 786440 | tf_op jit(solution)/shard_map/ppermute | solution.py:16
  246.4 24.2 %copy-start.4 = (bf16[1024,128]{1,0:T(8,128)(2,1)}, bf16[1024,128]{1,0:T(8,128)(2,1)S(1)}, u32[]{:S(2)}) copy-start(bf16[1024,128]{1,0:T(8,128)(2,1)S(1)} %collective-permute-done.16.refs_1_) | copy-start | bytes 786436
  249.5 21.1 %copy-start.5 = (bf16[1024,128]{1,0:T(8,128)(2,1)}, bf16[1024,128]{1,0:T(8,128)(2,1)S(1)}, u32[]{:S(2)}) copy-start(bf16[1024,128]{1,0:T(8,128)(2,1)S(1)} %collective-permute-done.17.refs_7_) | copy-start | bytes 786436
  249.5 5.2 %collective-permute-start.18 = (bf16[1024,128]{1,0:T(8,128)(2,1)S(1)}, bf16[1024,128]{1,0:T(8,128)(2,1)S(1)}, u32[]{:S(2)}, u32[]{:S(2)}) collective-permute-start(bf16[1024,128]{1,0:T(8,128)(2,1)S(1)} %collective-permute-done.16.refs_1_), channel_id=1, source_target_pairs={{0,7},{1,0},{2,1},{3,2},{4,3},{5,4},{6,5},{7,6},{8,15},{9,8},{10,9... | collective-permute-start | bytes 786440 | tf_op jit(solution)/shard_map/ppermute | solution.py:16
  249.6 6.4 %collective-permute-start.19 = (bf16[1024,128]{1,0:T(8,128)(2,1)S(1)}, bf16[1024,128]{1,0:T(8,128)(2,1)S(1)}, u32[]{:S(2)}, u32[]{:S(2)}) collective-permute-start(bf16[1024,128]{1,0:T(8,128)(2,1)S(1)} %collective-permute-done.17.refs_7_), channel_id=1, source_target_pairs={{0,1},{1,2},{2,3},{3,4},{4,5},{5,6},{6,7},{7,0},{8,9},{9,10},{10,1... | collective-permute-start | bytes 786440 | tf_op jit(solution)/shard_map/ppermute | solution.py:16
  254.7 15.9 %copy-start.6 = (bf16[1024,128]{1,0:T(8,128)(2,1)}, bf16[1024,128]{1,0:T(8,128)(2,1)S(1)}, u32[]{:S(2)}) copy-start(bf16[1024,128]{1,0:T(8,128)(2,1)S(1)} %collective-permute-done.18.refs_2_) | copy-start | bytes 786436
  256.0 7.7 %copy-start.7 = (bf16[1024,128]{1,0:T(8,128)(2,1)}, bf16[1024,128]{1,0:T(8,128)(2,1)S(1)}, u32[]{:S(2)}) copy-start(bf16[1024,128]{1,0:T(8,128)(2,1)S(1)} %collective-permute-done.19.refs_6_) | copy-start | bytes 786436
  256.0 6.4 %collective-permute-start.20 = (bf16[1024,128]{1,0:T(8,128)(2,1)S(1)}, bf16[1024,128]{1,0:T(8,128)(2,1)S(1)}, u32[]{:S(2)}, u32[]{:S(2)}) collective-permute-start(bf16[1024,128]{1,0:T(8,128)(2,1)S(1)} %collective-permute-done.18.refs_2_), channel_id=1, source_target_pairs={{0,7},{1,0},{2,1},{3,2},{4,3},{5,4},{6,5},{7,6},{8,15},{9,8},{10,9... | collective-permute-start | bytes 786440 | tf_op jit(solution)/shard_map/ppermute | solution.py:16
  256.1 7.6 %collective-permute-start.21 = (bf16[1024,128]{1,0:T(8,128)(2,1)S(1)}, bf16[1024,128]{1,0:T(8,128)(2,1)S(1)}, u32[]{:S(2)}, u32[]{:S(2)}) collective-permute-start(bf16[1024,128]{1,0:T(8,128)(2,1)S(1)} %collective-permute-done.19.refs_6_), channel_id=1, source_target_pairs={{0,1},{1,2},{2,3},{3,4},{4,5},{5,6},{6,7},{7,0},{8,9},{9,10},{10,1... | collective-permute-start | bytes 786440 | tf_op jit(solution)/shard_map/ppermute | solution.py:16
  262.4 8.2 %copy-start.2 = (bf16[1024,128]{1,0:T(8,128)(2,1)}, bf16[1024,128]{1,0:T(8,128)(2,1)S(1)}, u32[]{:S(2)}) copy-start(bf16[1024,128]{1,0:T(8,128)(2,1)S(1)} %collective-permute-done.20.refs_3_) | copy-start | bytes 786436
  263.7 6.9 %copy-start.3 = (bf16[1024,128]{1,0:T(8,128)(2,1)}, bf16[1024,128]{1,0:T(8,128)(2,1)S(1)}, u32[]{:S(2)}) copy-start(bf16[1024,128]{1,0:T(8,128)(2,1)S(1)} %collective-permute-done.21.refs_5_) | copy-start | bytes 786436
  263.7 5.5 %collective-permute-start.22 = (bf16[512,128]{1,0:T(8,128)(2,1)S(1)}, bf16[512,128]{1,0:T(8,128)(2,1)}, u32[]{:S(2)}, u32[]{:S(2)}) collective-permute-start(bf16[512,128]{1,0:T(8,128)(2,1)S(1)} %slice.112), channel_id=1, source_target_pairs={{0,7},{1,0},{2,1},{3,2},{4,3},{5,4},{6,5},{7,6},{8,15},{9,8},{10,9... | collective-permute-start | bytes 393224 | tf_op jit(solution)/shard_map/ppermute | solution.py:16
  263.8 6.8 %collective-permute-start.23 = (bf16[512,128]{1,0:T(8,128)(2,1)S(1)}, bf16[512,128]{1,0:T(8,128)(2,1)}, u32[]{:S(2)}, u32[]{:S(2)}) collective-permute-start(bf16[512,128]{1,0:T(8,128)(2,1)S(1)} %slice.113), channel_id=1, source_target_pairs={{0,1},{1,2},{2,3},{3,4},{4,5},{5,6},{6,7},{7,0},{8,9},{9,10},{10,1... | collective-permute-start | bytes 393224 | tf_op jit(solution)/shard_map/ppermute | solution.py:16
  278.8 20.2 %all-to-all-start.1 = ((bf16[8,64,896]{2,1,0:T(8,128)(2,1)}), bf16[8,64,896]{2,1,0:T(8,128)(2,1)S(1)}, u32[]{:S(2)}, u32[]{:S(2)}) async-start(bf16[8,64,896]{2,1,0:T(8,128)(2,1)} %bitcast.64), calls=%async_computation.1 | async-start | bytes 1835008 | tf_op jit(solution)/shard_map/all_to_all | solution.py:242
  300.6 21.1 %all-to-all-start.2 = ((bf16[8,64,896]{2,1,0:T(8,128)(2,1)}), bf16[8,64,896]{2,1,0:T(8,128)(2,1)S(1)}, u32[]{:S(2)}, u32[]{:S(2)}) async-start(bf16[8,64,896]{2,1,0:T(8,128)(2,1)} %bitcast.63), calls=%async_computation.2 | async-start | bytes 1835008 | tf_op jit(solution)/shard_map/all_to_all | solution.py:244
  307.9 25.9 %collective-permute-start.24 = (bf16[64,7168]{1,0:T(8,128)(2,1)}, bf16[64,7168]{1,0:T(8,128)(2,1)S(1)}, u32[]{:S(2)}, u32[]{:S(2)}) collective-permute-start(bf16[64,7168]{1,0:T(8,128)(2,1)} %add_convert_fusion.1), channel_id=1, source_target_pairs={{0,0},{32,64},{64,32},{96,128},{128,96},{160,192},{192,160},{224,2... | collective-permute-start | bytes 2752520 | tf_op jit(solution)/shard_map/ppermute | solution.py:250
  322.2 13.6 %collective-permute-start.25 = (bf16[64,7168]{1,0:T(8,128)(2,1)S(1)}, bf16[64,7168]{1,0:T(8,128)(2,1)S(1)}, u32[]{:S(2)}, u32[]{:S(2)}) collective-permute-start(bf16[64,7168]{1,0:T(8,128)(2,1)S(1)} %add_convert_fusion), channel_id=1, source_target_pairs={{0,32},{32,0},{64,96},{96,64},{128,160},{160,128},{192,224},{224,1... | collective-permute-start | bytes 2752520 | tf_op jit(solution)/shard_map/ppermute | solution.py:251
Sparse Core Ops, SparseCore 0:
  11.6 142.6 all-gather.5
  156.1 77.8 all-gather.3

commit v3 on v2

--- a/solution.py
+++ b/solution.py
@@ -51,40 +51,36 @@
 
 
 def hidden_kernel(n_rows, *refs):
-    rows, tails, weights = refs[:n_rows], refs[n_rows : 2 * n_rows], refs[2 * n_rows]
+    rows, tails = refs[:n_rows], refs[n_rows : 2 * n_rows]
+    weights = refs[2 * n_rows : -3]
     hidden, route, total = refs[-3:]
-    n_experts, _, pair = weights.shape
-    n_hid = pair // 2
+    n_experts, n_hid = len(weights) // 2, hidden.shape[1]
     step = pl.program_id(0)
 
-    def joined(blocks):
-        blocks = [r[...] for r in blocks]
-        return blocks[0] if len(blocks) == 1 else jnp.concatenate(blocks, axis=0)
-
     @pl.when(step == 0)
     def _():
         total[...] = jnp.zeros_like(total)
-        route[...] = joined(tails)
-
-    x = joined(rows)
+        route[...] = jnp.concatenate([r[...] for r in tails], axis=0)
+
+    x = jnp.concatenate([r[...] for r in rows], axis=0)
     for e in range(n_experts):
-        at = slice(pair * e, pair * (e + 1))
-        total[:, at] += jnp.dot(x, weights[e], preferred_element_type=jnp.float32)
+        at = slice(2 * n_hid * e, 2 * n_hid * (e + 1))
+        pair = jnp.concatenate([weights[2 * e][0], weights[2 * e + 1][0]], axis=1)
+        total[:, at] += jnp.dot(x, pair, preferred_element_type=jnp.float32)
 
     @pl.when(step == pl.num_programs(0) - 1)
     def _():
         named = route[...].astype(jnp.float32)
-        gate, up = total[:, :n_hid], total[:, n_hid:pair]
+        gate, up = total[:, :n_hid], total[:, n_hid : 2 * n_hid]
         for e in range(1, n_experts):
-            here, at = named == e, pair * e
+            here, at = named == e, 2 * n_hid * e
             gate = jnp.where(here, total[:, at : at + n_hid], gate)
-            up = jnp.where(here, total[:, at + n_hid : at + pair], up)
+            up = jnp.where(here, total[:, at + n_hid : at + 2 * n_hid], up)
         hidden[...] = (gate / (1.0 + jnp.exp(-gate)) * up).astype(hidden.dtype)
 
 
-def hidden_of(rows, weights, block):
-    n_experts, width, pair = weights.shape
-    n_hid = pair // 2
+def hidden_of(rows, gates, ups, block):
+    n_experts, width, n_hid = gates.shape
     count = sum(r.shape[0] for r in rows)
     made = jax.ShapeDtypeStruct((count, n_hid), jnp.bfloat16)
     return pl.pallas_call(
@@ -92,23 +88,23 @@
         grid=(width // block,),
         in_specs=[pl.BlockSpec((r.shape[0], block), lambda k: (0, k)) for r in rows]
         + [pl.BlockSpec((r.shape[0], n_hid), lambda k: (0, width // n_hid)) for r in rows]
-        + [pl.BlockSpec((n_experts, block, pair), lambda k: (0, k, 0))],
+        + [pl.BlockSpec((1, block, n_hid), lambda k, e=e: (e, k, 0)) for e in range(n_experts) for _ in range(2)],
         out_specs=[pl.BlockSpec((count, n_hid), lambda k: (0, 0))] * 2,
         out_shape=[made, made],
-        scratch_shapes=[pltpu.VMEM((count, pair * n_experts), jnp.float32)],
+        scratch_shapes=[pltpu.VMEM((count, 2 * n_hid * n_experts), jnp.float32)],
         compiler_params=pltpu.CompilerParams(
             dimension_semantics=("arbitrary",), vmem_limit_bytes=VMEM_BYTES
         ),
         cost_estimate=pl.CostEstimate(
-            flops=2 * count * width * pair * n_experts,
-            bytes_accessed=2 * width * (count + pair * n_experts),
+            flops=4 * count * width * n_hid * n_experts,
+            bytes_accessed=2 * width * (count + 2 * n_hid * n_experts),
             transcendentals=count * n_hid,
         ),
-    )(*rows, *rows, weights)
+    )(*rows, *rows, *[gates, ups] * n_experts)
 
 
 def out_kernel(n_experts, slices, route, *refs):
-    hidden, weights = refs[:slices], refs[slices : slices + 2]
+    hidden, weights = refs[:slices], refs[slices:-2]
     out, total = refs[-2:]
     step = pl.program_id(0)
     named = route[...].astype(jnp.float32)
@@ -122,11 +118,11 @@
         @pl.when(step == now)
         def _():
             sums = total[...]
-            for half, weight in zip((hidden[now], hidden[now + slices // 2]), weights):
+            for at, half in enumerate((hidden[now], hidden[now + slices // 2])):
                 terms = [jnp.where(named == e, half[...], jnp.zeros_like(half)) for e in range(n_experts)]
                 sums += jnp.dot(
                     jnp.concatenate(terms, axis=1),
-                    weight[...].reshape(-1, weight.shape[2]),
+                    jnp.concatenate([weights[2 * e + at][0] for e in range(n_experts)], axis=0),
                     preferred_element_type=jnp.float32,
                 )
             total[...] = sums
@@ -146,8 +142,11 @@
         grid=(steps,),
         in_specs=[pl.BlockSpec((count, n_hid), lambda k: (0, 0))]
         + [pl.BlockSpec((count, n_hid), lambda k, at=at: (at, 0)) for _, at in hidden]
-        + [pl.BlockSpec((n_experts, n_hid, part), lambda k: (0, k, 0))]
-        + [pl.BlockSpec((n_experts, n_hid, part), lambda k: (0, k + steps, 0))],
+        + [
+            pl.BlockSpec((1, n_hid, part), lambda k, e=e, at=at: (e, k + at, 0))
+            for e in range(n_experts)
+            for at in (0, steps)
+        ],
         out_specs=pl.BlockSpec((count, part), lambda k: (0, 0)),
         out_shape=jax.ShapeDtypeStruct((count, part), jnp.bfloat16),
         scratch_shapes=[pltpu.VMEM((count, part), jnp.float32)],
@@ -159,7 +158,7 @@
             bytes_accessed=2 * slices * n_hid * (count + n_experts * part),
             transcendentals=0,
         ),
-    )(route, *[h for h, _ in hidden], weights, weights)
+    )(route, *[h for h, _ in hidden], *[weights] * (2 * n_experts))
 
 
 def body(
@@ -185,10 +184,12 @@
         route = jnp.broadcast_to(routes[s].astype(jnp.bfloat16), (rows, hid))
         return jnp.concatenate([tokens[s], route], axis=1)
 
-    def by_place(near, far, s):
-        near = near.reshape(2, n_z - 1, rows, hid)[s]
-        far = far.reshape(2, 1, rows, hid)[s]
-        turned = jnp.concatenate([near[: n_z // 2], far, near[n_z // 2 :]], axis=0)
+    def by_place(first, second, s):
+        n_first = 2 * (n_z // 2 - 2) + 1
+        first = first.reshape(2, n_first, rows, hid)[s]
+        second = second.reshape(2, n_z - n_first, rows, hid)[s]
+        keep = (n_first + 1) // 2
+        turned = jnp.concatenate([first[:keep], second, first[keep:]], axis=0)
         return jnp.roll(turned, me_z, axis=0).reshape(-1, hid)
 
     def finished(s, out):
@@ -197,7 +198,8 @@
         return y.astype(jnp.bfloat16)
 
     order = Order(gates[0])
-    gate_up = lax.all_gather(jnp.concatenate([w_gate[0], w_up[0]], axis=1), "x")
+    gate_all = lax.all_gather(w_gate[0], "x")
+    up_all = lax.all_gather(w_up[0], "x")
     b, a = Ring(marked(0), "z"), Ring(marked(1), "z")
     b.send()
     a.send()
@@ -210,20 +212,21 @@
     (w_cut,) = b.wait(order, w_cut)
     b.send()
     w_cut = jnp.roll(w_cut, -me_z, axis=0).reshape(n_z * hid, part)
+    down = lax.all_gather(w_cut, "x")
     a.wait(order)
+    first = b.near() + a.near()
     a.send()
     b.wait(order)
     b.send()
+    first, first_route = hidden_of(first, gate_all, up_all, 1792)
+    (first,) = a.wait(order, first)
+    a.send()
+    b.wait(order)
     a.wait(order)
-    a.send()
-    down = lax.all_gather(w_cut, "x")
-    near = jnp.concatenate(b.near() + a.near(), axis=0)
-    near, near_route = hidden_of([near], gate_up, 1024)
-    (near,) = b.wait(order, near)
-    a.wait(order)
-    far, far_route = hidden_of(b.last + a.last, gate_up, 1024)
-    both = jnp.concatenate([by_place(near, far, s) for s in range(2)], axis=0)
-    named = [by_place(near_route, far_route, s) for s in range(2)]
+    second = [p for ring in (b, a) for p in (ring.up[-1], *ring.last, ring.down[0])]
+    second, second_route = hidden_of(second, gate_all, up_all, 1792)
+    both = jnp.concatenate([by_place(first, second, s) for s in range(2)], axis=0)
+    named = [by_place(first_route, second_route, s) for s in range(2)]
     h = Ring(both, "z")
     h.send()
     h.wait(order)

time: 345 us -> 331 us (0.959)
  waiting for transfers between devices: 163 us -> 202 us
  local copies, waits for them, and re-layouts: 38 us -> 9.64 us
  starting transfers between devices: 67.2 us -> 52.5 us
  other arithmetic: 17.1 us -> 9.78 us
    unnamed x46 -> x57, local copies, waits for them, and re-layouts: 25.9 us -> 1.72 us
    ppermute x24, waiting for transfers between devices: 154 us -> 172 us  [shifted(): lax.ppermute(block, axis, [(i, (i + distance) % n) for i in range(n)])]
    all_to_all x1, waiting for transfers between devices: 0.01 us -> 12.4 us  [body(): out_a = lax.all_to_all(out_a, 'z', 0, 0)]
    ppermute x1, starting transfers between devices: 11.5 us -> 4.41 us  [body(): from_near = lax.ppermute(results[1], 'section', near)]
    all_to_all x1, waiting for transfers between devices: 7.23 us -> 14 us  [body(): out_b = lax.all_to_all(out_rows(0), 'z', 0, 0)]
    ppermute x1, starting transfers between devices: 13.8 us -> 7.34 us  [body(): from_away = lax.ppermute(results[0], 'section', away)]
    concatenate x2 -> x1, other arithmetic: 4.25 us -> 0.02 us  [body(): jnp.concatenate([by_place(first, second, s) for s in range(2)], axis=0)]
  transfers between devices with their start and end apart: 31 -> 32, of which waited for: 22 -> 27; matrix products, arithmetic and copies ran while one was open for 14% -> 5% of each run, Pallas kernels for 11% -> 10%
where the time goes in v3:
time: 331 us
  waiting for transfers between devices  202 us (61%)
  starting transfers between devices  52.5 us (16%)
  Pallas kernels  43 us (13%)
  between operations  14.1 us (4%)
  other arithmetic  9.78 us (3%)
  local copies, waits for them, and re-layouts  9.64 us (3%)
    ppermute x24, waiting for transfers between devices, shifted(): lax.ppermute(block, axis, [(i, (i + distance) % n) for i in range(n)])  172 us
    pallas_call x2, Pallas kernels, hidden_of(): pl.pallas_call(functools.partial(hidden_kernel, len(rows)), grid=(width /...  25.8 us
    ppermute x24, starting transfers between devices, shifted(): lax.ppermute(block, axis, [(i, (i + distance) % n) for i in range(n)])  21.9 us
    pallas_call x2, Pallas kernels, out_of(): pl.pallas_call(functools.partial(out_kernel, n_experts, slices), grid=(st...  17.2 us
    all_to_all x1, waiting for transfers between devices, body(): out_b = lax.all_to_all(out_rows(0), 'z', 0, 0)  14 us
    all_to_all x1, waiting for transfers between devices, body(): out_a = lax.all_to_all(out_a, 'z', 0, 0)  12.4 us
    all_to_all x1, starting transfers between devices, body(): w_cut = lax.all_to_all(w_cut, 'z', 0, 0)  9.15 us
    ppermute x1, starting transfers between devices, body(): from_away = lax.ppermute(results[0], 'section', away)  7.34 us
  transfers between devices with their start and end apart: 32, of which 27 were waited for; matrix products, arithmetic and copies ran while one was open for 5% of the time, Pallas kernels for 10%

profile of v3, /device:TPU:1, one launch (start us, length us, event | category | flops | bytes accessed | tf_op | source)
XLA Modules:
  0.0 330.6 jit_solution(4145521300235021596)
XLA Ops:
  7.2 0.7 all-gather.4.cloned.1.call-update
  8.0 0.7 all-gather.6.cloned.1.call-update
  9.0 1.5 copy.21
  10.5 9.1 %all-to-all-start = ((bf16[8,128,896]{2,1,0:T(8,128)(2,1)}), bf16[8,128,896]{2,1,0:T(8,128)(2,1)}, u32[]{:S(2)}, u32[]{:S(2)}) async-start(bf16[8,128,896]{2,1,0:T(8,128)(2,1)} %bitcast.49), calls=%async_computation | async-start | bytes 3670016 | tf_op jit(solution)/shard_map/all_to_all | solution.py:207
  19.9 0.5 copy-done.24
  20.6 2.7 collective-permute-start
  23.5 2.7 collective-permute-start.2
  26.2 54.3 %collective-permute-done.refs_1_.refs_11_ = bf16[64,7296]{1,0:T(8,128)(2,1)} collective-permute-done((bf16[64,7296]{1,0:T(8,128)(2,1)S(1)}, bf16[64,7296]{1,0:T(8,128)(2,1)}, u32[]{:S(2)}, u32[]{:S(2)}) %collective-permute-start) | collective-permute-done | bytes 933920 | tf_op jit(solution)/shard_map/ppermute | solution.py:16
  80.6 1.6 collective-permute-done.1.refs_4_.refs_14_
  82.2 1.3 collective-permute-start.4
  83.7 16.9 %collective-permute-done.2.refs_6_.refs_16_ = bf16[64,7296]{1,0:T(8,128)(2,1)} collective-permute-done((bf16[64,7296]{1,0:T(8,128)(2,1)S(1)}, bf16[64,7296]{1,0:T(8,128)(2,1)}, u32[]{:S(2)}, u32[]{:S(2)}) %collective-permute-start.2) | collective-permute-done | bytes 933920 | tf_op jit(solution)/shard_map/ppermute | solution.py:16
  100.6 1.6 collective-permute-done.3.refs_9_.refs_19_
  102.2 18.4 %collective-permute-done.4.refs_2_.refs_12_ = bf16[64,7296]{1,0:T(8,128)(2,1)} collective-permute-done((bf16[64,7296]{1,0:T(8,128)(2,1)}, bf16[64,7296]{1,0:T(8,128)(2,1)}, u32[]{:S(2)}, u32[]{:S(2)}) %collective-permute-start.4) | collective-permute-done | bytes 933920 | tf_op jit(solution)/shard_map/ppermute | solution.py:16
  120.6 1.6 collective-permute-done.5.refs_3_.refs_13_
  122.2 3.5 %fusion = bf16[8,128,896]{2,1,0:T(8,128)(2,1)} fusion(s32[]{:T(128)S(6)} %select_n.120, bf16[8,128,896]{2,1,0:T(8,128)(2,1)} %all-to-all-done), kind=kLoop, calls=%fused_computation.2 | loop fusion | flops 917504 | bytes 3670020 | tf_op jit(solution)/shard_map/jit(_roll_dynamic)/concatenate | solution.py:214
  125.8 1.4 collective-permute-start.6
  127.4 2.5 collective-permute-start.8
  129.9 17.1 %collective-permute-done.6.refs_7_.refs_17_ = bf16[64,7296]{1,0:T(8,128)(2,1)} collective-permute-done((bf16[64,7296]{1,0:T(8,128)(2,1)}, bf16[64,7296]{1,0:T(8,128)(2,1)}, u32[]{:S(2)}, u32[]{:S(2)}) %collective-permute-start.6) | collective-permute-done | bytes 933920 | tf_op jit(solution)/shard_map/ppermute | solution.py:16
  147.0 2.2 collective-permute-done.7.refs_8_.refs_18_
  149.2 1.1 collective-permute-start.10
  150.6 16.3 %collective-permute-done.8.refs_0_.refs_8_ = bf16[64,7296]{1,0:T(8,128)(2,1)S(1)} collective-permute-done((bf16[64,7296]{1,0:T(8,128)(2,1)}, bf16[64,7296]{1,0:T(8,128)(2,1)S(1)}, u32[]{:S(2)}, u32[]{:S(2)}) %collective-permute-start.8) | collective-permute-done | bytes 933920 | tf_op jit(solution)/shard_map/ppermute | solution.py:16
  167.0 2.2 collective-permute-done.9.refs_3_.refs_11_
  169.2 0.8 slice.98
  170.0 1.1 collective-permute-start.12
  171.2 0.8 slice.99
  172.3 14.6 %shard_map.104 = (bf16[640,128]{1,0:T(8,128)(2,1)}, bf16[640,128]{1,0:T(8,128)(2,1)}) custom-call(bf16[64,7296]{1,0:T(8,128)(2,1)} %copy-done, bf16[64,7296]{1,0:T(8,128)(2,1)} %collective-permute-done.refs_1_.refs_11_, bf16[64,7296]{1,0:T(8,128)(2,1)} %collective-permute-done.4.refs_2_.refs_12_, bf16[64,7296]{1,0:T(8,128)(2,1)} %collective-permute-done.5.refs_3_.refs_13_, ...), custom_call_target="tpu_custom_call" | custom-call | flops 9395240960 | bytes 23855104 | tf_op jit(solution)/shard_map/pallas_call | solution.py:86
  187.0 2.2 collective-permute-done.11.refs_7_.refs_15_
  189.2 1.1 slice.100
  190.3 1.2 collective-permute-start.14
  191.5 1.1 slice.101
  192.6 0.5 collective-permute-start.15
  193.0 4.0 %collective-permute-done.12.refs_1_.refs_9_ = bf16[32,7296]{1,0:T(8,128)(2,1)S(1)} collective-permute-done((bf16[32,7296]{1,0:T(8,128)(2,1)}, bf16[32,7296]{1,0:T(8,128)(2,1)S(1)}, u32[]{:S(2)}, u32[]{:S(2)}) %collective-permute-start.12) | collective-permute-done | bytes 466976 | tf_op jit(solution)/shard_map/ppermute | solution.py:16
  197.0 2.2 collective-permute-done.13.refs_2_.refs_10_
  199.2 7.7 %collective-permute-done.14.refs_5_.refs_13_ = bf16[32,7296]{1,0:T(8,128)(2,1)S(1)} collective-permute-done((bf16[32,7296]{1,0:T(8,128)(2,1)S(1)}, bf16[32,7296]{1,0:T(8,128)(2,1)S(1)}, u32[]{:S(2)}, u32[]{:S(2)}) %collective-permute-start.14) | collective-permute-done | bytes 466976 | tf_op jit(solution)/shard_map/ppermute | solution.py:16
  207.0 2.2 collective-permute-done.15.refs_6_.refs_14_
  209.2 0.8 copy-done.9
  210.0 11.2 %shard_map.105 = (bf16[384,128]{1,0:T(8,128)(2,1)}, bf16[384,128]{1,0:T(8,128)(2,1)}) custom-call(bf16[64,7296]{1,0:T(8,128)(2,1)} %copy-done.4, bf16[32,7296]{1,0:T(8,128)(2,1)} %copy-done.7, bf16[32,7296]{1,0:T(8,128)(2,1)} %collective-permute-done.13.refs_2_.refs_10_, bf16[64,7296]{1,0:T(8,128)(2,1)} %copy-done.5, ...), custom_call_target="tpu_custom_call" | custom-call | flops 5637144576 | bytes 20185088 | tf_op jit(solution)/shard_map/pallas_call | solution.py:86
  221.2 0.9 fusion.32
  222.4 1.0 collective-permute-start.16
  223.5 0.5 collective-permute-start.17
  224.0 4.2 %collective-permute-done.16.refs_1_ = bf16[1024,128]{1,0:T(8,128)(2,1)S(1)} collective-permute-done((bf16[1024,128]{1,0:T(8,128)(2,1)S(1)}, bf16[1024,128]{1,0:T(8,128)(2,1)S(1)}, u32[]{:S(2)}, u32[]{:S(2)}) %collective-permute-start.16) | collective-permute-done | bytes 262176 | tf_op jit(solution)/shard_map/ppermute | solution.py:16
  228.1 2.2 collective-permute-done.17.refs_7_
  230.3 1.0 collective-permute-start.18
  231.8 4.2 %collective-permute-done.18.refs_2_ = bf16[1024,128]{1,0:T(8,128)(2,1)S(1)} collective-permute-done((bf16[1024,128]{1,0:T(8,128)(2,1)S(1)}, bf16[1024,128]{1,0:T(8,128)(2,1)S(1)}, u32[]{:S(2)}, u32[]{:S(2)}) %collective-permute-start.18) | collective-permute-done | bytes 262176 | tf_op jit(solution)/shard_map/ppermute | solution.py:16
  235.9 2.2 collective-permute-done.19.refs_6_
  238.4 1.3 collective-permute-start.21
  239.7 4.1 %collective-permute-done.20.refs_3_ = bf16[1024,128]{1,0:T(8,128)(2,1)S(1)} collective-permute-done((bf16[1024,128]{1,0:T(8,128)(2,1)S(1)}, bf16[1024,128]{1,0:T(8,128)(2,1)S(1)}, u32[]{:S(2)}, u32[]{:S(2)}) %collective-permute-start.20) | collective-permute-done | bytes 262176 | tf_op jit(solution)/shard_map/ppermute | solution.py:16
  243.8 1.4 collective-permute-done.21.refs_5_
  245.3 1.7 collective-permute-start.23
  247.1 1.0 fusion.3
  248.1 1.4 collective-permute-done.22.refs_4_
  249.5 1.1 collective-permute-done.23.refs_4_
  250.7 8.6 %shard_map.106 = bf16[512,896]{1,0:T(8,128)(2,1)} custom-call(bf16[512,128]{1,0:T(8,128)(2,1)} %bitcast.57, bf16[1024,128]{1,0:T(8,128)(2,1)} %copy-done.6, bf16[1024,128]{1,0:T(8,128)(2,1)} %copy-done.13, bf16[1024,128]{1,0:T(8,128)(2,1)} %copy-done.15, bf16[1024,128]{1,0:T(8,128)(2,1)} %copy-done.11, bf16[512,128]{1,0:T(8,128)(2,1)} %copy-done.22, ...), custom_call_target="tpu_custom_call" | custom-call | flops 3758096384 | bytes 8388608 | tf_op jit(solution)/shard_map/pallas_call | solution.py:140
  259.4 5.9 %all-to-all-start.1 = ((bf16[8,64,896]{2,1,0:T(8,128)(2,1)}), bf16[8,64,896]{2,1,0:T(8,128)(2,1)S(1)}, u32[]{:S(2)}, u32[]{:S(2)}) async-start(bf16[8,64,896]{2,1,0:T(8,128)(2,1)} %bitcast.54), calls=%async_computation.1 | async-start | bytes 1835008 | tf_op jit(solution)/shard_map/all_to_all | solution.py:245
  265.3 8.6 %shard_map.107 = bf16[512,896]{1,0:T(8,128)(2,1)} custom-call(bf16[512,128]{1,0:T(8,128)(2,1)} %bitcast.56, bf16[1024,128]{1,0:T(8,128)(2,1)} %copy-done.6, bf16[1024,128]{1,0:T(8,128)(2,1)} %copy-done.13, bf16[1024,128]{1,0:T(8,128)(2,1)} %copy-done.15, bf16[1024,128]{1,0:T(8,128)(2,1)} %copy-done.11, bf16[512,128]{1,0:T(8,128)(2,1)} %copy-done.21, ...), custom_call_target="tpu_custom_call" | custom-call | flops 3758096384 | bytes 8388608 | tf_op jit(solution)/shard_map/pallas_call | solution.py:140
  273.9 14.0 %all-to-all-done.1 = bf16[8,64,896]{2,1,0:T(8,128)(2,1)S(1)} async-done(((bf16[8,64,896]{2,1,0:T(8,128)(2,1)}), bf16[8,64,896]{2,1,0:T(8,128)(2,1)S(1)}, u32[]{:S(2)}, u32[]{:S(2)}) %all-to-all-start.1) | async-done | bytes 917536 | tf_op jit(solution)/shard_map/all_to_all | solution.py:245
  288.0 1.4 copy.17
  289.4 3.7 %all-to-all-start.2 = ((bf16[8,64,896]{2,1,0:T(8,128)(2,1)}), bf16[8,64,896]{2,1,0:T(8,128)(2,1)S(1)}, u32[]{:S(2)}, u32[]{:S(2)}) async-start(bf16[8,64,896]{2,1,0:T(8,128)(2,1)} %bitcast.24), calls=%async_computation.2 | async-start | bytes 1835008 | tf_op jit(solution)/shard_map/all_to_all | solution.py:247
  293.1 2.7 add_convert_fusion.1
  295.8 7.3 %collective-permute-start.24 = (bf16[64,7168]{1,0:T(8,128)(2,1)}, bf16[64,7168]{1,0:T(8,128)(2,1)S(1)}, u32[]{:S(2)}, u32[]{:S(2)}) collective-permute-start(bf16[64,7168]{1,0:T(8,128)(2,1)} %add_convert_fusion.1), channel_id=1, source_target_pairs={{0,0},{32,64},{64,32},{96,128},{128,96},{160,192},{192,160},{224,2... | collective-permute-start | bytes 2752520 | tf_op jit(solution)/shard_map/ppermute | solution.py:253
  303.1 12.4 %all-to-all-done.2 = bf16[8,64,896]{2,1,0:T(8,128)(2,1)S(1)} async-done(((bf16[8,64,896]{2,1,0:T(8,128)(2,1)}), bf16[8,64,896]{2,1,0:T(8,128)(2,1)S(1)}, u32[]{:S(2)}, u32[]{:S(2)}) %all-to-all-start.2) | async-done | bytes 917536 | tf_op jit(solution)/shard_map/all_to_all | solution.py:247
  316.2 4.4 %collective-permute-start.25 = (bf16[64,7168]{1,0:T(8,128)(2,1)S(1)}, bf16[64,7168]{1,0:T(8,128)(2,1)S(1)}, u32[]{:S(2)}, u32[]{:S(2)}) collective-permute-start(bf16[64,7168]{1,0:T(8,128)(2,1)S(1)} %add_convert_fusion), channel_id=1, source_target_pairs={{0,32},{32,0},{64,96},{96,64},{128,160},{160,128},{192,224},{224,1... | collective-permute-start | bytes 2752520 | tf_op jit(solution)/shard_map/ppermute | solution.py:254
  320.6 2.1 collective-permute-done.25
  322.7 1.3 select_bitcast_fusion
  (95 shorter events, 3.9 us)
Async XLA Ops:
  7.2 1.5 copy-start.10
  7.2 165.1 %all-gather.4.cloned.1.call-start = ((), (), s32[]{:S(2)}) async-start(), calls=%async_computation.3 | async-start | bytes 9175040 | tf_op jit(solution)/shard_map/all_gather | solution.py:201
  7.9 164.4 %all-gather.6.cloned.1.call-start = ((), (), s32[]{:S(2)}) async-start(), calls=%async_computation.4 | async-start | bytes 9175040 | tf_op jit(solution)/shard_map/all_gather | solution.py:202
  10.5 9.2 %copy-start.17 = (bf16[1,64,7168]{2,1,0:T(8,128)(2,1)S(1)}, bf16[1,64,7168]{2,1,0:T(8,128)(2,1)}, u32[]{:S(2)}) copy-start(bf16[1,64,7168]{2,1,0:T(8,128)(2,1)} %param.11) | copy-start | bytes 2752516
  10.5 9.2 %copy-start.18 = (bf16[1,64,7168]{2,1,0:T(8,128)(2,1)S(1)}, bf16[1,64,7168]{2,1,0:T(8,128)(2,1)}, u32[]{:S(2)}) copy-start(bf16[1,64,7168]{2,1,0:T(8,128)(2,1)} %param.12) | copy-start | bytes 2752516
  10.5 111.7 %all-to-all-start = ((bf16[8,128,896]{2,1,0:T(8,128)(2,1)}), bf16[8,128,896]{2,1,0:T(8,128)(2,1)}, u32[]{:S(2)}, u32[]{:S(2)}) async-start(bf16[8,128,896]{2,1,0:T(8,128)(2,1)} %bitcast.49), calls=%async_computation | async-start | bytes 3670016 | tf_op jit(solution)/shard_map/all_to_all | solution.py:207
  19.7 231.0 %all-gather.8.cloned.1.call-start = ((), (), s32[]{:S(2)}) async-start(), calls=%async_computation.5 | async-start | bytes 9175040 | tf_op jit(solution)/shard_map/all_gather | solution.py:215
  19.8 0.7 copy-start.24
  19.8 0.7 copy-start.25
  20.4 2.9 copy-start.2
  20.5 5.7 %copy-start.26 = (f32[1,64,1]{1,2,0:T(1,128)S(1)}, f32[1,64,1]{1,2,0:T(1,128)}, u32[]{:S(2)}) copy-start(f32[1,64,1]{1,2,0:T(1,128)} %param.15) | copy-start | bytes 772
  20.5 5.7 %copy-start.27 = (f32[1,64,1]{1,2,0:T(1,128)S(1)}, f32[1,64,1]{1,2,0:T(1,128)}, u32[]{:S(2)}) copy-start(f32[1,64,1]{1,2,0:T(1,128)} %param.16) | copy-start | bytes 772
  20.6 105.2 %copy-start = (bf16[64,7296]{1,0:T(8,128)(2,1)}, bf16[64,7296]{1,0:T(8,128)(2,1)S(1)}, u32[]{:S(2)}) copy-start(bf16[64,7296]{1,0:T(8,128)(2,1)S(1)} %pad_maximum_fusion.refs_0_.refs_10_) | copy-start | bytes 2801668
  20.6 60.0 %collective-permute-start = (bf16[64,7296]{1,0:T(8,128)(2,1)S(1)}, bf16[64,7296]{1,0:T(8,128)(2,1)}, u32[]{:S(2)}, u32[]{:S(2)}) collective-permute-start(bf16[64,7296]{1,0:T(8,128)(2,1)S(1)} %pad_maximum_fusion.refs_0_.refs_10_), channel_id=1, source_target_pairs={{0,7},{1,0},{2,1},{3,2},{4,3},{5,4},{6,5},{7,6},{8,15},{9,8},{10,9... | collective-permute-start | bytes 2801672 | tf_op jit(solution)/shard_map/ppermute | solution.py:16
  23.3 58.9 %collective-permute-start.1 = (bf16[64,7296]{1,0:T(8,128)(2,1)S(1)}, bf16[64,7296]{1,0:T(8,128)(2,1)}, u32[]{:S(2)}, u32[]{:S(2)}) collective-permute-start(bf16[64,7296]{1,0:T(8,128)(2,1)S(1)} %pad_maximum_fusion.refs_0_.refs_10_), channel_id=1, source_target_pairs={{0,1},{1,2},{2,3},{3,4},{4,5},{5,6},{6,7},{7,0},{8,9},{9,10},{10,1... | collective-permute-start | bytes 2801672 | tf_op jit(solution)/shard_map/ppermute | solution.py:16
  23.5 102.3 %copy-start.1 = (bf16[64,7296]{1,0:T(8,128)(2,1)}, bf16[64,7296]{1,0:T(8,128)(2,1)S(1)}, u32[]{:S(2)}) copy-start(bf16[64,7296]{1,0:T(8,128)(2,1)S(1)} %pad_maximum_fusion.1.refs_5_.refs_15_) | copy-start | bytes 2801668
  23.5 77.1 %collective-permute-start.2 = (bf16[64,7296]{1,0:T(8,128)(2,1)S(1)}, bf16[64,7296]{1,0:T(8,128)(2,1)}, u32[]{:S(2)}, u32[]{:S(2)}) collective-permute-start(bf16[64,7296]{1,0:T(8,128)(2,1)S(1)} %pad_maximum_fusion.1.refs_5_.refs_15_), channel_id=1, source_target_pairs={{0,7},{1,0},{2,1},{3,2},{4,3},{5,4},{6,5},{7,6},{8,15},{9,8},{10,9... | collective-permute-start | bytes 2801672 | tf_op jit(solution)/shard_map/ppermute | solution.py:16
  26.2 76.0 %collective-permute-start.3 = (bf16[64,7296]{1,0:T(8,128)(2,1)S(1)}, bf16[64,7296]{1,0:T(8,128)(2,1)}, u32[]{:S(2)}, u32[]{:S(2)}) collective-permute-start(bf16[64,7296]{1,0:T(8,128)(2,1)S(1)} %pad_maximum_fusion.1.refs_5_.refs_15_), channel_id=1, source_target_pairs={{0,1},{1,2},{2,3},{3,4},{4,5},{5,6},{6,7},{7,0},{8,9},{9,10},{10,1... | collective-permute-start | bytes 2801672 | tf_op jit(solution)/shard_map/ppermute | solution.py:16
  82.2 38.4 %collective-permute-start.4 = (bf16[64,7296]{1,0:T(8,128)(2,1)}, bf16[64,7296]{1,0:T(8,128)(2,1)}, u32[]{:S(2)}, u32[]{:S(2)}) collective-permute-start(bf16[64,7296]{1,0:T(8,128)(2,1)} %collective-permute-done.refs_1_.refs_11_), channel_id=1, source_target_pairs={{0,7},{1,0},{2,1},{3,2},{4,3},{5,4},{6,5},{7,6},{8,15},{9,8},{10,9... | collective-permute-start | bytes 2801672 | tf_op jit(solution)/shard_map/ppermute | solution.py:16
  83.5 38.7 %collective-permute-start.5 = (bf16[64,7296]{1,0:T(8,128)(2,1)}, bf16[64,7296]{1,0:T(8,128)(2,1)}, u32[]{:S(2)}, u32[]{:S(2)}) collective-permute-start(bf16[64,7296]{1,0:T(8,128)(2,1)} %collective-permute-done.1.refs_4_.refs_14_), channel_id=1, source_target_pairs={{0,1},{1,2},{2,3},{3,4},{4,5},{5,6},{6,7},{7,0},{8,9},{9,10},{10,1... | collective-permute-start | bytes 2801672 | tf_op jit(solution)/shard_map/ppermute | solution.py:16
  125.8 21.1 %collective-permute-start.6 = (bf16[64,7296]{1,0:T(8,128)(2,1)}, bf16[64,7296]{1,0:T(8,128)(2,1)}, u32[]{:S(2)}, u32[]{:S(2)}) collective-permute-start(bf16[64,7296]{1,0:T(8,128)(2,1)} %collective-permute-done.2.refs_6_.refs_16_), channel_id=1, source_target_pairs={{0,7},{1,0},{2,1},{3,2},{4,3},{5,4},{6,5},{7,6},{8,15},{9,8},{10,9... | collective-permute-start | bytes 2801672 | tf_op jit(solution)/shard_map/ppermute | solution.py:16
  127.2 22.0 %collective-permute-start.7 = (bf16[64,7296]{1,0:T(8,128)(2,1)}, bf16[64,7296]{1,0:T(8,128)(2,1)}, u32[]{:S(2)}, u32[]{:S(2)}) collective-permute-start(bf16[64,7296]{1,0:T(8,128)(2,1)} %collective-permute-done.3.refs_9_.refs_19_), channel_id=1, source_target_pairs={{0,1},{1,2},{2,3},{3,4},{4,5},{5,6},{6,7},{7,0},{8,9},{9,10},{10,1... | collective-permute-start | bytes 2801672 | tf_op jit(solution)/shard_map/ppermute | solution.py:16
  127.4 39.6 %collective-permute-start.8 = (bf16[64,7296]{1,0:T(8,128)(2,1)}, bf16[64,7296]{1,0:T(8,128)(2,1)S(1)}, u32[]{:S(2)}, u32[]{:S(2)}) collective-permute-start(bf16[64,7296]{1,0:T(8,128)(2,1)} %collective-permute-done.4.refs_2_.refs_12_), channel_id=1, source_target_pairs={{0,7},{1,0},{2,1},{3,2},{4,3},{5,4},{6,5},{7,6},{8,15},{9,8},{10,9... | collective-permute-start | bytes 2801672 | tf_op jit(solution)/shard_map/ppermute | solution.py:16
  129.9 39.3 %collective-permute-start.9 = (bf16[64,7296]{1,0:T(8,128)(2,1)}, bf16[64,7296]{1,0:T(8,128)(2,1)S(1)}, u32[]{:S(2)}, u32[]{:S(2)}) collective-permute-start(bf16[64,7296]{1,0:T(8,128)(2,1)} %collective-permute-done.5.refs_3_.refs_13_), channel_id=1, source_target_pairs={{0,1},{1,2},{2,3},{3,4},{4,5},{5,6},{6,7},{7,0},{8,9},{9,10},{10,1... | collective-permute-start | bytes 2801672 | tf_op jit(solution)/shard_map/ppermute | solution.py:16
  149.2 37.8 %collective-permute-start.10 = (bf16[64,7296]{1,0:T(8,128)(2,1)}, bf16[64,7296]{1,0:T(8,128)(2,1)}, u32[]{:S(2)}, u32[]{:S(2)}) collective-permute-start(bf16[64,7296]{1,0:T(8,128)(2,1)} %collective-permute-done.6.refs_7_.refs_17_), channel_id=1, source_target_pairs={{0,7},{1,0},{2,1},{3,2},{4,3},{5,4},{6,5},{7,6},{8,15},{9,8},{10,9... | collective-permute-start | bytes 2801672 | tf_op jit(solution)/shard_map/ppermute | solution.py:16
  150.3 38.9 %collective-permute-start.11 = (bf16[64,7296]{1,0:T(8,128)(2,1)}, bf16[64,7296]{1,0:T(8,128)(2,1)}, u32[]{:S(2)}, u32[]{:S(2)}) collective-permute-start(bf16[64,7296]{1,0:T(8,128)(2,1)} %collective-permute-done.7.refs_8_.refs_18_), channel_id=1, source_target_pairs={{0,1},{1,2},{2,3},{3,4},{4,5},{5,6},{6,7},{7,0},{8,9},{9,10},{10,1... | collective-permute-start | bytes 2801672 | tf_op jit(solution)/shard_map/ppermute | solution.py:16
  167.0 19.9 %copy-start.4 = (bf16[64,7296]{1,0:T(8,128)(2,1)}, bf16[64,7296]{1,0:T(8,128)(2,1)S(1)}, u32[]{:S(2)}) copy-start(bf16[64,7296]{1,0:T(8,128)(2,1)S(1)} %collective-permute-done.8.refs_0_.refs_8_) | copy-start | bytes 2801668
  169.2 17.7 %copy-start.5 = (bf16[64,7296]{1,0:T(8,128)(2,1)}, bf16[64,7296]{1,0:T(8,128)(2,1)S(1)}, u32[]{:S(2)}) copy-start(bf16[64,7296]{1,0:T(8,128)(2,1)S(1)} %collective-permute-done.9.refs_3_.refs_11_) | copy-start | bytes 2801668
  170.0 27.0 %collective-permute-start.12 = (bf16[32,7296]{1,0:T(8,128)(2,1)}, bf16[32,7296]{1,0:T(8,128)(2,1)S(1)}, u32[]{:S(2)}, u32[]{:S(2)}) collective-permute-start(bf16[32,7296]{1,0:T(8,128)(2,1)} %slice.98), channel_id=1, source_target_pairs={{0,7},{1,0},{2,1},{3,2},{4,3},{5,4},{6,5},{7,6},{8,15},{9,8},{10,9... | collective-permute-start | bytes 1400840 | tf_op jit(solution)/shard_map/ppermute | solution.py:16
  172.0 27.3 %collective-permute-start.13 = (bf16[32,7296]{1,0:T(8,128)(2,1)}, bf16[32,7296]{1,0:T(8,128)(2,1)}, u32[]{:S(2)}, u32[]{:S(2)}) collective-permute-start(bf16[32,7296]{1,0:T(8,128)(2,1)} %slice.99), channel_id=1, source_target_pairs={{0,1},{1,2},{2,3},{3,4},{4,5},{5,6},{6,7},{7,0},{8,9},{9,10},{10,1... | collective-permute-start | bytes 1400840 | tf_op jit(solution)/shard_map/ppermute | solution.py:16
  186.9 12.3 %copy-start.20 = (bf16[640,128]{1,0:T(8,128)(2,1)S(1)}, bf16[640,128]{1,0:T(8,128)(2,1)}, u32[]{:S(2)}) copy-start(bf16[640,128]{1,0:T(8,128)(2,1)} %get-tuple-element.71) | copy-start | bytes 491524
  190.3 16.7 %collective-permute-start.14 = (bf16[32,7296]{1,0:T(8,128)(2,1)S(1)}, bf16[32,7296]{1,0:T(8,128)(2,1)S(1)}, u32[]{:S(2)}, u32[]{:S(2)}) collective-permute-start(bf16[32,7296]{1,0:T(8,128)(2,1)S(1)} %slice.100), channel_id=1, source_target_pairs={{0,7},{1,0},{2,1},{3,2},{4,3},{5,4},{6,5},{7,6},{8,15},{9,8},{10,9... | collective-permute-start | bytes 1400840 | tf_op jit(solution)/shard_map/ppermute | solution.py:16
  192.6 16.7 %collective-permute-start.15 = (bf16[32,7296]{1,0:T(8,128)(2,1)S(1)}, bf16[32,7296]{1,0:T(8,128)(2,1)S(1)}, u32[]{:S(2)}, u32[]{:S(2)}) collective-permute-start(bf16[32,7296]{1,0:T(8,128)(2,1)S(1)} %slice.101), channel_id=1, source_target_pairs={{0,1},{1,2},{2,3},{3,4},{4,5},{5,6},{6,7},{7,0},{8,9},{9,10},{10,1... | collective-permute-start | bytes 1400840 | tf_op jit(solution)/shard_map/ppermute | solution.py:16
  197.0 12.2 %copy-start.7 = (bf16[32,7296]{1,0:T(8,128)(2,1)}, bf16[32,7296]{1,0:T(8,128)(2,1)S(1)}, u32[]{:S(2)}) copy-start(bf16[32,7296]{1,0:T(8,128)(2,1)S(1)} %collective-permute-done.12.refs_1_.refs_9_) | copy-start | bytes 1400836
  199.2 40.4 %copy-start.19 = (bf16[640,128]{1,0:T(8,128)(2,1)S(1)}, bf16[640,128]{1,0:T(8,128)(2,1)}, u32[]{:S(2)}) copy-start(bf16[640,128]{1,0:T(8,128)(2,1)} %get-tuple-element.89) | copy-start | bytes 491524
  207.0 2.2 copy-start.8
  209.2 0.8 copy-start.9
  221.2 25.9 %copy-start.23 = (bf16[384,128]{1,0:T(8,128)(2,1)S(1)}, bf16[384,128]{1,0:T(8,128)(2,1)}, u32[]{:S(2)}) copy-start(bf16[384,128]{1,0:T(8,128)(2,1)} %get-tuple-element.90) | copy-start | bytes 294916
  222.4 28.2 %copy-start.6 = (bf16[1024,128]{1,0:T(8,128)(2,1)}, bf16[1024,128]{1,0:T(8,128)(2,1)S(1)}, u32[]{:S(2)}) copy-start(bf16[1024,128]{1,0:T(8,128)(2,1)S(1)} %pad_maximum_fusion.2.refs_0_) | copy-start | bytes 786436
  222.4 5.7 %collective-permute-start.16 = (bf16[1024,128]{1,0:T(8,128)(2,1)S(1)}, bf16[1024,128]{1,0:T(8,128)(2,1)S(1)}, u32[]{:S(2)}, u32[]{:S(2)}) collective-permute-start(bf16[1024,128]{1,0:T(8,128)(2,1)S(1)} %pad_maximum_fusion.2.refs_0_), channel_id=1, source_target_pairs={{0,7},{1,0},{2,1},{3,2},{4,3},{5,4},{6,5},{7,6},{8,15},{9,8},{10,9... | collective-permute-start | bytes 786440 | tf_op jit(solution)/shard_map/ppermute | solution.py:16
  223.5 6.8 %collective-permute-start.17 = (bf16[1024,128]{1,0:T(8,128)(2,1)S(1)}, bf16[1024,128]{1,0:T(8,128)(2,1)S(1)}, u32[]{:S(2)}, u32[]{:S(2)}) collective-permute-start(bf16[1024,128]{1,0:T(8,128)(2,1)S(1)} %pad_maximum_fusion.2.refs_0_), channel_id=1, source_target_pairs={{0,1},{1,2},{2,3},{3,4},{4,5},{5,6},{6,7},{7,0},{8,9},{9,10},{10,1... | collective-permute-start | bytes 786440 | tf_op jit(solution)/shard_map/ppermute | solution.py:16
  228.1 22.5 %copy-start.13 = (bf16[1024,128]{1,0:T(8,128)(2,1)}, bf16[1024,128]{1,0:T(8,128)(2,1)S(1)}, u32[]{:S(2)}) copy-start(bf16[1024,128]{1,0:T(8,128)(2,1)S(1)} %collective-permute-done.16.refs_1_) | copy-start | bytes 786436
  230.3 20.4 %copy-start.14 = (bf16[1024,128]{1,0:T(8,128)(2,1)}, bf16[1024,128]{1,0:T(8,128)(2,1)S(1)}, u32[]{:S(2)}) copy-start(bf16[1024,128]{1,0:T(8,128)(2,1)S(1)} %collective-permute-done.17.refs_7_) | copy-start | bytes 786436
  230.3 5.6 %collective-permute-start.18 = (bf16[1024,128]{1,0:T(8,128)(2,1)S(1)}, bf16[1024,128]{1,0:T(8,128)(2,1)S(1)}, u32[]{:S(2)}, u32[]{:S(2)}) collective-permute-start(bf16[1024,128]{1,0:T(8,128)(2,1)S(1)} %collective-permute-done.16.refs_1_), channel_id=1, source_target_pairs={{0,7},{1,0},{2,1},{3,2},{4,3},{5,4},{6,5},{7,6},{8,15},{9,8},{10,9... | collective-permute-start | bytes 786440 | tf_op jit(solution)/shard_map/ppermute | solution.py:16
  231.3 6.8 %collective-permute-start.19 = (bf16[1024,128]{1,0:T(8,128)(2,1)S(1)}, bf16[1024,128]{1,0:T(8,128)(2,1)S(1)}, u32[]{:S(2)}, u32[]{:S(2)}) collective-permute-start(bf16[1024,128]{1,0:T(8,128)(2,1)S(1)} %collective-permute-done.17.refs_7_), channel_id=1, source_target_pairs={{0,1},{1,2},{2,3},{3,4},{4,5},{5,6},{6,7},{7,0},{8,9},{9,10},{10,1... | collective-permute-start | bytes 786440 | tf_op jit(solution)/shard_map/ppermute | solution.py:16
  235.9 14.8 %copy-start.15 = (bf16[1024,128]{1,0:T(8,128)(2,1)}, bf16[1024,128]{1,0:T(8,128)(2,1)S(1)}, u32[]{:S(2)}) copy-start(bf16[1024,128]{1,0:T(8,128)(2,1)S(1)} %collective-permute-done.18.refs_2_) | copy-start | bytes 786436
  238.2 12.5 %copy-start.16 = (bf16[1024,128]{1,0:T(8,128)(2,1)}, bf16[1024,128]{1,0:T(8,128)(2,1)S(1)}, u32[]{:S(2)}) copy-start(bf16[1024,128]{1,0:T(8,128)(2,1)S(1)} %collective-permute-done.19.refs_6_) | copy-start | bytes 786436
  238.2 5.6 %collective-permute-start.20 = (bf16[1024,128]{1,0:T(8,128)(2,1)S(1)}, bf16[1024,128]{1,0:T(8,128)(2,1)S(1)}, u32[]{:S(2)}, u32[]{:S(2)}) collective-permute-start(bf16[1024,128]{1,0:T(8,128)(2,1)S(1)} %collective-permute-done.18.refs_2_), channel_id=1, source_target_pairs={{0,7},{1,0},{2,1},{3,2},{4,3},{5,4},{6,5},{7,6},{8,15},{9,8},{10,9... | collective-permute-start | bytes 786440 | tf_op jit(solution)/shard_map/ppermute | solution.py:16
  238.4 6.8 %collective-permute-start.21 = (bf16[1024,128]{1,0:T(8,128)(2,1)S(1)}, bf16[1024,128]{1,0:T(8,128)(2,1)S(1)}, u32[]{:S(2)}, u32[]{:S(2)}) collective-permute-start(bf16[1024,128]{1,0:T(8,128)(2,1)S(1)} %collective-permute-done.19.refs_6_), channel_id=1, source_target_pairs={{0,1},{1,2},{2,3},{3,4},{4,5},{5,6},{6,7},{7,0},{8,9},{9,10},{10,1... | collective-permute-start | bytes 786440 | tf_op jit(solution)/shard_map/ppermute | solution.py:16
  243.8 6.9 %copy-start.11 = (bf16[1024,128]{1,0:T(8,128)(2,1)}, bf16[1024,128]{1,0:T(8,128)(2,1)S(1)}, u32[]{:S(2)}) copy-start(bf16[1024,128]{1,0:T(8,128)(2,1)S(1)} %collective-permute-done.20.refs_3_) | copy-start | bytes 786436
  245.2 5.5 %copy-start.12 = (bf16[1024,128]{1,0:T(8,128)(2,1)}, bf16[1024,128]{1,0:T(8,128)(2,1)S(1)}, u32[]{:S(2)}) copy-start(bf16[1024,128]{1,0:T(8,128)(2,1)S(1)} %collective-permute-done.21.refs_5_) | copy-start | bytes 786436
  245.2 4.3 %collective-permute-start.22 = (bf16[512,128]{1,0:T(8,128)(2,1)S(1)}, bf16[512,128]{1,0:T(8,128)(2,1)S(1)}, u32[]{:S(2)}, u32[]{:S(2)}) collective-permute-start(bf16[512,128]{1,0:T(8,128)(2,1)S(1)} %slice.112), channel_id=1, source_target_pairs={{0,7},{1,0},{2,1},{3,2},{4,3},{5,4},{6,5},{7,6},{8,15},{9,8},{10,9... | collective-permute-start | bytes 393224 | tf_op jit(solution)/shard_map/ppermute | solution.py:16
  245.3 5.3 %collective-permute-start.23 = (bf16[512,128]{1,0:T(8,128)(2,1)S(1)}, bf16[512,128]{1,0:T(8,128)(2,1)S(1)}, u32[]{:S(2)}, u32[]{:S(2)}) collective-permute-start(bf16[512,128]{1,0:T(8,128)(2,1)S(1)} %slice.113), channel_id=1, source_target_pairs={{0,1},{1,2},{2,3},{3,4},{4,5},{5,6},{6,7},{7,0},{8,9},{9,10},{10,1... | collective-permute-start | bytes 393224 | tf_op jit(solution)/shard_map/ppermute | solution.py:16
  249.5 1.2 copy-start.22
  250.7 8.7 %copy-start.21 = (bf16[512,128]{1,0:T(8,128)(2,1)}, bf16[512,128]{1,0:T(8,128)(2,1)S(1)}, u32[]{:S(2)}) copy-start(bf16[512,128]{1,0:T(8,128)(2,1)S(1)} %collective-permute-done.23.refs_4_) | copy-start | bytes 393220
  259.4 28.5 %all-to-all-start.1 = ((bf16[8,64,896]{2,1,0:T(8,128)(2,1)}), bf16[8,64,896]{2,1,0:T(8,128)(2,1)S(1)}, u32[]{:S(2)}, u32[]{:S(2)}) async-start(bf16[8,64,896]{2,1,0:T(8,128)(2,1)} %bitcast.54), calls=%async_computation.1 | async-start | bytes 1835008 | tf_op jit(solution)/shard_map/all_to_all | solution.py:245
  289.4 3.7 %copy-start.3 = (bf16[64,7168]{1,0:T(8,128)(2,1)S(1)}, bf16[64,7168]{1,0:T(8,128)(2,1)}, u32[]{:S(2)}) copy-start(bf16[64,7168]{1,0:T(8,128)(2,1)} %copy-done.2) | copy-start | bytes 2752516
  289.4 26.2 %all-to-all-start.2 = ((bf16[8,64,896]{2,1,0:T(8,128)(2,1)}), bf16[8,64,896]{2,1,0:T(8,128)(2,1)S(1)}, u32[]{:S(2)}, u32[]{:S(2)}) async-start(bf16[8,64,896]{2,1,0:T(8,128)(2,1)} %bitcast.24), calls=%async_computation.2 | async-start | bytes 1835008 | tf_op jit(solution)/shard_map/all_to_all | solution.py:247
  295.8 24.8 %collective-permute-start.24 = (bf16[64,7168]{1,0:T(8,128)(2,1)}, bf16[64,7168]{1,0:T(8,128)(2,1)S(1)}, u32[]{:S(2)}, u32[]{:S(2)}) collective-permute-start(bf16[64,7168]{1,0:T(8,128)(2,1)} %add_convert_fusion.1), channel_id=1, source_target_pairs={{0,0},{32,64},{64,32},{96,128},{128,96},{160,192},{192,160},{224,2... | collective-permute-start | bytes 2752520 | tf_op jit(solution)/shard_map/ppermute | solution.py:253
  316.2 6.5 %collective-permute-start.25 = (bf16[64,7168]{1,0:T(8,128)(2,1)S(1)}, bf16[64,7168]{1,0:T(8,128)(2,1)S(1)}, u32[]{:S(2)}, u32[]{:S(2)}) collective-permute-start(bf16[64,7168]{1,0:T(8,128)(2,1)S(1)} %add_convert_fusion), channel_id=1, source_target_pairs={{0,32},{32,0},{64,96},{96,64},{128,160},{160,128},{192,224},{224,1... | collective-permute-start | bytes 2752520 | tf_op jit(solution)/shard_map/ppermute | solution.py:254
Sparse Core Ops, SparseCore 0:
  9.8 80.6 all-gather.3
  92.4 77.7 all-gather.5
  172.0 77.7 all-gather.7

commit v4 on v3

--- a/solution.py
+++ b/solution.py
@@ -54,7 +54,7 @@
     rows, tails = refs[:n_rows], refs[n_rows : 2 * n_rows]
     weights = refs[2 * n_rows : -3]
     hidden, route, total = refs[-3:]
-    n_experts, n_hid = len(weights) // 2, hidden.shape[1]
+    n_experts, n_hid = len(weights), hidden.shape[1]
     step = pl.program_id(0)
 
     @pl.when(step == 0)
@@ -65,8 +65,7 @@
     x = jnp.concatenate([r[...] for r in rows], axis=0)
     for e in range(n_experts):
         at = slice(2 * n_hid * e, 2 * n_hid * (e + 1))
-        pair = jnp.concatenate([weights[2 * e][0], weights[2 * e + 1][0]], axis=1)
-        total[:, at] += jnp.dot(x, pair, preferred_element_type=jnp.float32)
+        total[:, at] += jnp.dot(x, weights[e][0], preferred_element_type=jnp.float32)
 
     @pl.when(step == pl.num_programs(0) - 1)
     def _():
@@ -79,8 +78,9 @@
         hidden[...] = (gate / (1.0 + jnp.exp(-gate)) * up).astype(hidden.dtype)
 
 
-def hidden_of(rows, gates, ups, block):
-    n_experts, width, n_hid = gates.shape
+def hidden_of(rows, weights, block):
+    n_experts, width, pair = weights.shape
+    n_hid = pair // 2
     count = sum(r.shape[0] for r in rows)
     made = jax.ShapeDtypeStruct((count, n_hid), jnp.bfloat16)
     return pl.pallas_call(
@@ -88,7 +88,7 @@
         grid=(width // block,),
         in_specs=[pl.BlockSpec((r.shape[0], block), lambda k: (0, k)) for r in rows]
         + [pl.BlockSpec((r.shape[0], n_hid), lambda k: (0, width // n_hid)) for r in rows]
-        + [pl.BlockSpec((1, block, n_hid), lambda k, e=e: (e, k, 0)) for e in range(n_experts) for _ in range(2)],
+        + [pl.BlockSpec((1, block, pair), lambda k, e=e: (e, k, 0)) for e in range(n_experts)],
         out_specs=[pl.BlockSpec((count, n_hid), lambda k: (0, 0))] * 2,
         out_shape=[made, made],
         scratch_shapes=[pltpu.VMEM((count, 2 * n_hid * n_experts), jnp.float32)],
@@ -100,10 +100,10 @@
             bytes_accessed=2 * width * (count + 2 * n_hid * n_experts),
             transcendentals=count * n_hid,
         ),
-    )(*rows, *rows, *[gates, ups] * n_experts)
-
-
-def out_kernel(n_experts, slices, route, *refs):
+    )(*rows, *rows, *[weights] * n_experts)
+
+
+def out_kernel(slices, place, route, *refs):
     hidden, weights = refs[:slices], refs[slices:-2]
     out, total = refs[-2:]
     step = pl.program_id(0)
@@ -118,11 +118,12 @@
         @pl.when(step == now)
         def _():
             sums = total[...]
-            for at, half in enumerate((hidden[now], hidden[now + slices // 2])):
+            for half, weight in zip((hidden[now], hidden[now + slices // 2]), weights):
+                n_experts, _, part = weight.shape
                 terms = [jnp.where(named == e, half[...], jnp.zeros_like(half)) for e in range(n_experts)]
                 sums += jnp.dot(
                     jnp.concatenate(terms, axis=1),
-                    jnp.concatenate([weights[2 * e + at][0] for e in range(n_experts)], axis=0),
+                    weight[...].reshape(-1, part),
                     preferred_element_type=jnp.float32,
                 )
             total[...] = sums
@@ -132,24 +133,28 @@
         out[...] = total[...].astype(out.dtype)
 
 
-def out_of(route, hidden, weights):
+def out_of(place, route, hidden, weights):
     slices = len(hidden)
     n_experts, _, part = weights.shape
     count, n_hid = route.shape
     steps = slices // 2
     return pl.pallas_call(
-        functools.partial(out_kernel, n_experts, slices),
-        grid=(steps,),
-        in_specs=[pl.BlockSpec((count, n_hid), lambda k: (0, 0))]
-        + [pl.BlockSpec((count, n_hid), lambda k, at=at: (at, 0)) for _, at in hidden]
-        + [
-            pl.BlockSpec((1, n_hid, part), lambda k, e=e, at=at: (e, k + at, 0))
-            for e in range(n_experts)
-            for at in (0, steps)
-        ],
-        out_specs=pl.BlockSpec((count, part), lambda k: (0, 0)),
+        functools.partial(out_kernel, slices),
+        grid_spec=pltpu.PrefetchScalarGridSpec(
+            num_scalar_prefetch=1,
+            grid=(steps,),
+            in_specs=[pl.BlockSpec((count, n_hid), lambda k, z: (0, 0))]
+            + [pl.BlockSpec((count, n_hid), lambda k, z, at=at: (at, 0)) for _, at in hidden]
+            + [
+                pl.BlockSpec(
+                    (n_experts, n_hid, part), lambda k, z, at=at: (0, lax.rem(k + at + z[0], slices), 0)
+                )
+                for at in (0, steps)
+            ],
+            out_specs=pl.BlockSpec((count, part), lambda k, z: (0, 0)),
+            scratch_shapes=[pltpu.VMEM((count, part), jnp.float32)],
+        ),
         out_shape=jax.ShapeDtypeStruct((count, part), jnp.bfloat16),
-        scratch_shapes=[pltpu.VMEM((count, part), jnp.float32)],
         compiler_params=pltpu.CompilerParams(
             dimension_semantics=("arbitrary",), vmem_limit_bytes=VMEM_BYTES
         ),
@@ -158,7 +163,7 @@
             bytes_accessed=2 * slices * n_hid * (count + n_experts * part),
             transcendentals=0,
         ),
-    )(route, *[h for h, _ in hidden], *[weights] * (2 * n_experts))
+    )(place, route, *[h for h, _ in hidden], weights, weights)
 
 
 def body(
@@ -198,8 +203,7 @@
         return y.astype(jnp.bfloat16)
 
     order = Order(gates[0])
-    gate_all = lax.all_gather(w_gate[0], "x")
-    up_all = lax.all_gather(w_up[0], "x")
+    gate_up = lax.all_gather(jnp.concatenate([w_gate[0], w_up[0]], axis=1), "x")
     b, a = Ring(marked(0), "z"), Ring(marked(1), "z")
     b.send()
     a.send()
@@ -211,20 +215,19 @@
     a.send()
     (w_cut,) = b.wait(order, w_cut)
     b.send()
-    w_cut = jnp.roll(w_cut, -me_z, axis=0).reshape(n_z * hid, part)
-    down = lax.all_gather(w_cut, "x")
+    down = lax.all_gather(w_cut.reshape(n_z * hid, part), "x")
     a.wait(order)
     first = b.near() + a.near()
     a.send()
     b.wait(order)
     b.send()
-    first, first_route = hidden_of(first, gate_all, up_all, 1792)
+    first, first_route = hidden_of(first, gate_up, 1792)
     (first,) = a.wait(order, first)
     a.send()
     b.wait(order)
     a.wait(order)
     second = [p for ring in (b, a) for p in (ring.up[-1], *ring.last, ring.down[0])]
-    second, second_route = hidden_of(second, gate_all, up_all, 1792)
+    second, second_route = hidden_of(second, gate_up, 1792)
     both = jnp.concatenate([by_place(first, second, s) for s in range(2)], axis=0)
     named = [by_place(first_route, second_route, s) for s in range(2)]
     h = Ring(both, "z")
@@ -240,7 +243,7 @@
 
     def out_rows(s):
         hidden = [(piece, s) for piece in h.up] + [(h.last[s], 0)] + [(piece, s) for piece in h.down]
-        return out_of(named[s], hidden, down).reshape(n_z, rows, part)
+        return out_of(me_z.astype(jnp.int32).reshape(1), named[s], hidden, down).reshape(n_z, rows, part)
 
     out_b = lax.all_to_all(out_rows(0), "z", 0, 0)
     out_b, out_a = order(out_b, out_rows(1))

time: 331 us -> 328 us (level)
  waiting for transfers between devices: 202 us -> 190 us
  starting transfers between devices: 52.5 us -> 57.5 us
    all_to_all x1, waiting for transfers between devices: 12.4 us -> 6.38 us  [body(): out_a = lax.all_to_all(out_a, 'z', 0, 0)]
  transfers between devices with their start and end apart: 32 -> 31, of which waited for: 27 -> 26; matrix products, arithmetic and copies ran while one was open for 5% -> 4% of each run, Pallas kernels for 10% -> 11%
where the time goes in v4:
time: 328 us; the launch traced here: 327 us
  waiting for transfers between devices  190 us (58%)
  starting transfers between devices  57.5 us (18%)
  Pallas kernels  42.7 us (13%)
  between operations  14.4 us (4%)
  local copies, waits for them, and re-layouts  12 us (4%)
  other arithmetic  10.5 us (3%)
    ppermute x24, waiting for transfers between devices, shifted(): lax.ppermute(block, axis, [(i, (i + distance) % n) for i in range(n)])  170 us
    pallas_call x2, Pallas kernels, hidden_of(): pl.pallas_call(functools.partial(hidden_kernel, len(rows)), grid=(width /...  26.3 us
    ppermute x24, starting transfers between devices, shifted(): lax.ppermute(block, axis, [(i, (i + distance) % n) for i in range(n)])  21.8 us
    pallas_call x2, Pallas kernels, out_of(): pl.pallas_call(functools.partial(out_kernel, slices), grid_spec=pltpu.Pre...  16.4 us
    all_to_all x1, waiting for transfers between devices, body(): out_b = lax.all_to_all(out_rows(0), 'z', 0, 0)  11.5 us
    ppermute x1, starting transfers between devices, body(): from_away = lax.ppermute(results[0], 'section', away)  10.3 us
    all_to_all x1, starting transfers between devices, body(): w_cut = lax.all_to_all(w_cut, 'z', 0, 0)  9.15 us
    ppermute x1, starting transfers between devices, body(): from_near = lax.ppermute(results[1], 'section', near)  7.48 us
  transfers between devices with their start and end apart: 31, of which 26 were waited for; matrix products, arithmetic and copies ran while one was open for 4% of the time, Pallas kernels for 11%

profile of v4, /device:TPU:1, one launch (start us, length us, event | category | flops | bytes accessed | tf_op | source)
XLA Modules:
  0.0 327.3 jit_solution(16982875713088798694)
XLA Ops:
  7.2 4.3 %pad_maximum_fusion = bf16[7168,256]{1,0:T(8,128)(2,1)} fusion(bf16[7168,128]{1,0:T(8,128)(2,1)} %bitcast.66, bf16[7168,128]{1,0:T(8,128)(2,1)} %bitcast.67), kind=kLoop, calls=%fused_computation | loop fusion | flops 7340032 | bytes 7340032 | tf_op jit(solution)/shard_map/concatenate | solution.py:206
  11.6 1.5 copy-done.15
  13.4 1.5 copy.21
  14.9 9.1 %all-to-all-start = ((bf16[8,128,896]{2,1,0:T(8,128)(2,1)}), bf16[8,128,896]{2,1,0:T(8,128)(2,1)}, u32[]{:S(2)}, u32[]{:S(2)}) async-start(bf16[8,128,896]{2,1,0:T(8,128)(2,1)} %bitcast.53), calls=%async_computation | async-start | bytes 3670016 | tf_op jit(solution)/shard_map/all_to_all | solution.py:211
  24.2 0.5 copy-done.29
  24.9 2.7 collective-permute-start
  27.8 2.7 collective-permute-start.2
  30.6 54.3 %collective-permute-done.refs_1_.refs_11_ = bf16[64,7296]{1,0:T(8,128)(2,1)S(1)} collective-permute-done((bf16[64,7296]{1,0:T(8,128)(2,1)S(1)}, bf16[64,7296]{1,0:T(8,128)(2,1)S(1)}, u32[]{:S(2)}, u32[]{:S(2)}) %collective-permute-start) | collective-permute-done | bytes 933920 | tf_op jit(solution)/shard_map/ppermute | solution.py:16
  84.9 1.6 collective-permute-done.1.refs_4_.refs_14_
  86.5 1.3 collective-permute-start.4
  88.0 16.9 %collective-permute-done.2.refs_6_.refs_16_ = bf16[64,7296]{1,0:T(8,128)(2,1)S(1)} collective-permute-done((bf16[64,7296]{1,0:T(8,128)(2,1)S(1)}, bf16[64,7296]{1,0:T(8,128)(2,1)S(1)}, u32[]{:S(2)}, u32[]{:S(2)}) %collective-permute-start.2) | collective-permute-done | bytes 933920 | tf_op jit(solution)/shard_map/ppermute | solution.py:16
  104.9 1.6 collective-permute-done.3.refs_9_.refs_19_
  106.5 18.4 %collective-permute-done.4.refs_2_.refs_12_ = bf16[64,7296]{1,0:T(8,128)(2,1)S(1)} collective-permute-done((bf16[64,7296]{1,0:T(8,128)(2,1)S(1)}, bf16[64,7296]{1,0:T(8,128)(2,1)S(1)}, u32[]{:S(2)}, u32[]{:S(2)}) %collective-permute-start.4) | collective-permute-done | bytes 933920 | tf_op jit(solution)/shard_map/ppermute | solution.py:16
  124.9 0.9 copy-done.10
  125.9 0.7 collective-permute-done.5.refs_3_.refs_13_
  126.6 1.4 collective-permute-start.6
  128.1 2.5 collective-permute-start.8
  130.7 17.1 %collective-permute-done.6.refs_7_.refs_17_ = bf16[64,7296]{1,0:T(8,128)(2,1)} collective-permute-done((bf16[64,7296]{1,0:T(8,128)(2,1)}, bf16[64,7296]{1,0:T(8,128)(2,1)}, u32[]{:S(2)}, u32[]{:S(2)}) %collective-permute-start.6) | collective-permute-done | bytes 933920 | tf_op jit(solution)/shard_map/ppermute | solution.py:16
  147.7 2.2 collective-permute-done.7.refs_8_.refs_18_
  150.0 1.2 collective-permute-start.10
  151.4 16.2 %collective-permute-done.8.refs_0_.refs_8_ = bf16[64,7296]{1,0:T(8,128)(2,1)S(1)} collective-permute-done((bf16[64,7296]{1,0:T(8,128)(2,1)}, bf16[64,7296]{1,0:T(8,128)(2,1)S(1)}, u32[]{:S(2)}, u32[]{:S(2)}) %collective-permute-start.8) | collective-permute-done | bytes 933920 | tf_op jit(solution)/shard_map/ppermute | solution.py:16
  167.6 2.2 collective-permute-done.9.refs_3_.refs_11_
  169.9 0.9 slice.98
  170.7 1.2 collective-permute-start.12
  171.9 0.8 slice.99
  173.0 15.1 %shard_map.104 = (bf16[640,128]{1,0:T(8,128)(2,1)}, bf16[640,128]{1,0:T(8,128)(2,1)}) custom-call(bf16[64,7296]{1,0:T(8,128)(2,1)} %copy-done, bf16[64,7296]{1,0:T(8,128)(2,1)} %copy-done.6, bf16[64,7296]{1,0:T(8,128)(2,1)} %copy-done.10, bf16[64,7296]{1,0:T(8,128)(2,1)} %collective-permute-done.5.refs_3_.refs_13_, bf16[64,7296]{1,0:T(8,128)(2,1)} %copy-done.7, ...), custom_call_target="tpu_custom_call" | custom-call | flops 9395240960 | bytes 23855104 | tf_op jit(solution)/shard_map/pallas_call | solution.py:86
  188.1 1.9 collective-permute-done.11.refs_7_.refs_15_
  190.0 1.1 slice.100
  191.1 1.2 collective-permute-start.14
  192.3 1.1 slice.101
  193.3 0.4 collective-permute-start.15
  193.7 4.0 %collective-permute-done.12.refs_1_.refs_9_ = bf16[32,7296]{1,0:T(8,128)(2,1)S(1)} collective-permute-done((bf16[32,7296]{1,0:T(8,128)(2,1)}, bf16[32,7296]{1,0:T(8,128)(2,1)S(1)}, u32[]{:S(2)}, u32[]{:S(2)}) %collective-permute-start.12) | collective-permute-done | bytes 466976 | tf_op jit(solution)/shard_map/ppermute | solution.py:16
  197.8 2.2 collective-permute-done.13.refs_2_.refs_10_
  200.0 7.7 %collective-permute-done.14.refs_5_.refs_13_ = bf16[32,7296]{1,0:T(8,128)(2,1)S(1)} collective-permute-done((bf16[32,7296]{1,0:T(8,128)(2,1)S(1)}, bf16[32,7296]{1,0:T(8,128)(2,1)S(1)}, u32[]{:S(2)}, u32[]{:S(2)}) %collective-permute-start.14) | collective-permute-done | bytes 466976 | tf_op jit(solution)/shard_map/ppermute | solution.py:16
  207.8 2.2 collective-permute-done.15.refs_6_.refs_14_
  210.0 0.8 copy-done.14
  210.8 11.2 %shard_map.105 = (bf16[384,128]{1,0:T(8,128)(2,1)}, bf16[384,128]{1,0:T(8,128)(2,1)}) custom-call(bf16[64,7296]{1,0:T(8,128)(2,1)} %copy-done.4, bf16[32,7296]{1,0:T(8,128)(2,1)} %copy-done.12, bf16[32,7296]{1,0:T(8,128)(2,1)} %collective-permute-done.13.refs_2_.refs_10_, bf16[64,7296]{1,0:T(8,128)(2,1)} %copy-done.5, ...), custom_call_target="tpu_custom_call" | custom-call | flops 5637144576 | bytes 20185088 | tf_op jit(solution)/shard_map/pallas_call | solution.py:86
  222.0 0.9 fusion.31
  223.2 1.3 collective-permute-start.16
  224.7 4.2 %collective-permute-done.16.refs_1_ = bf16[1024,128]{1,0:T(8,128)(2,1)S(1)} collective-permute-done((bf16[1024,128]{1,0:T(8,128)(2,1)S(1)}, bf16[1024,128]{1,0:T(8,128)(2,1)S(1)}, u32[]{:S(2)}, u32[]{:S(2)}) %collective-permute-start.16) | collective-permute-done | bytes 262176 | tf_op jit(solution)/shard_map/ppermute | solution.py:16
  228.9 2.4 collective-permute-done.17.refs_7_
  231.3 1.1 collective-permute-start.18
  232.4 0.4 collective-permute-start.19
  232.8 3.8 %collective-permute-done.18.refs_2_ = bf16[1024,128]{1,0:T(8,128)(2,1)S(1)} collective-permute-done((bf16[1024,128]{1,0:T(8,128)(2,1)S(1)}, bf16[1024,128]{1,0:T(8,128)(2,1)S(1)}, u32[]{:S(2)}, u32[]{:S(2)}) %collective-permute-start.18) | collective-permute-done | bytes 262176 | tf_op jit(solution)/shard_map/ppermute | solution.py:16
  236.5 2.3 collective-permute-done.19.refs_6_
  238.9 1.4 collective-permute-start.21
  240.4 3.7 %collective-permute-done.20.refs_3_ = bf16[1024,128]{1,0:T(8,128)(2,1)S(1)} collective-permute-done((bf16[1024,128]{1,0:T(8,128)(2,1)S(1)}, bf16[1024,128]{1,0:T(8,128)(2,1)S(1)}, u32[]{:S(2)}, u32[]{:S(2)}) %collective-permute-start.20) | collective-permute-done | bytes 262176 | tf_op jit(solution)/shard_map/ppermute | solution.py:16
  244.1 1.3 collective-permute-done.21.refs_5_
  245.7 1.5 collective-permute-start.23
  247.3 1.0 fusion.2
  248.3 2.0 collective-permute-done.22.refs_4_
  250.3 1.1 collective-permute-done.23.refs_4_
  251.5 8.2 %shard_map.106 = bf16[512,896]{1,0:T(8,128)(2,1)} custom-call(s32[1]{0:T(128)} %bitcast.18.place, bf16[512,128]{1,0:T(8,128)(2,1)} %bitcast.70, bf16[1024,128]{1,0:T(8,128)(2,1)} %copy-done.11, bf16[1024,128]{1,0:T(8,128)(2,1)} %copy-done.18, bf16[1024,128]{1,0:T(8,128)(2,1)} %copy-done.20, bf16[1024,128]{1,0:T(8,128)(2,1)} %copy-done.16, ...), custom_call_target="tpu_custom_call" | custom-call | flops 3758096384 | bytes 8388608 | tf_op jit(solution)/shard_map/pallas_call | solution.py:141
  259.7 5.0 %all-to-all-start.1 = ((bf16[8,64,896]{2,1,0:T(8,128)(2,1)}), bf16[8,64,896]{2,1,0:T(8,128)(2,1)S(1)}, u32[]{:S(2)}, u32[]{:S(2)}) async-start(bf16[8,64,896]{2,1,0:T(8,128)(2,1)} %bitcast.65), calls=%async_computation.1 | async-start | bytes 1835008 | tf_op jit(solution)/shard_map/all_to_all | solution.py:248
  264.6 8.2 %shard_map.107 = bf16[512,896]{1,0:T(8,128)(2,1)} custom-call(s32[1]{0:T(128)} %bitcast.18.place, bf16[512,128]{1,0:T(8,128)(2,1)} %bitcast.69, bf16[1024,128]{1,0:T(8,128)(2,1)} %copy-done.11, bf16[1024,128]{1,0:T(8,128)(2,1)} %copy-done.18, bf16[1024,128]{1,0:T(8,128)(2,1)} %copy-done.20, bf16[1024,128]{1,0:T(8,128)(2,1)} %copy-done.16, ...), custom_call_target="tpu_custom_call" | custom-call | flops 3758096384 | bytes 8388608 | tf_op jit(solution)/shard_map/pallas_call | solution.py:141
  272.8 11.5 %all-to-all-done.1 = bf16[8,64,896]{2,1,0:T(8,128)(2,1)S(1)} async-done(((bf16[8,64,896]{2,1,0:T(8,128)(2,1)}), bf16[8,64,896]{2,1,0:T(8,128)(2,1)S(1)}, u32[]{:S(2)}, u32[]{:S(2)}) %all-to-all-start.1) | async-done | bytes 917536 | tf_op jit(solution)/shard_map/all_to_all | solution.py:248
  284.5 1.4 copy.17
  285.8 3.7 %all-to-all-start.2 = ((bf16[8,64,896]{2,1,0:T(8,128)(2,1)}), bf16[8,64,896]{2,1,0:T(8,128)(2,1)S(1)}, u32[]{:S(2)}, u32[]{:S(2)}) async-start(bf16[8,64,896]{2,1,0:T(8,128)(2,1)} %bitcast.28), calls=%async_computation.2 | async-start | bytes 1835008 | tf_op jit(solution)/shard_map/all_to_all | solution.py:250
  289.5 2.7 add_convert_fusion.1
  292.2 10.3 %collective-permute-start.24 = (bf16[64,7168]{1,0:T(8,128)(2,1)}, bf16[64,7168]{1,0:T(8,128)(2,1)S(1)}, u32[]{:S(2)}, u32[]{:S(2)}) collective-permute-start(bf16[64,7168]{1,0:T(8,128)(2,1)} %add_convert_fusion.1), channel_id=1, source_target_pairs={{0,0},{32,64},{64,32},{96,128},{128,96},{160,192},{192,160},{224,2... | collective-permute-start | bytes 2752520 | tf_op jit(solution)/shard_map/ppermute | solution.py:256
  302.6 6.4 %all-to-all-done.2 = bf16[8,64,896]{2,1,0:T(8,128)(2,1)S(1)} async-done(((bf16[8,64,896]{2,1,0:T(8,128)(2,1)}), bf16[8,64,896]{2,1,0:T(8,128)(2,1)S(1)}, u32[]{:S(2)}, u32[]{:S(2)}) %all-to-all-start.2) | async-done | bytes 917536 | tf_op jit(solution)/shard_map/all_to_all | solution.py:250
  309.6 7.5 %collective-permute-start.25 = (bf16[64,7168]{1,0:T(8,128)(2,1)S(1)}, bf16[64,7168]{1,0:T(8,128)(2,1)S(1)}, u32[]{:S(2)}, u32[]{:S(2)}) collective-permute-start(bf16[64,7168]{1,0:T(8,128)(2,1)S(1)} %add_convert_fusion), channel_id=1, source_target_pairs={{0,32},{32,0},{64,96},{96,64},{128,160},{160,128},{192,224},{224,1... | collective-permute-start | bytes 2752520 | tf_op jit(solution)/shard_map/ppermute | solution.py:257
  317.1 2.1 collective-permute-done.25
  319.2 1.3 select_bitcast_fusion
  (102 shorter events, 3.7 us)
Async XLA Ops:
  7.2 165.8 %all-gather.6.cloned.1.call-start = ((), (), s32[]{:S(2)}) async-start(), calls=%async_computation.4 | async-start | bytes 18350080 | tf_op jit(solution)/shard_map/all_gather | solution.py:206
  11.5 1.5 copy-start.15
  14.9 9.2 %copy-start.22 = (bf16[1,64,7168]{2,1,0:T(8,128)(2,1)S(1)}, bf16[1,64,7168]{2,1,0:T(8,128)(2,1)}, u32[]{:S(2)}) copy-start(bf16[1,64,7168]{2,1,0:T(8,128)(2,1)} %param.11) | copy-start | bytes 2752516
  14.9 9.2 %copy-start.23 = (bf16[1,64,7168]{2,1,0:T(8,128)(2,1)S(1)}, bf16[1,64,7168]{2,1,0:T(8,128)(2,1)}, u32[]{:S(2)}) copy-start(bf16[1,64,7168]{2,1,0:T(8,128)(2,1)} %param.12) | copy-start | bytes 2752516
  14.9 111.7 %all-to-all-start = ((bf16[8,128,896]{2,1,0:T(8,128)(2,1)}), bf16[8,128,896]{2,1,0:T(8,128)(2,1)}, u32[]{:S(2)}, u32[]{:S(2)}) async-start(bf16[8,128,896]{2,1,0:T(8,128)(2,1)} %bitcast.53), calls=%async_computation | async-start | bytes 3670016 | tf_op jit(solution)/shard_map/all_to_all | solution.py:211
  24.0 227.4 %all-gather.4.cloned.1.call-start = ((), (), s32[]{:S(2)}) async-start(), calls=%async_computation.3 | async-start | bytes 9175040 | tf_op jit(solution)/shard_map/all_gather | solution.py:218
  24.1 0.7 copy-start.29
  24.1 0.7 copy-start.30
  24.8 2.9 copy-start.2
  24.8 5.7 %copy-start.31 = (f32[1,64,1]{1,2,0:T(1,128)S(1)}, f32[1,64,1]{1,2,0:T(1,128)}, u32[]{:S(2)}) copy-start(f32[1,64,1]{1,2,0:T(1,128)} %param.15) | copy-start | bytes 772
  24.8 5.7 %copy-start.32 = (f32[1,64,1]{1,2,0:T(1,128)S(1)}, f32[1,64,1]{1,2,0:T(1,128)}, u32[]{:S(2)}) copy-start(f32[1,64,1]{1,2,0:T(1,128)} %param.16) | copy-start | bytes 772
  24.9 101.7 %copy-start = (bf16[64,7296]{1,0:T(8,128)(2,1)}, bf16[64,7296]{1,0:T(8,128)(2,1)S(1)}, u32[]{:S(2)}) copy-start(bf16[64,7296]{1,0:T(8,128)(2,1)S(1)} %pad_maximum_fusion.1.refs_0_.refs_10_) | copy-start | bytes 2801668
  24.9 60.0 %collective-permute-start = (bf16[64,7296]{1,0:T(8,128)(2,1)S(1)}, bf16[64,7296]{1,0:T(8,128)(2,1)S(1)}, u32[]{:S(2)}, u32[]{:S(2)}) collective-permute-start(bf16[64,7296]{1,0:T(8,128)(2,1)S(1)} %pad_maximum_fusion.1.refs_0_.refs_10_), channel_id=1, source_target_pairs={{0,7},{1,0},{2,1},{3,2},{4,3},{5,4},{6,5},{7,6},{8,15},{9,8},{10,9... | collective-permute-start | bytes 2801672 | tf_op jit(solution)/shard_map/ppermute | solution.py:16
  27.6 58.9 %collective-permute-start.1 = (bf16[64,7296]{1,0:T(8,128)(2,1)S(1)}, bf16[64,7296]{1,0:T(8,128)(2,1)S(1)}, u32[]{:S(2)}, u32[]{:S(2)}) collective-permute-start(bf16[64,7296]{1,0:T(8,128)(2,1)S(1)} %pad_maximum_fusion.1.refs_0_.refs_10_), channel_id=1, source_target_pairs={{0,1},{1,2},{2,3},{3,4},{4,5},{5,6},{6,7},{7,0},{8,9},{9,10},{10,1... | collective-permute-start | bytes 2801672 | tf_op jit(solution)/shard_map/ppermute | solution.py:16
  27.8 144.9 %copy-start.1 = (bf16[64,7296]{1,0:T(8,128)(2,1)}, bf16[64,7296]{1,0:T(8,128)(2,1)S(1)}, u32[]{:S(2)}) copy-start(bf16[64,7296]{1,0:T(8,128)(2,1)S(1)} %pad_maximum_fusion.2.refs_5_.refs_15_) | copy-start | bytes 2801668
  27.8 77.1 %collective-permute-start.2 = (bf16[64,7296]{1,0:T(8,128)(2,1)S(1)}, bf16[64,7296]{1,0:T(8,128)(2,1)S(1)}, u32[]{:S(2)}, u32[]{:S(2)}) collective-permute-start(bf16[64,7296]{1,0:T(8,128)(2,1)S(1)} %pad_maximum_fusion.2.refs_5_.refs_15_), channel_id=1, source_target_pairs={{0,7},{1,0},{2,1},{3,2},{4,3},{5,4},{6,5},{7,6},{8,15},{9,8},{10,9... | collective-permute-start | bytes 2801672 | tf_op jit(solution)/shard_map/ppermute | solution.py:16
  30.5 76.0 %collective-permute-start.3 = (bf16[64,7296]{1,0:T(8,128)(2,1)S(1)}, bf16[64,7296]{1,0:T(8,128)(2,1)S(1)}, u32[]{:S(2)}, u32[]{:S(2)}) collective-permute-start(bf16[64,7296]{1,0:T(8,128)(2,1)S(1)} %pad_maximum_fusion.2.refs_5_.refs_15_), channel_id=1, source_target_pairs={{0,1},{1,2},{2,3},{3,4},{4,5},{5,6},{6,7},{7,0},{8,9},{9,10},{10,1... | collective-permute-start | bytes 2801672 | tf_op jit(solution)/shard_map/ppermute | solution.py:16
  84.9 21.6 %copy-start.6 = (bf16[64,7296]{1,0:T(8,128)(2,1)}, bf16[64,7296]{1,0:T(8,128)(2,1)S(1)}, u32[]{:S(2)}) copy-start(bf16[64,7296]{1,0:T(8,128)(2,1)S(1)} %collective-permute-done.refs_1_.refs_11_) | copy-start | bytes 2801668
  86.5 38.4 %copy-start.7 = (bf16[64,7296]{1,0:T(8,128)(2,1)}, bf16[64,7296]{1,0:T(8,128)(2,1)S(1)}, u32[]{:S(2)}) copy-start(bf16[64,7296]{1,0:T(8,128)(2,1)S(1)} %collective-permute-done.1.refs_4_.refs_14_) | copy-start | bytes 2801668
  86.5 38.4 %collective-permute-start.4 = (bf16[64,7296]{1,0:T(8,128)(2,1)S(1)}, bf16[64,7296]{1,0:T(8,128)(2,1)S(1)}, u32[]{:S(2)}, u32[]{:S(2)}) collective-permute-start(bf16[64,7296]{1,0:T(8,128)(2,1)S(1)} %collective-permute-done.refs_1_.refs_11_), channel_id=1, source_target_pairs={{0,7},{1,0},{2,1},{3,2},{4,3},{5,4},{6,5},{7,6},{8,15},{9,8},{10,9... | collective-permute-start | bytes 2801672 | tf_op jit(solution)/shard_map/ppermute | solution.py:16
  87.8 38.7 %collective-permute-start.5 = (bf16[64,7296]{1,0:T(8,128)(2,1)S(1)}, bf16[64,7296]{1,0:T(8,128)(2,1)}, u32[]{:S(2)}, u32[]{:S(2)}) collective-permute-start(bf16[64,7296]{1,0:T(8,128)(2,1)S(1)} %collective-permute-done.1.refs_4_.refs_14_), channel_id=1, source_target_pairs={{0,1},{1,2},{2,3},{3,4},{4,5},{5,6},{6,7},{7,0},{8,9},{9,10},{10,1... | collective-permute-start | bytes 2801672 | tf_op jit(solution)/shard_map/ppermute | solution.py:16
  104.9 20.0 %copy-start.8 = (bf16[64,7296]{1,0:T(8,128)(2,1)}, bf16[64,7296]{1,0:T(8,128)(2,1)S(1)}, u32[]{:S(2)}) copy-start(bf16[64,7296]{1,0:T(8,128)(2,1)S(1)} %collective-permute-done.2.refs_6_.refs_16_) | copy-start | bytes 2801668
  106.5 18.4 %copy-start.9 = (bf16[64,7296]{1,0:T(8,128)(2,1)}, bf16[64,7296]{1,0:T(8,128)(2,1)S(1)}, u32[]{:S(2)}) copy-start(bf16[64,7296]{1,0:T(8,128)(2,1)S(1)} %collective-permute-done.3.refs_9_.refs_19_) | copy-start | bytes 2801668
  124.9 0.9 copy-start.10
  126.6 21.1 %collective-permute-start.6 = (bf16[64,7296]{1,0:T(8,128)(2,1)}, bf16[64,7296]{1,0:T(8,128)(2,1)}, u32[]{:S(2)}, u32[]{:S(2)}) collective-permute-start(bf16[64,7296]{1,0:T(8,128)(2,1)} %copy-done.8), channel_id=1, source_target_pairs={{0,7},{1,0},{2,1},{3,2},{4,3},{5,4},{6,5},{7,6},{8,15},{9,8},{10,9... | collective-permute-start | bytes 2801672 | tf_op jit(solution)/shard_map/ppermute | solution.py:16
  128.0 22.0 %collective-permute-start.7 = (bf16[64,7296]{1,0:T(8,128)(2,1)}, bf16[64,7296]{1,0:T(8,128)(2,1)}, u32[]{:S(2)}, u32[]{:S(2)}) collective-permute-start(bf16[64,7296]{1,0:T(8,128)(2,1)} %copy-done.9), channel_id=1, source_target_pairs={{0,1},{1,2},{2,3},{3,4},{4,5},{5,6},{6,7},{7,0},{8,9},{9,10},{10,1... | collective-permute-start | bytes 2801672 | tf_op jit(solution)/shard_map/ppermute | solution.py:16
  128.1 39.5 %collective-permute-start.8 = (bf16[64,7296]{1,0:T(8,128)(2,1)}, bf16[64,7296]{1,0:T(8,128)(2,1)S(1)}, u32[]{:S(2)}, u32[]{:S(2)}) collective-permute-start(bf16[64,7296]{1,0:T(8,128)(2,1)} %copy-done.10), channel_id=1, source_target_pairs={{0,7},{1,0},{2,1},{3,2},{4,3},{5,4},{6,5},{7,6},{8,15},{9,8},{10,9... | collective-permute-start | bytes 2801672 | tf_op jit(solution)/shard_map/ppermute | solution.py:16
  130.7 39.2 %collective-permute-start.9 = (bf16[64,7296]{1,0:T(8,128)(2,1)}, bf16[64,7296]{1,0:T(8,128)(2,1)S(1)}, u32[]{:S(2)}, u32[]{:S(2)}) collective-permute-start(bf16[64,7296]{1,0:T(8,128)(2,1)} %collective-permute-done.5.refs_3_.refs_13_), channel_id=1, source_target_pairs={{0,1},{1,2},{2,3},{3,4},{4,5},{5,6},{6,7},{7,0},{8,9},{9,10},{10,1... | collective-permute-start | bytes 2801672 | tf_op jit(solution)/shard_map/ppermute | solution.py:16
  150.0 38.1 %collective-permute-start.10 = (bf16[64,7296]{1,0:T(8,128)(2,1)}, bf16[64,7296]{1,0:T(8,128)(2,1)}, u32[]{:S(2)}, u32[]{:S(2)}) collective-permute-start(bf16[64,7296]{1,0:T(8,128)(2,1)} %collective-permute-done.6.refs_7_.refs_17_), channel_id=1, source_target_pairs={{0,7},{1,0},{2,1},{3,2},{4,3},{5,4},{6,5},{7,6},{8,15},{9,8},{10,9... | collective-permute-start | bytes 2801672 | tf_op jit(solution)/shard_map/ppermute | solution.py:16
  151.1 38.9 %collective-permute-start.11 = (bf16[64,7296]{1,0:T(8,128)(2,1)}, bf16[64,7296]{1,0:T(8,128)(2,1)}, u32[]{:S(2)}, u32[]{:S(2)}) collective-permute-start(bf16[64,7296]{1,0:T(8,128)(2,1)} %collective-permute-done.7.refs_8_.refs_18_), channel_id=1, source_target_pairs={{0,1},{1,2},{2,3},{3,4},{4,5},{5,6},{6,7},{7,0},{8,9},{9,10},{10,1... | collective-permute-start | bytes 2801672 | tf_op jit(solution)/shard_map/ppermute | solution.py:16
  167.6 20.5 %copy-start.4 = (bf16[64,7296]{1,0:T(8,128)(2,1)}, bf16[64,7296]{1,0:T(8,128)(2,1)S(1)}, u32[]{:S(2)}) copy-start(bf16[64,7296]{1,0:T(8,128)(2,1)S(1)} %collective-permute-done.8.refs_0_.refs_8_) | copy-start | bytes 2801668
  169.9 2.0 copy-start.5
  170.7 27.0 %collective-permute-start.12 = (bf16[32,7296]{1,0:T(8,128)(2,1)}, bf16[32,7296]{1,0:T(8,128)(2,1)S(1)}, u32[]{:S(2)}, u32[]{:S(2)}) collective-permute-start(bf16[32,7296]{1,0:T(8,128)(2,1)} %slice.98), channel_id=1, source_target_pairs={{0,7},{1,0},{2,1},{3,2},{4,3},{5,4},{6,5},{7,6},{8,15},{9,8},{10,9... | collective-permute-start | bytes 1400840 | tf_op jit(solution)/shard_map/ppermute | solution.py:16
  172.7 27.3 %collective-permute-start.13 = (bf16[32,7296]{1,0:T(8,128)(2,1)}, bf16[32,7296]{1,0:T(8,128)(2,1)}, u32[]{:S(2)}, u32[]{:S(2)}) collective-permute-start(bf16[32,7296]{1,0:T(8,128)(2,1)} %slice.99), channel_id=1, source_target_pairs={{0,1},{1,2},{2,3},{3,4},{4,5},{5,6},{6,7},{7,0},{8,9},{9,10},{10,1... | collective-permute-start | bytes 1400840 | tf_op jit(solution)/shard_map/ppermute | solution.py:16
  188.1 11.9 %copy-start.25 = (bf16[640,128]{1,0:T(8,128)(2,1)S(1)}, bf16[640,128]{1,0:T(8,128)(2,1)}, u32[]{:S(2)}) copy-start(bf16[640,128]{1,0:T(8,128)(2,1)} %get-tuple-element.71) | copy-start | bytes 491524
  191.1 16.7 %collective-permute-start.14 = (bf16[32,7296]{1,0:T(8,128)(2,1)S(1)}, bf16[32,7296]{1,0:T(8,128)(2,1)S(1)}, u32[]{:S(2)}, u32[]{:S(2)}) collective-permute-start(bf16[32,7296]{1,0:T(8,128)(2,1)S(1)} %slice.100), channel_id=1, source_target_pairs={{0,7},{1,0},{2,1},{3,2},{4,3},{5,4},{6,5},{7,6},{8,15},{9,8},{10,9... | collective-permute-start | bytes 1400840 | tf_op jit(solution)/shard_map/ppermute | solution.py:16
  193.3 16.7 %collective-permute-start.15 = (bf16[32,7296]{1,0:T(8,128)(2,1)S(1)}, bf16[32,7296]{1,0:T(8,128)(2,1)S(1)}, u32[]{:S(2)}, u32[]{:S(2)}) collective-permute-start(bf16[32,7296]{1,0:T(8,128)(2,1)S(1)} %slice.101), channel_id=1, source_target_pairs={{0,1},{1,2},{2,3},{3,4},{4,5},{5,6},{6,7},{7,0},{8,9},{9,10},{10,1... | collective-permute-start | bytes 1400840 | tf_op jit(solution)/shard_map/ppermute | solution.py:16
  197.8 12.3 %copy-start.12 = (bf16[32,7296]{1,0:T(8,128)(2,1)}, bf16[32,7296]{1,0:T(8,128)(2,1)S(1)}, u32[]{:S(2)}) copy-start(bf16[32,7296]{1,0:T(8,128)(2,1)S(1)} %collective-permute-done.12.refs_1_.refs_9_) | copy-start | bytes 1400836
  200.0 40.3 %copy-start.24 = (bf16[640,128]{1,0:T(8,128)(2,1)S(1)}, bf16[640,128]{1,0:T(8,128)(2,1)}, u32[]{:S(2)}) copy-start(bf16[640,128]{1,0:T(8,128)(2,1)} %get-tuple-element.89) | copy-start | bytes 491524
  207.8 2.2 copy-start.13
  210.0 0.8 copy-start.14
  222.0 25.3 %copy-start.28 = (bf16[384,128]{1,0:T(8,128)(2,1)S(1)}, bf16[384,128]{1,0:T(8,128)(2,1)}, u32[]{:S(2)}) copy-start(bf16[384,128]{1,0:T(8,128)(2,1)} %get-tuple-element.90) | copy-start | bytes 294916
  223.2 28.2 %copy-start.11 = (bf16[1024,128]{1,0:T(8,128)(2,1)}, bf16[1024,128]{1,0:T(8,128)(2,1)S(1)}, u32[]{:S(2)}) copy-start(bf16[1024,128]{1,0:T(8,128)(2,1)S(1)} %pad_maximum_fusion.3.refs_0_) | copy-start | bytes 786436
  223.2 5.7 %collective-permute-start.16 = (bf16[1024,128]{1,0:T(8,128)(2,1)S(1)}, bf16[1024,128]{1,0:T(8,128)(2,1)S(1)}, u32[]{:S(2)}, u32[]{:S(2)}) collective-permute-start(bf16[1024,128]{1,0:T(8,128)(2,1)S(1)} %pad_maximum_fusion.3.refs_0_), channel_id=1, source_target_pairs={{0,7},{1,0},{2,1},{3,2},{4,3},{5,4},{6,5},{7,6},{8,15},{9,8},{10,9... | collective-permute-start | bytes 786440 | tf_op jit(solution)/shard_map/ppermute | solution.py:16
  224.5 6.8 %collective-permute-start.17 = (bf16[1024,128]{1,0:T(8,128)(2,1)S(1)}, bf16[1024,128]{1,0:T(8,128)(2,1)S(1)}, u32[]{:S(2)}, u32[]{:S(2)}) collective-permute-start(bf16[1024,128]{1,0:T(8,128)(2,1)S(1)} %pad_maximum_fusion.3.refs_0_), channel_id=1, source_target_pairs={{0,1},{1,2},{2,3},{3,4},{4,5},{5,6},{6,7},{7,0},{8,9},{9,10},{10,1... | collective-permute-start | bytes 786440 | tf_op jit(solution)/shard_map/ppermute | solution.py:16
  228.9 22.5 %copy-start.18 = (bf16[1024,128]{1,0:T(8,128)(2,1)}, bf16[1024,128]{1,0:T(8,128)(2,1)S(1)}, u32[]{:S(2)}) copy-start(bf16[1024,128]{1,0:T(8,128)(2,1)S(1)} %collective-permute-done.16.refs_1_) | copy-start | bytes 786436
  231.3 20.1 %copy-start.19 = (bf16[1024,128]{1,0:T(8,128)(2,1)}, bf16[1024,128]{1,0:T(8,128)(2,1)S(1)}, u32[]{:S(2)}) copy-start(bf16[1024,128]{1,0:T(8,128)(2,1)S(1)} %collective-permute-done.17.refs_7_) | copy-start | bytes 786436
  231.3 5.2 %collective-permute-start.18 = (bf16[1024,128]{1,0:T(8,128)(2,1)S(1)}, bf16[1024,128]{1,0:T(8,128)(2,1)S(1)}, u32[]{:S(2)}, u32[]{:S(2)}) collective-permute-start(bf16[1024,128]{1,0:T(8,128)(2,1)S(1)} %collective-permute-done.16.refs_1_), channel_id=1, source_target_pairs={{0,7},{1,0},{2,1},{3,2},{4,3},{5,4},{6,5},{7,6},{8,15},{9,8},{10,9... | collective-permute-start | bytes 786440 | tf_op jit(solution)/shard_map/ppermute | solution.py:16
  232.4 6.4 %collective-permute-start.19 = (bf16[1024,128]{1,0:T(8,128)(2,1)S(1)}, bf16[1024,128]{1,0:T(8,128)(2,1)S(1)}, u32[]{:S(2)}, u32[]{:S(2)}) collective-permute-start(bf16[1024,128]{1,0:T(8,128)(2,1)S(1)} %collective-permute-done.17.refs_7_), channel_id=1, source_target_pairs={{0,1},{1,2},{2,3},{3,4},{4,5},{5,6},{6,7},{7,0},{8,9},{9,10},{10,1... | collective-permute-start | bytes 786440 | tf_op jit(solution)/shard_map/ppermute | solution.py:16
  236.5 14.9 %copy-start.20 = (bf16[1024,128]{1,0:T(8,128)(2,1)}, bf16[1024,128]{1,0:T(8,128)(2,1)S(1)}, u32[]{:S(2)}) copy-start(bf16[1024,128]{1,0:T(8,128)(2,1)S(1)} %collective-permute-done.18.refs_2_) | copy-start | bytes 786436
  238.9 12.6 %copy-start.21 = (bf16[1024,128]{1,0:T(8,128)(2,1)}, bf16[1024,128]{1,0:T(8,128)(2,1)S(1)}, u32[]{:S(2)}) copy-start(bf16[1024,128]{1,0:T(8,128)(2,1)S(1)} %collective-permute-done.19.refs_6_) | copy-start | bytes 786436
  238.9 5.2 %collective-permute-start.20 = (bf16[1024,128]{1,0:T(8,128)(2,1)S(1)}, bf16[1024,128]{1,0:T(8,128)(2,1)S(1)}, u32[]{:S(2)}, u32[]{:S(2)}) collective-permute-start(bf16[1024,128]{1,0:T(8,128)(2,1)S(1)} %collective-permute-done.18.refs_2_), channel_id=1, source_target_pairs={{0,7},{1,0},{2,1},{3,2},{4,3},{5,4},{6,5},{7,6},{8,15},{9,8},{10,9... | collective-permute-start | bytes 786440 | tf_op jit(solution)/shard_map/ppermute | solution.py:16
  238.9 6.4 %collective-permute-start.21 = (bf16[1024,128]{1,0:T(8,128)(2,1)S(1)}, bf16[1024,128]{1,0:T(8,128)(2,1)S(1)}, u32[]{:S(2)}, u32[]{:S(2)}) collective-permute-start(bf16[1024,128]{1,0:T(8,128)(2,1)S(1)} %collective-permute-done.19.refs_6_), channel_id=1, source_target_pairs={{0,1},{1,2},{2,3},{3,4},{4,5},{5,6},{6,7},{7,0},{8,9},{9,10},{10,1... | collective-permute-start | bytes 786440 | tf_op jit(solution)/shard_map/ppermute | solution.py:16
  244.1 7.3 %copy-start.16 = (bf16[1024,128]{1,0:T(8,128)(2,1)}, bf16[1024,128]{1,0:T(8,128)(2,1)S(1)}, u32[]{:S(2)}) copy-start(bf16[1024,128]{1,0:T(8,128)(2,1)S(1)} %collective-permute-done.20.refs_3_) | copy-start | bytes 786436
  245.4 6.1 %copy-start.17 = (bf16[1024,128]{1,0:T(8,128)(2,1)}, bf16[1024,128]{1,0:T(8,128)(2,1)S(1)}, u32[]{:S(2)}) copy-start(bf16[1024,128]{1,0:T(8,128)(2,1)S(1)} %collective-permute-done.21.refs_5_) | copy-start | bytes 786436
  245.4 4.9 %collective-permute-start.22 = (bf16[512,128]{1,0:T(8,128)(2,1)S(1)}, bf16[512,128]{1,0:T(8,128)(2,1)S(1)}, u32[]{:S(2)}, u32[]{:S(2)}) collective-permute-start(bf16[512,128]{1,0:T(8,128)(2,1)S(1)} %slice.112), channel_id=1, source_target_pairs={{0,7},{1,0},{2,1},{3,2},{4,3},{5,4},{6,5},{7,6},{8,15},{9,8},{10,9... | collective-permute-start | bytes 393224 | tf_op jit(solution)/shard_map/ppermute | solution.py:16
  245.7 5.7 %collective-permute-start.23 = (bf16[512,128]{1,0:T(8,128)(2,1)S(1)}, bf16[512,128]{1,0:T(8,128)(2,1)S(1)}, u32[]{:S(2)}, u32[]{:S(2)}) collective-permute-start(bf16[512,128]{1,0:T(8,128)(2,1)S(1)} %slice.113), channel_id=1, source_target_pairs={{0,1},{1,2},{2,3},{3,4},{4,5},{5,6},{6,7},{7,0},{8,9},{9,10},{10,1... | collective-permute-start | bytes 393224 | tf_op jit(solution)/shard_map/ppermute | solution.py:16
  250.3 1.1 copy-start.27
  251.4 8.3 %copy-start.26 = (bf16[512,128]{1,0:T(8,128)(2,1)}, bf16[512,128]{1,0:T(8,128)(2,1)S(1)}, u32[]{:S(2)}) copy-start(bf16[512,128]{1,0:T(8,128)(2,1)S(1)} %collective-permute-done.23.refs_4_) | copy-start | bytes 393220
  259.7 24.7 %all-to-all-start.1 = ((bf16[8,64,896]{2,1,0:T(8,128)(2,1)}), bf16[8,64,896]{2,1,0:T(8,128)(2,1)S(1)}, u32[]{:S(2)}, u32[]{:S(2)}) async-start(bf16[8,64,896]{2,1,0:T(8,128)(2,1)} %bitcast.65), calls=%async_computation.1 | async-start | bytes 1835008 | tf_op jit(solution)/shard_map/all_to_all | solution.py:248
  285.8 3.7 %copy-start.3 = (bf16[64,7168]{1,0:T(8,128)(2,1)S(1)}, bf16[64,7168]{1,0:T(8,128)(2,1)}, u32[]{:S(2)}) copy-start(bf16[64,7168]{1,0:T(8,128)(2,1)} %copy-done.2) | copy-start | bytes 2752516
  285.8 23.1 %all-to-all-start.2 = ((bf16[8,64,896]{2,1,0:T(8,128)(2,1)}), bf16[8,64,896]{2,1,0:T(8,128)(2,1)S(1)}, u32[]{:S(2)}, u32[]{:S(2)}) async-start(bf16[8,64,896]{2,1,0:T(8,128)(2,1)} %bitcast.28), calls=%async_computation.2 | async-start | bytes 1835008 | tf_op jit(solution)/shard_map/all_to_all | solution.py:250
  292.2 24.8 %collective-permute-start.24 = (bf16[64,7168]{1,0:T(8,128)(2,1)}, bf16[64,7168]{1,0:T(8,128)(2,1)S(1)}, u32[]{:S(2)}, u32[]{:S(2)}) collective-permute-start(bf16[64,7168]{1,0:T(8,128)(2,1)} %add_convert_fusion.1), channel_id=1, source_target_pairs={{0,0},{32,64},{64,32},{96,128},{128,96},{160,192},{192,160},{224,2... | collective-permute-start | bytes 2752520 | tf_op jit(solution)/shard_map/ppermute | solution.py:256
  309.6 9.6 %collective-permute-start.25 = (bf16[64,7168]{1,0:T(8,128)(2,1)S(1)}, bf16[64,7168]{1,0:T(8,128)(2,1)S(1)}, u32[]{:S(2)}, u32[]{:S(2)}) collective-permute-start(bf16[64,7168]{1,0:T(8,128)(2,1)S(1)} %add_convert_fusion), channel_id=1, source_target_pairs={{0,32},{32,0},{64,96},{96,64},{128,160},{160,128},{192,224},{224,1... | collective-permute-start | bytes 2752520 | tf_op jit(solution)/shard_map/ppermute | solution.py:257
Sparse Core Ops, SparseCore 0:
  11.7 142.7 all-gather.5
  156.2 77.8 all-gather.3
